TPU v7x, 512 devices: a whole 4x4x16 slice. The times are simulated.
512 devices in a mesh: ctx: 16 (over z_hi, y, core), zero: 32 (over z_lo, x).
Axes of the slice: x: 4, y: 4, z: 16 (z_hi: 2, z_lo: 8; z = z_hi * 8 + z_lo), core: 2. Of those that a mesh axis runs over, the one named last changes fastest.
Arguments:
- tokens: bfloat16 [65536, 2048], P(('ctx', 'zero')), may hold values from -6 to 6
- in_weight: bfloat16 [3, 2048, 2048], P(None, 'zero', 'ctx'), may hold values from -0.125 to 0.125
- filters: float32 [128, 128], P('ctx'), may hold values from -1 to 1
- doc_offset: int32 [16, 4096], P(None, 'zero'), may hold values from 0 to 1023, as said below
- cotangent: bfloat16 [65536, 2048], P(('ctx', 'zero')), may hold values from -6 to 6
Outputs:
- gated_out: bfloat16 [65536, 2048], P(('ctx', 'zero'))
- grad_in_weight: float32 [3, 2048, 2048], P(None, 'zero', 'ctx')
- grad_filters: float32 [128, 128], P('ctx')
Inputs may be any that keep to these rules, and one draw needn't show every extreme that they name: `doc_offset`: offset from the document's first token; offsets rise by one along the sequence and restart at 0 where a document begins; every document has at most 1024 tokens and the first has exactly 1024.
All inputs are finite; a program needn't handle non-finite values.
Results may differ from a plain program's by a relative error of at most 0.033.
Values may be sent and summed in bfloat16 or wider, within the bound.
No kernel may reach another device: no remote copies, remote signals or barrier semaphores. Data moves between devices by JAX's collectives and lax.ppermute only.
A program may use at most 128 MiB of HBM per device.

v0:
```python
import jax
import jax.numpy as jnp
from jax import lax
from jax.sharding import PartitionSpec as P


def passed_along(shard, axis, by):
    count = lax.axis_size(axis)
    return lax.ppermute(shard, axis, [(i, (i + by) % count) for i in range(count)])


def split_pair(values_f):
    upper = values_f.astype(jnp.bfloat16)
    lower = (values_f - upper.astype(jnp.float32)).astype(jnp.bfloat16)
    return (upper, lower)


def conv_cols(matrix, source, group_count):
    upper, lower = split_pair(matrix)
    source_split = source.reshape(source.shape[0], group_count, -1)
    result = jnp.einsum("ugc,gtu->gct", source_split, upper, preferred_element_type=jnp.float32)
    result = result + jnp.einsum(
        "ugc,gtu->gct", source_split, lower, preferred_element_type=jnp.float32
    )
    result = result.transpose(2, 0, 1)
    return result.reshape(result.shape[0], -1)


def receive_tail(product, tap_count):
    tail_rows = product[:, product.shape[1] - (tap_count - 1) :, :]
    before = passed_along(tail_rows, "zero", 1)
    rolled = jnp.concatenate([jnp.zeros_like(before[:1]), before[:-1]], 0)
    return jnp.where(lax.axis_index("zero") == 0, rolled, before)


def body(tokens, in_weight, filters, doc_offset, cotangent):
    ctx_count = lax.axis_size("ctx")
    zero_count = lax.axis_size("zero")
    tok_rows = tokens.shape[0]
    tap_count = filters.shape[1]
    group_count = filters.shape[0]
    col_width = in_weight.shape[2]
    ext_rows = tok_rows + tap_count - 1
    gathered = lax.all_gather(tokens, "ctx", axis=0, tiled=True)
    rows_all = lax.all_gather(in_weight, "zero", axis=1, tiled=True)
    projected = jnp.einsum("td,sdc->stc", gathered, rows_all, preferred_element_type=jnp.float32)
    projected = projected.astype(jnp.bfloat16).reshape(3, ctx_count, tok_rows, col_width)
    queries, key_part, values = (projected[0], projected[1], projected[2])
    product = (key_part.astype(jnp.float32) * values.astype(jnp.float32)).astype(jnp.bfloat16)
    tap_lag = jnp.arange(tok_rows)[:, None] + (tap_count - 1) - jnp.arange(ext_rows)[None, :]
    in_range = (tap_lag >= 0) & (tap_lag < tap_count)
    toeplitz = jnp.where(
        in_range[None], filters[:, jnp.clip(tap_lag, 0, tap_count - 1)], jnp.float32(0.0)
    )
    keep_mask = (tap_lag[None, :, :] <= doc_offset[:, :, None]).astype(jnp.float32)
    before = receive_tail(product, tap_count)
    extended = jnp.concatenate([before, product], 1)

    def joined_block(block_args):
        source, keep_rows = block_args
        return conv_cols(toeplitz * keep_rows[None], source, group_count)

    mixed = lax.map(joined_block, (extended, keep_mask))
    gated_out = (queries.astype(jnp.float32) * mixed).astype(jnp.bfloat16)
    out_rows = lax.all_to_all(gated_out, "ctx", split_axis=0, concat_axis=2, tiled=True).reshape(
        tok_rows, -1
    )
    cotangent_cols = lax.all_to_all(
        cotangent.reshape(1, tok_rows, -1), "ctx", split_axis=2, concat_axis=0, tiled=True
    )
    cotangent_f = cotangent_cols.astype(jnp.float32)
    grad_query = cotangent_f * mixed
    grad_mixed = cotangent_f * queries.astype(jnp.float32)

    def backward_block(block_args):
        source, grad_rows, keep_rows = block_args
        mat_upper, mat_lower = split_pair(toeplitz * keep_rows[None])
        source_split = source.reshape(ext_rows, group_count, -1)
        grad_upper, grad_lower = split_pair(grad_rows.reshape(tok_rows, group_count, -1))
        grad_ext = jnp.einsum(
            "gtu,tgc->gcu", mat_upper, grad_upper, preferred_element_type=jnp.float32
        )
        grad_ext = grad_ext + jnp.einsum(
            "gtu,tgc->gcu", mat_upper, grad_lower, preferred_element_type=jnp.float32
        )
        grad_ext = grad_ext + jnp.einsum(
            "gtu,tgc->gcu", mat_lower, grad_upper, preferred_element_type=jnp.float32
        )
        grad_ext = grad_ext.transpose(2, 0, 1).reshape(ext_rows, col_width)
        pair_sums = jnp.einsum(
            "tgc,ugc->gtu", grad_upper, source_split, preferred_element_type=jnp.float32
        )
        pair_sums = pair_sums + jnp.einsum(
            "tgc,ugc->gtu", grad_lower, source_split, preferred_element_type=jnp.float32
        )
        pair_sums = pair_sums * keep_rows[None]
        flattened = jnp.concatenate(
            [
                pair_sums.reshape(group_count, tok_rows * ext_rows),
                jnp.zeros((group_count, tok_rows), jnp.float32),
            ],
            1,
        )
        diagonals = flattened.reshape(group_count, tok_rows, ext_rows + 1)[:, :, :tap_count]
        return (grad_ext, jnp.flip(jnp.sum(diagonals, axis=1), axis=1))

    grad_ext, filter_terms = lax.map(backward_block, (extended, grad_mixed, keep_mask))
    received = passed_along(
        grad_ext[:, : tap_count - 1, :].astype(jnp.bfloat16), "zero", -1
    ).astype(jnp.float32)
    shifted = jnp.concatenate([received[1:], jnp.zeros_like(received[:1])], 0)
    received = jnp.where(lax.axis_index("zero") == zero_count - 1, shifted, received)
    grad_product = grad_ext[:, tap_count - 1 :, :] + jnp.pad(
        received, ((0, 0), (tok_rows - (tap_count - 1), 0), (0, 0))
    )
    grad_key = grad_product * values.astype(jnp.float32)
    grad_value = grad_product * key_part.astype(jnp.float32)
    grads = (
        jnp.stack([grad_query, grad_key, grad_value])
        .astype(jnp.bfloat16)
        .reshape(3, ctx_count * tok_rows, col_width)
    )
    partial_weight = jnp.einsum("td,stc->sdc", gathered, grads, preferred_element_type=jnp.float32)
    grad_in_weight = lax.psum_scatter(
        partial_weight.astype(jnp.bfloat16), "zero", scatter_dimension=1, tiled=True
    ).astype(jnp.float32)
    grad_filters = lax.psum(jnp.sum(filter_terms, axis=0), "zero")
    return (out_rows, grad_in_weight, grad_filters)


def solution(mesh):
    return jax.shard_map(
        body,
        mesh=mesh,
        in_specs=(
            P(("ctx", "zero"), None),
            P(None, "zero", "ctx"),
            P("ctx", None),
            P(None, "zero"),
            P(("ctx", "zero"), None),
        ),
        out_specs=(P(("ctx", "zero"), None), P(None, "zero", "ctx"), P("ctx", None)),
        check_vma=False,
    )
```

profile of v0, /device:TPU:8, one launch (start us, length us, event | category | flops | bytes accessed | tf_op | source)
XLA Modules:
  0.0 1095.7 jit_solution(16292704230912726044)
XLA Ops:
  8.6 2.4 copy.57
  11.5 11.5 %reduce = bf16[2048,128]{1,0:T(8,128)(2,1)S(1)} reduce(bf16[2048,1,128]{2,1,0:T(2,128)(2,1)S(1)} %bitcast.127, bf16[]{:T(256)} %broadcast.121), dimensions={1}, to_apply=%bitcast.75.reduce_sub_computation | reduce | bytes 1048578
  23.1 0.9 reshape.167
  24.0 18.2 %all-to-all-start.1 = ((bf16[16,2,8192]{2,1,0:T(2,128)(2,1)}), bf16[16,2,8192]{2,1,0:T(2,128)(2,1)}, u32[]{:S(2)}, u32[]{:S(2)}) async-start(bf16[16,2,8192]{2,1,0:T(2,128)(2,1)} %reshape.167), calls=%async_computation.1 | async-start | bytes 1048576 | tf_op jit(solution)/shard_map/all_to_all | solution.py:68
  42.8 60.9 %gather_fusion = f32[32640,8]{1,0:T(8,128)} fusion(f32[8,128]{0,1:T(8,128)S(1)} %copy.53, s32[32768]{0:T(1024)S(1)} %pad_clamp_fusion), kind=kCustom, calls=%fused_computation | custom fusion | bytes 2219520 | tf_op jit(solution)/shard_map/gather | solution.py:53
  103.7 9.6 copy.54
  113.4 2.4 reshape.161
  116.3 132.3 %all-gather.3.cloned.1.call-done = bf16[3,2048,128]{2,1,0:T(8,128)(2,1)} async-done(((bf16[3,64,128]{2,1,0:T(8,128)(2,1)}), bf16[3,2048,128]{2,1,0:T(8,128)(2,1)}) %all-gather.3.cloned.1.call-update) | async-done | bytes 1572880 | tf_op jit(solution)/shard_map/all_gather | solution.py:45
  248.6 177.5 %all-gather.5.cloned.1.call-done = bf16[2048,2048]{1,0:T(8,128)(2,1)} async-done(((bf16[128,2048]{1,0:T(8,128)(2,1)}), bf16[2048,2048]{1,0:T(8,128)(2,1)}) %all-gather.5.cloned.1.call-update) | async-done | bytes 8388624 | tf_op jit(solution)/shard_map/all_gather | solution.py:44
  426.1 7.3 fusion.25
  433.4 1.3 convert_bitcast_fusion.2
  435.9 1.0 slice.45
  436.9 3.6 collective-permute-start
  440.7 3.5 reshape.168
  444.2 3.0 bitcast_convert_fusion
  447.2 1.2 copy.67
  448.4 13.5 %collective-permute-done = bf16[16,127,128]{1,2,0:T(8,128)(2,1)} collective-permute-done((bf16[16,127,128]{1,2,0:T(8,128)(2,1)}, bf16[16,127,128]{1,2,0:T(8,128)(2,1)}, u32[]{:S(2)}, u32[]{:S(2)}) %collective-permute-start) | collective-permute-done | bytes 520224 | tf_op jit(solution)/shard_map/ppermute | solution.py:9
  461.9 1.1 slice.46
  463.1 1.4 pad_maximum_fusion
  464.6 32.6 %while.22 = (s32[]{:T(128)}, f32[16,128,128]{1,2,0:T(8,128)}, bf16[16,255,128]{1,2,0:T(8,128)(2,1)}, f32[16,128,255]{2,1,0:T(8,128)S(1)}, f32[8,128,255]{2,1,0:T(8,128)S(1)}, /*index=5*/s32[]{:T(128)}) while((s32[]{:T(128)}, f32[16,128,128]{1,2,0:T(8,128)}, bf16[16,255,128]{1,2,0:T(8,128)(2,1)}, f32[16,128,255]{2,1,0:T(8,128)S(1)}, ...), condition=%wide.region_1.2_spmd, body=%wide.region_0.1_spmd.sunk | while | flops 18555904 | bytes 3200589 | solution.py:63
  497.2 3.6 multiply_convert_fusion.8
  500.8 80.1 %while.23 = (s32[]{:T(128)}, f32[16,255,128]{1,2,0:T(8,128)}, f32[16,8,128]{2,1,0:T(8,128)S(1)}, f32[16,128,128]{1,2,0:T(8,128)}, f32[16,128,255]{2,1,0:T(8,128)...) while((s32[]{:T(128)}, f32[16,255,128]{1,2,0:T(8,128)}, ...), condition=%wide.region_4.5_spmd, body=%wide.region_2.4_spmd.sunk | while | flops 45027072 | bytes 30123688 | solution.py:107
  500.8 0.9 constant_dynamic-slice_fusion.7
  505.8 0.9 constant_dynamic-slice_fusion.7
  510.8 0.9 constant_dynamic-slice_fusion.7
  515.8 0.9 constant_dynamic-slice_fusion.7
  520.8 0.9 constant_dynamic-slice_fusion.7
  525.9 0.9 constant_dynamic-slice_fusion.7
  535.9 0.9 constant_dynamic-slice_fusion.7
  545.9 0.9 constant_dynamic-slice_fusion.7
  555.9 0.9 constant_dynamic-slice_fusion.7
  560.9 0.9 constant_dynamic-slice_fusion.7
  565.9 0.9 constant_dynamic-slice_fusion.7
  570.9 0.9 constant_dynamic-slice_fusion.7
  580.9 2.1 slice.59
  583.1 2.5 collective-permute-start.1
  585.5 1.4 copy.58
  586.9 1.0 stack.12
  587.9 5.2 all-to-all-start
  593.2 21.8 %collective-permute-done.1 = bf16[16,127,128]{1,2,0:T(8,128)(2,1)S(1)} collective-permute-done((bf16[16,127,128]{1,2,0:T(8,128)(2,1)}, bf16[16,127,128]{1,2,0:T(8,128)(2,1)S(1)}, u32[]{:S(2)}, u32[]{:S(2)}) %collective-permute-start.1) | collective-permute-done | bytes 520224 | tf_op jit(solution)/shard_map/ppermute | solution.py:9
  615.3 2.5 multiply_convert_fusion.7
  618.8 1.0 stack.14
  619.8 7.0 fusion.22
  626.8 2.5 copy.64
  629.3 1.3 dynamic-slice
  631.3 124.5 %psum.7 = f32[8,128]{1,0:T(8,128)} all-reduce(f32[8,128]{1,0:T(8,128)S(1)} %reduce_sum.18), channel_id=1, replica_groups=mesh['ctx'=16,'zero'=32] {'zero'}, use_global_device_ids=true, to_apply=%region_7.8 | all-reduce | flops 1024 | bytes 8192 | tf_op jit(solution)/shard_map/psum | solution.py:127
  755.8 1.0 copy.66
  756.8 330.8 %all-reduce.7.cloned.1.call-done = bf16[3,2048,128]{2,0,1:T(4,128)(2,1)} async-done(((bf16[3,2048,128]{2,0,1:T(4,128)(2,1)}), bf16[3,2048,128]{2,0,1:T(4,128)(2,1)}) %all-reduce.7.cloned.1.call-update) | async-done | bytes 1572880
  (411 shorter events, 108.5 us)
Async XLA Ops:
  7.2 241.4 %all-gather.3.cloned.1.call-start = ((), (), s32[]{:S(2)}) async-start(), calls=%async_computation.2 | async-start | bytes 1622016 | tf_op jit(solution)/shard_map/all_gather | solution.py:45
  7.9 418.2 %all-gather.5.cloned.1.call-start = ((), (), s32[]{:S(2)}) async-start(), calls=%async_computation.3 | async-start | bytes 8912896 | tf_op jit(solution)/shard_map/all_gather | solution.py:44
  11.0 31.6 %copy-start.12 = (f32[8,128]{1,0:T(8,128)S(1)}, f32[8,128]{1,0:T(8,128)}, u32[]{:S(2)}) copy-start(f32[8,128]{1,0:T(8,128)} %param.11) | copy-start | bytes 12292
  24.0 416.7 %all-to-all-start.1 = ((bf16[16,2,8192]{2,1,0:T(2,128)(2,1)}), bf16[16,2,8192]{2,1,0:T(2,128)(2,1)}, u32[]{:S(2)}, u32[]{:S(2)}) async-start(bf16[16,2,8192]{2,1,0:T(2,128)(2,1)} %reshape.167), calls=%async_computation.1 | async-start | bytes 1048576 | tf_op jit(solution)/shard_map/all_to_all | solution.py:68
  113.4 2.5 copy-start.11
  435.1 1.8 copy-start.2
  435.1 5.4 copy-start.8
  435.9 4.6 copy-start.6
  436.9 25.0 %collective-permute-start = (bf16[16,127,128]{1,2,0:T(8,128)(2,1)}, bf16[16,127,128]{1,2,0:T(8,128)(2,1)}, u32[]{:S(2)}, u32[]{:S(2)}) collective-permute-start(bf16[16,127,128]{1,2,0:T(8,128)(2,1)} %slice.45), channel_id=1, source_target_pairs={{0,1},{1,2},{2,3},{3,4},{4,5},{5,6},{6,7},{7,8},{8,9},{9,10},{10,1... | collective-permute-start | bytes 1560584 | tf_op jit(solution)/shard_map/ppermute | solution.py:9
  444.2 3.0 copy-start.9
  447.2 15.9 %copy-start.7 = (bf16[16,128,128]{1,2,0:T(8,128)(2,1)S(1)}, bf16[16,128,128]{1,2,0:T(8,128)(2,1)}, u32[]{:S(2)}) copy-start(bf16[16,128,128]{1,2,0:T(8,128)(2,1)} %copy-done.6) | copy-start | bytes 1572868
  500.8 2.1 copy-start.4
  504.2 1.6 copy-start.5
  505.8 2.1 copy-start.4
  509.2 1.6 copy-start.5
  510.8 2.1 copy-start.4
  514.2 1.6 copy-start.5
  515.8 2.1 copy-start.4
  519.2 1.6 copy-start.5
  520.8 2.1 copy-start.4
  524.2 1.6 copy-start.5
  525.9 2.1 copy-start.4
  529.2 1.6 copy-start.5
  530.9 2.1 copy-start.4
  534.2 1.6 copy-start.5
  535.9 2.1 copy-start.4
  539.2 1.6 copy-start.5
  540.9 2.1 copy-start.4
  544.2 1.6 copy-start.5
  545.9 2.1 copy-start.4
  549.2 1.6 copy-start.5
  550.9 2.1 copy-start.4
  554.3 1.6 copy-start.5
  555.9 2.1 copy-start.4
  559.3 1.6 copy-start.5
  560.9 2.1 copy-start.4
  564.3 1.6 copy-start.5
  565.9 2.1 copy-start.4
  569.3 1.6 copy-start.5
  570.9 2.1 copy-start.4
  574.3 1.6 copy-start.5
  575.9 2.1 copy-start.4
  583.1 32.0 %collective-permute-start.1 = (bf16[16,127,128]{1,2,0:T(8,128)(2,1)}, bf16[16,127,128]{1,2,0:T(8,128)(2,1)S(1)}, u32[]{:S(2)}, u32[]{:S(2)}) collective-permute-start(bf16[16,127,128]{1,2,0:T(8,128)(2,1)} %slice.59), channel_id=1, source_target_pairs={{0,31},{1,0},{2,1},{3,2},{4,3},{5,4},{6,5},{7,6},{8,7},{9,8},{10,9... | collective-permute-start | bytes 1560584 | tf_op jit(solution)/shard_map/ppermute | solution.py:9
  587.9 167.9 %all-to-all-start = ((bf16[16,128,128]{1,2,0:T(8,128)(2,1)}), bf16[16,128,128]{1,2,0:T(8,128)(2,1)S(1)}, u32[]{:S(2)}, u32[]{:S(2)}) async-start(bf16[16,128,128]{1,2,0:T(8,128)(2,1)} %get-tuple-element.113), calls=%async_computation | async-start | bytes 1048576 | tf_op jit(solution)/shard_map/all_to_all | solution.py:65
  593.2 22.2 %copy-start.1 = (f32[16,8,16,128]{3,2,1,0:T(8,128)S(1)}, f32[16,8,16,128]{3,2,1,0:T(8,128)}, u32[]{:S(2)}) copy-start(f32[16,8,16,128]{3,2,1,0:T(8,128)} %copy-done) | copy-start | bytes 3145732
  593.2 22.2 %copy-start.3 = (f32[16,8,16,128]{3,2,1,0:T(8,128)S(1)}, f32[16,8,16,128]{3,2,1,0:T(8,128)}, u32[]{:S(2)}) copy-start(f32[16,8,16,128]{3,2,1,0:T(8,128)} %copy-done.2) | copy-start | bytes 3145732
  593.2 494.5 %all-reduce.7.cloned.1.call-start = ((), (), s32[]{:S(2)}) async-start(), calls=%async_computation.4 | async-start | bytes 4194304
  617.8 2.0 copy-start.10
  (2 other events, 2.6 us)
Sparse Core Ops, SparseCore 0:
  10.1 238.4 all-gather.2
  251.9 174.1 all-gather.4
  629.4 458.1 all-reduce.6
where the time goes:
time: 1100 us
  waiting for transfers between devices  677 us (62%)
  local copies, waits for them, and re-layouts  178 us (16%)
  blocking collectives  125 us (11%)
  matrix products  42.9 us (4%)
  starting transfers between devices  29.6 us (3%)
  other arithmetic  28.1 us (3%)
  between operations  14.8 us (1%)
    unnamed x4, waiting for transfers between devices  332 us
    all_gather x1, waiting for transfers between devices, body(): gathered = lax.all_gather(tokens, 'ctx', axis=0, tiled=True)  178 us
    all_gather x1, waiting for transfers between devices, body(): rows_all = lax.all_gather(in_weight, 'zero', axis=1, tiled=True)  132 us
    psum x1, blocking collectives, body(): grad_filters = lax.psum(jnp.sum(filter_terms, axis=0), 'zero')  125 us
    gather x3, local copies, waits for them, and re-layouts, body(): filters[:, jnp.clip(tap_lag, 0, tap_count - 1)]  72.9 us
    ppermute x2, waiting for transfers between devices, passed_along(): lax.ppermute(shard, axis, [(i, (i + by) % count) for i in range(count)])  35.4 us
    dynamic_slice x32, local copies, waits for them, and re-layouts, body(): mixed = lax.map(joined_block, (extended, keep_mask))  27.1 us
  transfers between devices with their start and end apart: 7, of which 5 were waited for; matrix products, arithmetic and copies ran while one was open for 12% of the time, Pallas kernels for 0%

commit v1 on v0

v1 whole, which is shorter than its diff:
```python
import jax
import jax.numpy as jnp
from jax import lax
from jax.experimental import pallas as pl
from jax.experimental.pallas import tpu as pltpu
from jax.sharding import Mesh, PartitionSpec as P

BF = jnp.bfloat16
F32 = jnp.float32
LANES = 128
GSIZE = 16
PER = LANES // GSIZE
CTX = ("z_hi", "y", "core")
ZERO = ("z_lo", "x")
TOK_AX = ("y", "core")
Z_AX = ("z_hi", "z_lo")
SEQ_AX = ("z_hi", "z_lo", "x")


def swap_blocks(pieces, axes):
    return lax.all_to_all(pieces, axes, split_axis=0, concat_axis=0, tiled=True)


def spread(shard, axes):
    count = lax.axis_size(axes)
    return swap_blocks(jnp.broadcast_to(shard[None], (count,) + shard.shape), axes)


def iotas():
    rows = lax.broadcasted_iota(jnp.int32, (LANES, LANES), 0)
    cols = lax.broadcasted_iota(jnp.int32, (LANES, LANES), 1)
    return rows, cols


def group_lanes(block, g):
    lane = lax.broadcasted_iota(jnp.int32, block.shape, 1)
    return jnp.where(lane // GSIZE == g, block, jnp.zeros_like(block))


def circulants(taps_ref, table_ref):
    for g in range(taps_ref.shape[0]):
        rows = jnp.broadcast_to(taps_ref[g : g + 1, :], (LANES, LANES))
        table_ref[g] = pltpu.roll(rows, 0, 1, stride=1, stride_axis=0).astype(BF)


def back_kernel(off_ref, taps_ref, q_ref, cot_ref, prev_ref, own_ref, table):
    @pl.when(pl.program_id(0) == 0)
    def _():
        circulants(taps_ref, table)

    u, t = iotas()
    off = jnp.broadcast_to(off_ref[0], (LANES, LANES))
    lag = t - u
    m_own = jnp.where((lag >= 0) & (lag <= off), 1.0, 0.0).astype(BF)
    m_prev = jnp.where((lag < 0) & (lag + LANES <= off), 1.0, 0.0).astype(BF)
    grad = (cot_ref[0].astype(F32) * q_ref[0].astype(F32)).astype(BF)
    for half in range(grad.shape[1] // LANES):
        cols = slice(half * LANES, (half + 1) * LANES)
        g_half = grad[:, cols]
        right = jnp.concatenate([group_lanes(g_half, g) for g in range(PER)], 0)
        tabs = [table[half * PER + g] for g in range(PER)]
        prev = jnp.concatenate([tab * m_prev for tab in tabs], 1)
        own = jnp.concatenate([tab * m_own for tab in tabs], 1)
        prev_ref[0, :, cols] = jnp.dot(prev, right, preferred_element_type=F32).astype(BF)
        own_ref[0, :, cols] = jnp.dot(own, right, preferred_element_type=F32)


def front_kernel(off_ref, taps_ref, q_ref, cot_ref, prod_ref, halo_ref, gated_ref, gq_ref, df_ref, table, acc):
    step = pl.program_id(0)

    @pl.when(step == 0)
    def _():
        circulants(taps_ref, table)
        acc[...] = jnp.zeros_like(acc)

    t, u = iotas()
    off = jnp.broadcast_to(off_ref[0], (LANES, LANES)).T
    lag = t - u
    is_own = (lag >= 0) & (lag <= off)
    is_prev = (lag < 0) & (lag + LANES <= off)
    m_own = jnp.where(is_own, 1.0, 0.0).astype(BF)
    m_prev = jnp.where(is_prev, 1.0, 0.0).astype(BF)
    q = q_ref[0].astype(F32)
    cot = cot_ref[0].astype(F32)
    grad = (cot * q).astype(BF)
    for half in range(grad.shape[1] // LANES):
        cols = slice(half * LANES, (half + 1) * LANES)
        ext = jnp.concatenate([halo_ref[0, :, cols], prod_ref[0, :, cols]], 0)
        right = jnp.concatenate([group_lanes(ext, g) for g in range(PER)], 0)
        left = []
        for g in range(PER):
            tab = table[half * PER + g]
            left += [tab * m_prev, tab * m_own]
        mixed = jnp.dot(jnp.concatenate(left, 1), right, preferred_element_type=F32)
        gated_ref[0, :, cols] = (q[:, cols] * mixed).astype(BF)
        gq_ref[0, :, cols] = (cot[:, cols] * mixed).astype(BF)
        g_half = grad[:, cols]
        rows = jnp.concatenate([group_lanes(g_half, g) for g in range(PER)], 0)
        sums = lax.dot_general(rows, ext, (((1,), (1,)), ((), ())), preferred_element_type=F32)
        for g in range(PER):
            part = sums[g * LANES : (g + 1) * LANES]
            picked = jnp.where(is_own, part[:, LANES:], jnp.where(is_prev, part[:, :LANES], 0.0))
            acc[half * PER + g] += picked

    @pl.when(step == pl.num_programs(0) - 1)
    def _():
        for g in range(acc.shape[0]):
            lined = acc[g]
            for bit in range(7):
                turned = pltpu.roll(lined, LANES - (1 << bit), 1)
                lined = jnp.where((t >> bit) & 1 == 1, turned, lined)
            df_ref[g : g + 1, :] = jnp.sum(lined, axis=0, keepdims=True)


def block_spec(width):
    return pl.BlockSpec((1, LANES, width), lambda i: (i, 0, 0))


def whole_spec(shape):
    return pl.BlockSpec(shape, lambda i: (0,) * len(shape))


PARAMS = pltpu.CompilerParams(dimension_semantics=("arbitrary",), vmem_limit_bytes=40 << 20)


def back(off, taps, q, cot):
    n, _, width = q.shape
    groups = taps.shape[0]
    off_spec = pl.BlockSpec((1, 1, LANES), lambda i: (i, 0, 0))
    flops = 2 * n * 2 * LANES * LANES * PER * width
    return pl.pallas_call(
        back_kernel,
        grid=(n,),
        in_specs=[off_spec, whole_spec(taps.shape), block_spec(width), block_spec(width)],
        out_specs=[block_spec(width), block_spec(width)],
        out_shape=[jax.ShapeDtypeStruct(q.shape, BF), jax.ShapeDtypeStruct(q.shape, F32)],
        scratch_shapes=[pltpu.VMEM((groups, LANES, LANES), BF)],
        compiler_params=PARAMS,
        cost_estimate=pl.CostEstimate(flops=flops, bytes_accessed=10 * q.size, transcendentals=0),
    )(off, taps, q, cot)


def front(off, taps, q, cot, product, halo):
    n, _, width = q.shape
    groups = taps.shape[0]
    off_spec = pl.BlockSpec((1, 1, LANES), lambda i: (i, 0, 0))
    flops = 4 * n * 2 * LANES * LANES * PER * width
    return pl.pallas_call(
        front_kernel,
        grid=(n,),
        in_specs=[off_spec, whole_spec(taps.shape)] + [block_spec(width)] * 4,
        out_specs=[block_spec(width), block_spec(width), whole_spec(taps.shape)],
        out_shape=[
            jax.ShapeDtypeStruct(q.shape, BF),
            jax.ShapeDtypeStruct(q.shape, BF),
            jax.ShapeDtypeStruct(taps.shape, F32),
        ],
        scratch_shapes=[
            pltpu.VMEM((groups, LANES, LANES), BF),
            pltpu.VMEM((groups, LANES, LANES), F32),
        ],
        compiler_params=PARAMS,
        cost_estimate=pl.CostEstimate(flops=flops, bytes_accessed=12 * q.size, transcendentals=0),
    )(off, taps, q, cot, product, halo)


def seq_pairs(by, turn):
    halves = lax.axis_size("z_hi")
    zeros = lax.axis_size(ZERO)
    pairs = []
    for h in range(halves):
        for z in range(zeros):
            to = z + by
            h_to = h if 0 <= to < zeros else (h + turn) % halves
            pairs.append((h * zeros + z, h_to * zeros + to % zeros))
    return pairs


def halo_forward(product):
    most = lax.ppermute(product[:-1], SEQ_AX, seq_pairs(1, 0))
    last = lax.ppermute(product[-1:], SEQ_AX, seq_pairs(1, 1))
    first = lax.axis_index(ZERO) == 0
    return jnp.where(first, jnp.concatenate([last, most], 0), jnp.concatenate([most, last], 0))


def halo_back(grad_prev):
    first = lax.axis_index(ZERO) == 0
    most = jnp.where(first, grad_prev[1:], grad_prev[:-1])
    last = jnp.where(first, grad_prev[:1], grad_prev[-1:])
    most = lax.ppermute(most, SEQ_AX, seq_pairs(-1, 0))
    last = lax.ppermute(last, SEQ_AX, seq_pairs(-1, -1))
    return jnp.concatenate([most, last], 0)


def body(tokens, in_weight, filters, doc_offset, cotangent):
    hi, lo, xs = lax.axis_size("z_hi"), lax.axis_size("z_lo"), lax.axis_size("x")
    blocks = lax.axis_size(TOK_AX)
    rows = tokens.shape[0]
    feats, width = in_weight.shape[1:]
    wide = hi * width
    by_z = spread(in_weight, Z_AX)
    by_x = spread(by_z, "x")
    by_x = by_x.reshape(xs, hi, lo, 3, feats, width)
    weight = by_x.transpose(2, 0, 4, 3, 1, 5).reshape(lo * xs * feats, 3 * wide)
    gathered = lax.all_gather(tokens, TOK_AX, axis=0, tiled=True)
    cot = cotangent.reshape(rows, hi, blocks, width).transpose(2, 0, 1, 3).reshape(blocks, rows, wide)
    cot = swap_blocks(cot, TOK_AX)
    other = lax.ppermute(filters, "z_hi", [(i, hi - 1 - i) for i in range(hi)])
    upper = lax.axis_index("z_hi") == 0
    taps = jnp.where(upper, jnp.concatenate([filters, other], 0), jnp.concatenate([other, filters], 0))
    taps_back = jnp.roll(jnp.flip(taps, 1), 1, axis=1)
    off = lax.dynamic_slice_in_dim(doc_offset, lax.axis_index("z_hi") * blocks, blocks, 0)[:, None, :]

    projected = jnp.dot(gathered, weight, preferred_element_type=F32).astype(BF)
    projected = projected.reshape(blocks, rows, 3, wide)
    q, k, v = projected[:, :, 0], projected[:, :, 1], projected[:, :, 2]
    product = (k.astype(F32) * v.astype(F32)).astype(BF)
    halo = halo_forward(product)
    grad_prev, grad_own = back(off, taps, q, cot)
    received = halo_back(grad_prev)
    gated, grad_q, grad_taps = front(off, taps_back, q, cot, product, halo)

    out = swap_blocks(gated, TOK_AX)
    out = out.reshape(blocks, rows, hi, width).transpose(1, 2, 0, 3).reshape(rows, -1)

    grad_product = grad_own + received.astype(F32)
    grad_k = (grad_product * v.astype(F32)).astype(BF)
    grad_v = (grad_product * k.astype(F32)).astype(BF)
    grads = jnp.concatenate([grad_q, grad_k, grad_v], 2).reshape(blocks * rows, 3 * wide)
    partial = lax.dot_general(gathered, grads, (((0,), (0,)), ((), ())), preferred_element_type=F32).astype(BF)
    partial = partial.reshape(lo, xs, feats, 3, hi, width).transpose(1, 4, 0, 3, 2, 5)
    over_x = jnp.sum(swap_blocks(partial, "x").astype(F32), 0).astype(BF)
    over_x = over_x.reshape(hi * lo, 3, feats, width)
    grad_weight = jnp.sum(swap_blocks(over_x, Z_AX).astype(F32), 0)

    grad_taps = jnp.roll(jnp.flip(grad_taps, 1), 1, axis=1)
    grad_taps = jnp.sum(spread(grad_taps, "x"), 0).reshape(hi, 1, -1, LANES)
    grad_taps = jnp.broadcast_to(grad_taps, (hi, lo) + grad_taps.shape[2:])
    grad_taps = jnp.sum(swap_blocks(grad_taps.reshape(hi * lo, -1, LANES), Z_AX), 0)
    return (out, grad_weight, grad_taps)


def sharded(mesh):
    return jax.shard_map(
        body,
        mesh=mesh,
        in_specs=(P(CTX + ZERO, None), P(None, ZERO, CTX), P(CTX, None), P(None, ZERO), P(CTX + ZERO, None)),
        out_specs=(P(CTX + ZERO, None), P(None, ZERO, CTX), P(CTX, None)),
        check_vma=False,
    )


def solution(mesh):
    return sharded(Mesh(mesh.devices.reshape(2, 4, 2, 8, 4), CTX + ZERO))
```

time: 1100 us -> 354 us (0.32)
  the two profiles are of different devices: /device:TPU:8 before, /device:TPU:32 now
where the time goes in v1:
time: 354 us; the launch traced here: 353 us
  waiting for transfers between devices  96.9 us (27%)
  blocking collectives  95 us (27%)
  starting transfers between devices  58.6 us (17%)
  local copies, waits for them, and re-layouts  47.1 us (13%)
  Pallas kernels  16.8 us (5%)
  matrix products  14.9 us (4%)
  between operations  14.3 us (4%)
  other arithmetic  9.01 us (3%)
    all_to_all x2, blocking collectives, swap_blocks(): return lax.all_to_all(pieces, axes, split_axis=0, concat_axis=0, tiled=True)  95 us
    all_to_all x6, waiting for transfers between devices, swap_blocks(): return lax.all_to_all(pieces, axes, split_axis=0, concat_axis=0, tiled=True)  64.2 us
    all_to_all x6, starting transfers between devices, swap_blocks(): return lax.all_to_all(pieces, axes, split_axis=0, concat_axis=0, tiled=True)  44.7 us
    pallas_call x1, Pallas kernels, front(): pl.pallas_call(front_kernel, grid=(n,), in_specs=[off_spec, whole_spec(ta...  12.9 us
    ppermute x1, waiting for transfers between devices, halo_forward(): last = lax.ppermute(product[-1:], SEQ_AX, seq_pairs(1, 1))  12.4 us
    ppermute x1, waiting for transfers between devices, halo_back(): last = lax.ppermute(last, SEQ_AX, seq_pairs(-1, -1))  12.3 us
    reshape x1, local copies, waits for them, and re-layouts, body(): weight = by_x.transpose(2, 0, 4, 3, 1, 5).reshape(lo * xs * feats, 3 * wide)  8.02 us
    dot_general x1, matrix products, body(): projected = jnp.dot(gathered, weight, preferred_element_type=F32).astype(BF)  7.81 us
  transfers between devices with their start and end apart: 12, of which 7 were waited for; matrix products, arithmetic and copies ran while one was open for 19% of the time, Pallas kernels for 0%

profile of v1, /device:TPU:32, one launch (start us, length us, event | category | flops | bytes accessed | tf_op | source)
XLA Modules:
  0.0 352.6 jit_solution(18119073256558479469)
XLA Ops:
  7.2 0.7 all-gather.2.cloned.1.call-update
  7.9 1.0 broadcast_in_dim.13
  8.9 56.5 %all_to_all.40 = bf16[16,3,64,128]{3,2,1,0:T(8,128)(2,1)S(1)} all-to-all(bf16[16,3,64,128]{3,2,1,0:T(8,128)(2,1)S(1)} %broadcast_in_dim.13), channel_id=1, replica_groups=mesh['z_hi'=2,'y'=4,'core'=2,'z_lo'=8,'x'=4] {'z_hi','z_lo'}, dimensions={0} | all-to-all | bytes 1572864 | tf_op jit(solution)/shard_map/all_to_all | solution.py:21
  65.4 2.5 broadcast_in_dim.14
  67.9 4.8 %all-to-all-start.1 = ((bf16[4,16,3,64,128]{4,3,2,1,0:T(8,128)(2,1)}), bf16[4,16,3,64,128]{4,3,2,1,0:T(8,128)(2,1)}, u32[]{:S(2)}, u32[]{:S(2)}) async-start(bf16[4,16,3,64,128]{4,3,2,1,0:T(8,128)(2,1)} %broadcast_in_dim.14), calls=%async_computation.1 | async-start | bytes 6291456 | tf_op jit(solution)/shard_map/all_to_all | solution.py:21
  72.7 5.2 %collective-permute-start = (f32[8,128]{1,0:T(8,128)S(1)}, f32[8,128]{1,0:T(8,128)S(1)}, u32[]{:S(2)}, u32[]{:S(2)}) collective-permute-start(f32[8,128]{1,0:T(8,128)S(1)} %copy-done.5), channel_id=1, source_target_pairs={{0,256},{256,0},{1,257},{257,1},{2,258},{258,2},{3,259},{259,3},{4... | collective-permute-start | bytes 12296 | tf_op jit(solution)/shard_map/ppermute | solution.py:208
  78.0 0.1 copy.63
  78.1 0.4 copy.80
  78.5 1.1 reshape.52
  79.6 7.3 %collective-permute-done = f32[8,128]{1,0:T(8,128)S(1)} collective-permute-done((f32[8,128]{1,0:T(8,128)S(1)}, f32[8,128]{1,0:T(8,128)S(1)}, u32[]{:S(2)}, u32[]{:S(2)}) %collective-permute-start) | collective-permute-done | bytes 4128 | tf_op jit(solution)/shard_map/ppermute | solution.py:208
  87.0 21.7 %all-to-all-done.1 = bf16[4,16,3,64,128]{4,3,2,1,0:T(8,128)(2,1)} async-done(((bf16[4,16,3,64,128]{4,3,2,1,0:T(8,128)(2,1)}), bf16[4,16,3,64,128]{4,3,2,1,0:T(8,128)(2,1)}, u32[]{:S(2)}, u32[]{:S(2)}) %all-to-all-start.1) | async-done | bytes 3145760 | tf_op jit(solution)/shard_map/all_to_all | solution.py:21
  108.7 4.5 %all-to-all-start.2 = ((bf16[8,128,256]{2,1,0:T(8,128)(2,1)}), bf16[8,128,256]{2,1,0:T(8,128)(2,1)S(1)}, u32[]{:S(2)}, u32[]{:S(2)}) async-start(bf16[8,128,256]{2,1,0:T(8,128)(2,1)} %reshape.52), calls=%async_computation.2 | async-start | bytes 1048576 | tf_op jit(solution)/shard_map/all_to_all | solution.py:21
  113.1 6.9 %copy.46 = bf16[8,4,64,3,2,128]{5,4,3,2,1,0:T(2,128)(2,1)} copy(bf16[8,4,64,3,2,128]{5,2,3,0,4,1:T(8,128)(2,1)} %bitcast.2) | data formatting | bytes 6291456 | tf_op jit(solution)/shard_map/transpose | solution.py:204
  120.0 8.0 %reshape.49 = bf16[2048,768]{1,0:T(8,128)(2,1)} reshape(bf16[8,4,64,3,2,128]{5,4,3,2,1,0:T(2,128)(2,1)} %copy.46) | data formatting | bytes 6291456 | tf_op jit(solution)/shard_map/reshape | solution.py:204
  128.0 7.8 %convolution_convert_fusion.1 = bf16[1024,768]{1,0:T(8,128)(2,1)} fusion(bf16[1024,2048]{1,0:T(8,128)(2,1)} %all-gather.2.cloned.1.call-done, bf16[2048,768]{1,0:T(8,128)(2,1)} %reshape.49), kind=kOutput, calls=%fused_computation.2 | convolution fusion | flops 3222011904 | bytes 8912896 | tf_op jit(solution)/shard_map/dot_general | solution.py:214
  135.8 4.2 %reshape.61 = bf16[8,128,3,256]{3,2,1,0:T(4,128)(2,1)S(1)} reshape(bf16[1024,768]{1,0:T(8,128)(2,1)} %convolution_convert_fusion.1) | data formatting | bytes 3145728 | tf_op jit(solution)/shard_map/reshape | solution.py:215
  140.0 3.3 fusion.4
  143.4 3.9 %shard_map.77 = (bf16[8,128,256]{2,1,0:T(8,128)(2,1)S(1)}, f32[8,128,256]{2,1,0:T(8,128)S(1)}) custom-call(s32[8,1,128]{2,1,0:T(1,128)S(1)} %bitcast.50, f32[16,128]{1,0:T(8,128)S(1)} %maximum_select_fusion.1.taps_ref, bf16[8,128,256]{2,1,0:T(8,128)(2,1)S(1)} %bitcast.46, bf16[8,128,256]{2,1,0:T(8,128)(2,1)S(1)} %all-to-all-done.2.cot_ref), custom_call_target="tpu_custom_call" | custom-call | flops 1073741824 | bytes 2621440 | tf_op jit(solution)/shard_map/pallas_call | solution.py:131
  147.3 1.9 collective-permute-start.3
  149.3 1.9 collective-permute-start.4
  151.2 12.3 %collective-permute-done.4 = bf16[1,128,256]{2,1,0:T(8,128)(2,1)S(1)} collective-permute-done((bf16[1,128,256]{2,1,0:T(8,128)(2,1)S(1)}, bf16[1,128,256]{2,1,0:T(8,128)(2,1)S(1)}, u32[]{:S(2)}, u32[]{:S(2)}) %collective-permute-start.4) | collective-permute-done | bytes 65568 | tf_op jit(solution)/shard_map/ppermute | solution.py:191
  163.6 1.3 fusion.1
  164.9 2.5 collective-permute-start.2
  167.5 2.4 collective-permute-start.1
  170.0 12.4 %collective-permute-done.1 = bf16[1,128,256]{2,1,0:T(8,128)(2,1)S(1)} collective-permute-done((bf16[1,128,256]{2,1,0:T(8,128)(2,1)S(1)}, bf16[1,128,256]{2,1,0:T(8,128)(2,1)S(1)}, u32[]{:S(2)}, u32[]{:S(2)}) %collective-permute-start.1) | collective-permute-done | bytes 65568 | tf_op jit(solution)/shard_map/ppermute | solution.py:181
  182.5 12.9 %shard_map.76 = (bf16[8,128,256]{2,1,0:T(8,128)(2,1)}, bf16[8,128,256]{2,1,0:T(8,128)(2,1)S(1)}, f32[16,128]{1,0:T(8,128)S(1)}) custom-call(s32[8,1,128]{2,1,0:T(1,128)S(1)} %bitcast.51, f32[16,128]{1,0:T(8,128)S(1)} %pad_maximum_fusion.2.taps_ref, bf16[8,128,256]{2,1,0:T(8,128)(2,1)S(1)} %bitcast.47, bf16[8,128,256]{2,1,0:T(8,128)(2,1)S(1)} %all-to-all-done.2.cot_ref, ...), custom_call_target="tpu_custom_call" | custom-call | flops 2147483648 | bytes 3145728 | tf_op jit(solution)/shard_map/pallas_call | solution.py:148
  195.7 0.6 broadcast_in_dim.15
  196.3 3.3 all-to-all-start.6
  199.6 0.1 pad_maximum_fusion
  199.7 5.3 %all-to-all-done.6 = f32[4,16,128]{2,1,0:T(8,128)S(1)} async-done(((f32[4,16,128]{2,1,0:T(8,128)}), f32[4,16,128]{2,1,0:T(8,128)S(1)}, u32[]{:S(2)}, u32[]{:S(2)}) %all-to-all-start.6) | async-done | bytes 32800 | tf_op jit(solution)/shard_map/all_to_all | solution.py:21
  205.0 0.6 broadcast_in_dim.33
  205.6 15.7 %all-to-all-start.7 = ((f32[16,8,128]{2,1,0:T(8,128)}), f32[16,8,128]{2,1,0:T(8,128)S(1)}, u32[]{:S(2)}, u32[]{:S(2)}) async-start(f32[16,8,128]{2,1,0:T(8,128)} %bitcast.15), calls=%async_computation.7 | async-start | bytes 131072 | tf_op jit(solution)/shard_map/all_to_all | solution.py:21
  221.3 7.1 %fusion = bf16[2048,768]{0,1:T(8,128)(2,1)} fusion(bf16[1024,768]{1,0:T(8,128)(2,1)S(1)} %bitcast.57, bf16[1024,2048]{1,0:T(8,128)(2,1)} %all-gather.2.cloned.1.call-done), kind=kOutput, calls=%fused_computation.1 | convolution fusion | flops 3222798336 | bytes 8912896 | tf_op jit(solution)/shard_map/dot_general | solution.py:230
  228.4 3.2 copy.53
  231.6 2.4 reshape.56
  234.0 7.3 %copy.54 = bf16[4,2,8,3,64,128]{5,1,3,4,2,0:T(2,128)(2,1)} copy(bf16[4,2,8,3,64,128]{5,1,3,4,0,2:T(2,128)(2,1)} %bitcast.52) | data formatting | bytes 6291456 | tf_op jit(solution)/shard_map/transpose | solution.py:231
  241.3 38.5 %all_to_all.41 = bf16[4,2,8,3,64,128]{5,1,3,4,2,0:T(2,128)(2,1)S(1)} all-to-all(bf16[4,2,8,3,64,128]{5,1,3,4,2,0:T(2,128)(2,1)} %copy.54), channel_id=1, replica_groups=mesh['z_hi'=2,'y'=4,'core'=2,'z_lo'=8,'x'=4] {'x'}, dimensions={0} | all-to-all | bytes 6291456 | tf_op jit(solution)/shard_map/all_to_all | solution.py:21
  279.8 4.4 %all-to-all-start.3 = ((bf16[8,128,256]{2,1,0:T(8,128)(2,1)}), bf16[8,128,256]{2,1,0:T(8,128)(2,1)}, u32[]{:S(2)}, u32[]{:S(2)}) async-start(bf16[8,128,256]{2,1,0:T(8,128)(2,1)} %get-tuple-element.8), calls=%async_computation.3 | async-start | bytes 1048576 | tf_op jit(solution)/shard_map/all_to_all | solution.py:21
  284.3 6.0 %reduce_sum.39 = bf16[2,8,3,64,128]{4,0,2,3,1:T(2,128)(2,1)} reduce(bf16[4,2,8,3,64,128]{5,1,3,4,2,0:T(2,128)(2,1)S(1)} %all_to_all.41, bf16[]{:T(256)} %constant.25.clone.1), dimensions={0}, to_apply=%region_0.1 | reduce | flops 1179648 | bytes 3932162 | tf_op jit(solution)/shard_map/reduce_sum | solution.py:232
  290.3 2.2 copy.56
  292.5 1.9 all-to-all-done.3
  294.3 12.0 %all-to-all-start.5 = ((bf16[16,3,64,128]{3,2,1,0:T(8,128)(2,1)}), bf16[16,3,64,128]{3,2,1,0:T(8,128)(2,1)S(1)}, u32[]{:S(2)}, u32[]{:S(2)}) async-start(bf16[16,3,64,128]{3,2,1,0:T(8,128)(2,1)} %bitcast.13), calls=%async_computation.5 | async-start | bytes 1572864 | tf_op jit(solution)/shard_map/all_to_all | solution.py:21
  306.4 0.6 reduce_sum.42
  307.0 1.2 reshape.53
  308.2 0.6 copy.52
  308.8 0.9 copy.78
  309.7 35.3 %all-to-all-done.5 = bf16[16,3,64,128]{3,2,1,0:T(8,128)(2,1)S(1)} async-done(((bf16[16,3,64,128]{3,2,1,0:T(8,128)(2,1)}), bf16[16,3,64,128]{3,2,1,0:T(8,128)(2,1)S(1)}, u32[]{:S(2)}, u32[]{:S(2)}) %all-to-all-start.5) | async-done | bytes 786464 | tf_op jit(solution)/shard_map/all_to_all | solution.py:21
  345.0 0.8 convert_reduce_fusion
  (33 shorter events, 0.8 us)
Async XLA Ops:
  7.2 70.8 %copy-start = (s32[16,128]{1,0:T(8,128)S(1)}, s32[16,128]{1,0:T(8,128)}, u32[]{:S(2)}) copy-start(s32[16,128]{1,0:T(8,128)} %param.8) | copy-start | bytes 24580
  7.2 120.8 %all-gather.2.cloned.1.call-start = ((), (), s32[]{:S(2)}) async-start(), calls=%async_computation.8 | async-start | bytes 4718592 | tf_op jit(solution)/shard_map/all_gather | solution.py:205
  67.9 4.8 %copy-start.5 = (f32[8,128]{1,0:T(8,128)S(1)}, f32[8,128]{1,0:T(8,128)}, u32[]{:S(2)}) copy-start(f32[8,128]{1,0:T(8,128)} %param.7) | copy-start | bytes 12292
  67.9 10.0 %copy-start.4 = (bf16[128,2048]{1,0:T(8,128)(2,1)S(1)}, bf16[128,2048]{1,0:T(8,128)(2,1)}, u32[]{:S(2)}) copy-start(bf16[128,2048]{1,0:T(8,128)(2,1)} %param.9) | copy-start | bytes 1572868
  67.9 40.7 %all-to-all-start.1 = ((bf16[4,16,3,64,128]{4,3,2,1,0:T(8,128)(2,1)}), bf16[4,16,3,64,128]{4,3,2,1,0:T(8,128)(2,1)}, u32[]{:S(2)}, u32[]{:S(2)}) async-start(bf16[4,16,3,64,128]{4,3,2,1,0:T(8,128)(2,1)} %broadcast_in_dim.14), calls=%async_computation.1 | async-start | bytes 6291456 | tf_op jit(solution)/shard_map/all_to_all | solution.py:21
  72.7 14.2 %collective-permute-start = (f32[8,128]{1,0:T(8,128)S(1)}, f32[8,128]{1,0:T(8,128)S(1)}, u32[]{:S(2)}, u32[]{:S(2)}) collective-permute-start(f32[8,128]{1,0:T(8,128)S(1)} %copy-done.5), channel_id=1, source_target_pairs={{0,256},{256,0},{1,257},{257,1},{2,258},{258,2},{3,259},{259,3},{4... | collective-permute-start | bytes 12296 | tf_op jit(solution)/shard_map/ppermute | solution.py:208
  108.7 34.7 %all-to-all-start.2 = ((bf16[8,128,256]{2,1,0:T(8,128)(2,1)}), bf16[8,128,256]{2,1,0:T(8,128)(2,1)S(1)}, u32[]{:S(2)}, u32[]{:S(2)}) async-start(bf16[8,128,256]{2,1,0:T(8,128)(2,1)} %reshape.52), calls=%async_computation.2 | async-start | bytes 1048576 | tf_op jit(solution)/shard_map/all_to_all | solution.py:21
  143.4 20.2 %copy-start.1 = (bf16[8,128,1,256]{3,2,1,0:T(2,128)(2,1)S(1)}, bf16[8,128,1,256]{3,2,1,0:T(2,128)(2,1)}, u32[]{:S(2)}) copy-start(bf16[8,128,1,256]{3,2,1,0:T(2,128)(2,1)} %get-tuple-element.13) | copy-start | bytes 1572868
  143.4 20.2 %copy-start.2 = (bf16[8,128,1,256]{3,2,1,0:T(2,128)(2,1)S(1)}, bf16[8,128,1,256]{3,2,1,0:T(2,128)(2,1)}, u32[]{:S(2)}) copy-start(bf16[8,128,1,256]{3,2,1,0:T(2,128)(2,1)} %get-tuple-element.14) | copy-start | bytes 1572868
  147.3 16.2 %collective-permute-start.3 = (bf16[7,128,256]{2,1,0:T(8,128)(2,1)S(1)}, bf16[7,128,256]{2,1,0:T(8,128)(2,1)S(1)}, u32[]{:S(2)}, u32[]{:S(2)}) collective-permute-start(bf16[7,128,256]{2,1,0:T(8,128)(2,1)S(1)} %slice_select_fusion), channel_id=1, source_target_pairs={{0,31},{1,0},{2,1},{3,2},{4,3},{5,4},{6,5},{7,6},{8,7},{9,8},{10,9... | collective-permute-start | bytes 1376264 | tf_op jit(solution)/shard_map/ppermute | solution.py:190
  149.3 14.3 %collective-permute-start.4 = (bf16[1,128,256]{2,1,0:T(8,128)(2,1)S(1)}, bf16[1,128,256]{2,1,0:T(8,128)(2,1)S(1)}, u32[]{:S(2)}, u32[]{:S(2)}) collective-permute-start(bf16[1,128,256]{2,1,0:T(8,128)(2,1)S(1)} %slice_select_fusion.1), channel_id=1, source_target_pairs={{0,287},{1,0},{2,1},{3,2},{4,3},{5,4},{6,5},{7,6},{8,7},{9,8},{10,... | collective-permute-start | bytes 196616 | tf_op jit(solution)/shard_map/ppermute | solution.py:191
  164.9 17.6 %collective-permute-start.2 = (bf16[7,128,256]{2,1,0:T(8,128)(2,1)S(1)}, bf16[7,128,256]{2,1,0:T(8,128)(2,1)S(1)}, u32[]{:S(2)}, u32[]{:S(2)}) collective-permute-start(bf16[7,128,256]{2,1,0:T(8,128)(2,1)S(1)} %slice.70), channel_id=1, source_target_pairs={{0,1},{1,2},{2,3},{3,4},{4,5},{5,6},{6,7},{7,8},{8,9},{9,10},{10,1... | collective-permute-start | bytes 1376264 | tf_op jit(solution)/shard_map/ppermute | solution.py:180
  167.5 14.9 %collective-permute-start.1 = (bf16[1,128,256]{2,1,0:T(8,128)(2,1)S(1)}, bf16[1,128,256]{2,1,0:T(8,128)(2,1)S(1)}, u32[]{:S(2)}, u32[]{:S(2)}) collective-permute-start(bf16[1,128,256]{2,1,0:T(8,128)(2,1)S(1)} %slice.69), channel_id=1, source_target_pairs={{0,1},{1,2},{2,3},{3,4},{4,5},{5,6},{6,7},{7,8},{8,9},{9,10},{10,1... | collective-permute-start | bytes 196616 | tf_op jit(solution)/shard_map/ppermute | solution.py:181
  182.5 17.0 %copy-start.3 = (bf16[8,128,256]{2,1,0:T(8,128)(2,1)S(1)}, bf16[8,128,256]{2,1,0:T(8,128)(2,1)}, u32[]{:S(2)}) copy-start(bf16[8,128,256]{2,1,0:T(8,128)(2,1)} %get-tuple-element.17) | copy-start | bytes 1572868
  196.3 8.7 %all-to-all-start.6 = ((f32[4,16,128]{2,1,0:T(8,128)}), f32[4,16,128]{2,1,0:T(8,128)S(1)}, u32[]{:S(2)}, u32[]{:S(2)}) async-start(f32[4,16,128]{2,1,0:T(8,128)} %broadcast_in_dim.15), calls=%async_computation.6 | async-start | bytes 65536 | tf_op jit(solution)/shard_map/all_to_all | solution.py:21
  205.6 35.7 %all-to-all-start.7 = ((f32[16,8,128]{2,1,0:T(8,128)}), f32[16,8,128]{2,1,0:T(8,128)S(1)}, u32[]{:S(2)}, u32[]{:S(2)}) async-start(f32[16,8,128]{2,1,0:T(8,128)} %bitcast.15), calls=%async_computation.7 | async-start | bytes 131072 | tf_op jit(solution)/shard_map/all_to_all | solution.py:21
  279.8 14.5 %all-to-all-start.3 = ((bf16[8,128,256]{2,1,0:T(8,128)(2,1)}), bf16[8,128,256]{2,1,0:T(8,128)(2,1)}, u32[]{:S(2)}, u32[]{:S(2)}) async-start(bf16[8,128,256]{2,1,0:T(8,128)(2,1)} %get-tuple-element.8), calls=%async_computation.3 | async-start | bytes 1048576 | tf_op jit(solution)/shard_map/all_to_all | solution.py:21
  294.3 50.7 %all-to-all-start.5 = ((bf16[16,3,64,128]{3,2,1,0:T(8,128)(2,1)}), bf16[16,3,64,128]{3,2,1,0:T(8,128)(2,1)S(1)}, u32[]{:S(2)}, u32[]{:S(2)}) async-start(bf16[16,3,64,128]{3,2,1,0:T(8,128)(2,1)} %bitcast.13), calls=%async_computation.5 | async-start | bytes 1572864 | tf_op jit(solution)/shard_map/all_to_all | solution.py:21
Sparse Core Ops, SparseCore 0:
  10.2 43.9 all-gather.1

commit v2 on v1

v2 whole, which is shorter than its diff:
```python
import jax
import jax.numpy as jnp
from jax import lax
from jax.experimental import pallas as pl
from jax.experimental.pallas import tpu as pltpu
from jax.sharding import Mesh, PartitionSpec as P

BF = jnp.bfloat16
F32 = jnp.float32
LANES = 128
HALF = 64
GSIZE = 16
PER = LANES // GSIZE
EXTRA = 16
CTX = ("z_hi", "y", "core")
ZERO = ("z_p", "z_c", "x")
TOK_AX = ("y", "core", "z_c")
Z_AX = ("z_hi", "z_p", "z_c")
SEQ_AX = ("z_hi", "z_p", "x")


def swap_blocks(pieces, axes):
    return lax.all_to_all(pieces, axes, split_axis=0, concat_axis=0, tiled=True)


def turned(shard, axis, by):
    count = lax.axis_size(axis)
    return lax.ppermute(shard, axis, [(i, (i + by) % count) for i in range(count)])


def iotas():
    rows = lax.broadcasted_iota(jnp.int32, (LANES, LANES), 0)
    cols = lax.broadcasted_iota(jnp.int32, (LANES, LANES), 1)
    return rows, cols


def group_lanes(block, g):
    lane = lax.broadcasted_iota(jnp.int32, block.shape, 1)
    return jnp.where(lane // GSIZE == g, block, jnp.zeros_like(block))


def lane_halves(first, second):
    low = lax.broadcasted_iota(jnp.int32, first.shape, 1) < HALF
    return (
        jnp.where(low, first, pltpu.roll(second, HALF, 1)),
        jnp.where(low, pltpu.roll(first, HALF, 1), second),
    )


def circulants(taps_ref, table_ref):
    for g in range(taps_ref.shape[0]):
        rows = jnp.broadcast_to(taps_ref[g : g + 1, :], (LANES, LANES))
        table_ref[g] = pltpu.roll(rows, 0, 1, stride=1, stride_axis=0).astype(BF)


def project_kernel(x_ref, tok_ref, *refs):
    w_refs, (q_ref, k_ref, v_ref, prod_ref, table) = refs[:-5], refs[-5:]
    hi, lo, parts, short, _ = w_refs[0].shape
    xs = len(w_refs)

    @pl.when(pl.program_id(0) == 0)
    def _():
        for step, w_ref in enumerate(w_refs):
            x = lax.rem(x_ref[0] - step + xs, xs)
            for l in range(lo):
                at = pl.multiple_of((l * xs + x) * (2 * short), 2 * short)
                for p in range(parts):
                    cols = slice(p * LANES, (p + 1) * LANES)
                    top, low = lane_halves(w_ref[0, l, p].astype(F32), w_ref[1, l, p].astype(F32))
                    table[pl.ds(at, short), cols] = top.astype(BF)
                    table[pl.ds(at + short, short), cols] = low.astype(BF)

    result = jnp.dot(tok_ref[...], table[...], preferred_element_type=F32).astype(BF)
    count, rows = q_ref.shape[:2]
    q, k, v = [result[:, p * LANES : (p + 1) * LANES] for p in range(parts)]
    product = (k.astype(F32) * v.astype(F32)).astype(BF)
    for ref, side in ((q_ref, q), (k_ref, k), (v_ref, v), (prod_ref, product)):
        for j in range(count):
            ref[j] = side[j * rows : (j + 1) * rows]


def back_kernel(off_ref, taps_ref, q_ref, cot_ref, prev_ref, own_ref, table):
    @pl.when(pl.program_id(0) == 0)
    def _():
        circulants(taps_ref, table)

    u, t = iotas()
    lag = t - u
    for j in range(q_ref.shape[0]):
        off = jnp.broadcast_to(off_ref[j], (LANES, LANES))
        m_own = jnp.where((lag >= 0) & (lag <= off), 1.0, 0.0).astype(BF)
        m_prev = jnp.where((lag < 0) & (lag + LANES <= off), 1.0, 0.0).astype(BF)
        grad = (cot_ref[j].astype(F32) * q_ref[j].astype(F32)).astype(BF)
        right = jnp.concatenate([group_lanes(grad, g) for g in range(PER)], 0)
        prev = jnp.concatenate([table[g] * m_prev for g in range(PER)], 1)
        own = jnp.concatenate([table[g] * m_own for g in range(PER)], 1)
        prev_ref[j] = jnp.dot(prev, right, preferred_element_type=F32).astype(BF)
        own_ref[j] = jnp.dot(own, right, preferred_element_type=F32)


def front_kernel(off_ref, taps_ref, q_ref, cot_ref, prod_ref, halo_ref, gated_ref, gq_ref, df_ref, table, acc):
    step = pl.program_id(0)

    @pl.when(step == 0)
    def _():
        circulants(taps_ref, table)
        acc[...] = jnp.zeros_like(acc)

    t, u = iotas()
    lag = t - u
    for j in range(q_ref.shape[0]):
        off = jnp.broadcast_to(off_ref[j], (LANES, LANES)).T
        is_own = (lag >= 0) & (lag <= off)
        is_prev = (lag < 0) & (lag + LANES <= off)
        m_own = jnp.where(is_own, 1.0, 0.0).astype(BF)
        m_prev = jnp.where(is_prev, 1.0, 0.0).astype(BF)
        q = q_ref[j].astype(F32)
        cot = cot_ref[j].astype(F32)
        grad = (cot * q).astype(BF)
        ext = jnp.concatenate([halo_ref[j], prod_ref[j]], 0)
        right = jnp.concatenate([group_lanes(ext, g) for g in range(PER)], 0)
        left = []
        for g in range(PER):
            left += [table[g] * m_prev, table[g] * m_own]
        mixed = jnp.dot(jnp.concatenate(left, 1), right, preferred_element_type=F32)
        gated_ref[j] = (q * mixed).astype(BF)
        gq_ref[j] = (cot * mixed).astype(BF)
        rows = jnp.concatenate([group_lanes(grad, g) for g in range(PER)], 0)
        sums = lax.dot_general(rows, ext, (((1,), (1,)), ((), ())), preferred_element_type=F32)
        for g in range(PER):
            part = sums[g * LANES : (g + 1) * LANES]
            acc[g] += jnp.where(is_own, part[:, LANES:], jnp.where(is_prev, part[:, :LANES], 0.0))

    @pl.when(step == pl.num_programs(0) - 1)
    def _():
        for g in range(PER):
            lined = acc[g]
            for bit in range(7):
                moved = pltpu.roll(lined, LANES - (1 << bit), 1)
                lined = jnp.where((t >> bit) & 1 == 1, moved, lined)
            df_ref[g : g + 1, :] = jnp.sum(lined, axis=0, keepdims=True)


def weight_kernel(x_ref, tok_ref, gq_ref, own_ref, got_ref, k_ref, v_ref, taps_ref, out_ref, grads):
    blocks, rows, _ = own_ref.shape
    xs, hi = out_ref.shape[:2]
    short = (out_ref.shape[3] - EXTRA) // 3

    @pl.when(pl.program_id(0) == 0)
    def _():
        for j in range(blocks):
            grad = own_ref[j] + got_ref[j].astype(F32)
            at = slice(j * rows, (j + 1) * rows)
            grads[at, :LANES] = gq_ref[j]
            grads[at, LANES : 2 * LANES] = (grad * v_ref[j].astype(F32)).astype(BF)
            grads[at, 2 * LANES :] = (grad * k_ref[j].astype(F32)).astype(BF)

    result = lax.dot_general(tok_ref[...], grads[...], (((0,), (0,)), ((), ())), preferred_element_type=F32)
    for x in range(xs):
        slot = lax.rem(x - x_ref[0] + xs, xs)
        for p in range(3):
            block = result[x * 2 * short : (x + 1) * 2 * short, p * LANES : (p + 1) * LANES]
            for h, piece in enumerate(lane_halves(block[:short], block[short:])):
                out_ref[slot, h, 0, p * short : (p + 1) * short] = piece.astype(BF)
        for h in range(hi):
            out_ref[slot, h, 0, 3 * short :] = taps_ref[h]


def block_spec(count):
    return pl.BlockSpec((count, LANES, LANES), lambda i: (i, 0, 0))


def whole_spec(shape):
    return pl.BlockSpec(shape, lambda i: (0,) * len(shape))


SCALAR = pl.BlockSpec(memory_space=pltpu.SMEM)
PARAMS = pltpu.CompilerParams(dimension_semantics=("arbitrary",), vmem_limit_bytes=48 << 20)


def cost(flops, moved):
    return pl.CostEstimate(flops=flops, bytes_accessed=moved, transcendentals=0)


def project(x, tokens, pieces):
    depth = tokens.shape[1]
    blocks, at_once = tokens.shape[0] // LANES, 2
    return pl.pallas_call(
        project_kernel,
        grid=(blocks // at_once,),
        in_specs=[SCALAR, pl.BlockSpec((at_once * LANES, depth), lambda i: (i, 0))]
        + [whole_spec(piece.shape) for piece in pieces],
        out_specs=[block_spec(at_once)] * 4,
        out_shape=[jax.ShapeDtypeStruct((blocks, LANES, LANES), BF)] * 4,
        scratch_shapes=[pltpu.VMEM((depth, 3 * LANES), BF)],
        compiler_params=PARAMS,
        cost_estimate=cost(2 * tokens.size * 3 * LANES, 2 * tokens.size),
    )(x, tokens, *pieces)


def back(off, taps, q, cot):
    n, at_once = q.shape[0], 2
    return pl.pallas_call(
        back_kernel,
        grid=(n // at_once,),
        in_specs=[pl.BlockSpec((at_once, 1, LANES), lambda i: (i, 0, 0)), whole_spec(taps.shape)]
        + [block_spec(at_once)] * 2,
        out_specs=[block_spec(at_once)] * 2,
        out_shape=[jax.ShapeDtypeStruct(q.shape, BF), jax.ShapeDtypeStruct(q.shape, F32)],
        scratch_shapes=[pltpu.VMEM((PER, LANES, LANES), BF)],
        compiler_params=PARAMS,
        cost_estimate=cost(2 * q.size * 2 * LANES * PER, 10 * q.size),
    )(off, taps, q, cot)


def front(off, taps, q, cot, product, halo):
    n, at_once = q.shape[0], 2
    return pl.pallas_call(
        front_kernel,
        grid=(n // at_once,),
        in_specs=[pl.BlockSpec((at_once, 1, LANES), lambda i: (i, 0, 0)), whole_spec(taps.shape)]
        + [block_spec(at_once)] * 4,
        out_specs=[block_spec(at_once)] * 2 + [whole_spec(taps.shape)],
        out_shape=[jax.ShapeDtypeStruct(q.shape, BF)] * 2 + [jax.ShapeDtypeStruct(taps.shape, F32)],
        scratch_shapes=[pltpu.VMEM((PER, LANES, LANES), BF), pltpu.VMEM((PER, LANES, LANES), F32)],
        compiler_params=PARAMS,
        cost_estimate=cost(4 * q.size * 2 * LANES * PER, 12 * q.size),
    )(off, taps, q, cot, product, halo)


def weight_grad(x, tokens, operands, dims):
    xs, hi, lo, feats = dims
    rows = 3 * feats // 2 + EXTRA
    return pl.pallas_call(
        weight_kernel,
        grid=(lo,),
        in_specs=[SCALAR, pl.BlockSpec((tokens.shape[0], xs * feats), lambda i: (0, i))]
        + [whole_spec(operand.shape) for operand in operands],
        out_specs=pl.BlockSpec((xs, hi, 1, rows, LANES), lambda i: (0, 0, i, 0, 0)),
        out_shape=jax.ShapeDtypeStruct((xs, hi, lo, rows, LANES), BF),
        scratch_shapes=[pltpu.VMEM((tokens.shape[0], 3 * LANES), BF)],
        compiler_params=PARAMS,
        cost_estimate=cost(2 * tokens.size * 3 * LANES, 2 * tokens.size),
    )(x, tokens, *operands)


def seq_pairs(by, turn):
    halves = lax.axis_size("z_hi")
    steps = lax.axis_size(("z_p", "x"))
    pairs = []
    for h in range(halves):
        for i in range(steps):
            to = i + by
            h_to = h if 0 <= to < steps else (h + turn) % halves
            pairs.append((h * steps + i, h_to * steps + to % steps))
    return pairs


def at_start():
    return lax.axis_index(("z_p", "x")) == 0


def at_last_x():
    return lax.axis_index("x") == lax.axis_size("x") - 1


def halo_forward(product):
    pairs = product.reshape(-1, 2, LANES, LANES)
    even, odd = pairs[:, 0], pairs[:, 1]
    far = jnp.where(at_last_x(), odd, even)
    near = jnp.where(at_last_x(), even, odd)
    most = lax.ppermute(far[:-1], SEQ_AX, seq_pairs(1, 0))
    last = lax.ppermute(far[-1:], SEQ_AX, seq_pairs(1, 1))
    near = turned(near, "x", 1)
    far = jnp.where(at_start(), jnp.concatenate([last, most], 0), jnp.concatenate([most, last], 0))
    return jnp.stack([far, near], 1).reshape(product.shape)


def halo_back(grad_prev):
    pairs = grad_prev.reshape(-1, 2, LANES, LANES)
    far, near = pairs[:, 0], pairs[:, 1]
    most = jnp.where(at_start(), far[1:], far[:-1])
    last = jnp.where(at_start(), far[:1], far[-1:])
    most = lax.ppermute(most, SEQ_AX, seq_pairs(-1, 0))
    last = lax.ppermute(last, SEQ_AX, seq_pairs(-1, -1))
    near = turned(near, "x", -1)
    far = jnp.concatenate([most, last], 0)
    even = jnp.where(at_last_x(), near, far)
    odd = jnp.where(at_last_x(), far, near)
    return jnp.stack([even, odd], 1).reshape(grad_prev.shape)


def split_rows(values):
    upper = values.astype(BF)
    lower = (values - upper.astype(F32)).astype(BF)
    return jnp.concatenate([upper, lower], -2)


def body(tokens, in_weight, filters, doc_offset, cotangent):
    hi, xs = lax.axis_size("z_hi"), lax.axis_size("x")
    lo = lax.axis_size(("z_p", "z_c"))
    blocks = lax.axis_size(TOK_AX)
    places = blocks // 2
    rows = tokens.shape[0]
    feats, width = in_weight.shape[1:]
    short = feats // 2
    row_count = 3 * short
    x = lax.axis_index("x").astype(jnp.int32)[None]
    member = lax.axis_index("z_c")

    gathered = lax.all_gather(tokens, TOK_AX, axis=0, tiled=True)
    packed = in_weight.reshape(3, 2, short, 2, HALF).transpose(3, 0, 2, 1, 4).reshape(2, row_count, LANES)
    packed = jnp.broadcast_to(packed[None, None], (hi, lo // 2, 2, row_count, LANES))
    by_z = swap_blocks(packed.reshape(hi * lo, row_count, LANES), Z_AX)
    pieces = [by_z] + [turned(by_z, "x", step) for step in range(1, xs)]
    pieces = [piece.reshape(hi, lo, 3, short, LANES) for piece in pieces]
    cot = cotangent.reshape(rows, hi, places, 2, HALF).transpose(2, 3, 0, 1, 4).reshape(blocks, rows, LANES)
    cot = swap_blocks(cot, TOK_AX)

    other = turned(filters, "z_hi", 1)
    upper = lax.axis_index("z_hi") == 0
    taps = jnp.where(upper, jnp.stack([filters, other]), jnp.stack([other, filters]))
    taps = lax.dynamic_slice_in_dim(taps, member * (PER // 2), PER // 2, 1).reshape(PER, LANES)
    taps_back = jnp.roll(jnp.flip(taps, 1), 1, axis=1)
    off = lax.dynamic_slice_in_dim(doc_offset, lax.axis_index("z_hi") * places, places, 0)
    off_other = turned(off, "z_c", 1)
    off = jnp.where(member == 0, jnp.stack([off, off_other], 1), jnp.stack([off_other, off], 1))
    off = off.reshape(blocks, 1, LANES)

    q, k, v, product = project(x, gathered, pieces)
    halo = halo_forward(product)
    grad_prev, grad_own = back(off, taps, q, cot)
    got = halo_back(grad_prev)
    gated, grad_q, grad_taps = front(off, taps_back, q, cot, product, halo)
    out = swap_blocks(gated, TOK_AX)
    out = out.reshape(places, 2, rows, hi, HALF).transpose(2, 3, 0, 1, 4).reshape(rows, -1)

    grad_taps = split_rows(grad_taps.reshape(hi, PER // 2, LANES))
    grad_taps = jnp.pad(grad_taps, ((0, 0), (0, EXTRA - PER), (0, 0)))
    partial = weight_grad(x, gathered, (grad_q, grad_own, got, k, v, grad_taps), (xs, hi, lo, feats))
    parts = [partial[0]] + [turned(partial[step], "x", step) for step in range(1, xs)]
    over_x = sum(part.astype(F32) for part in parts)
    taps_x = over_x[:, :, row_count : row_count + PER // 2] + over_x[:, :, row_count + PER // 2 : row_count + PER]
    taps_x = jnp.pad(split_rows(taps_x), ((0, 0), (0, 0), (0, EXTRA - PER), (0, 0)))
    over_x = jnp.concatenate([over_x[:, :, :row_count].astype(BF), taps_x], 2)
    over_z = swap_blocks(over_x.reshape(hi * lo, row_count + EXTRA, LANES), Z_AX)
    over_z = jnp.sum(over_z.reshape(hi * lo // 2, 2, row_count + EXTRA, LANES).astype(F32), 0)
    grad_weight = over_z[:, :row_count].reshape(2, 3, short, 2, HALF).transpose(1, 3, 2, 0, 4)
    grad_weight = grad_weight.reshape(3, feats, width)
    grad_taps = over_z[:, row_count : row_count + PER // 2] + over_z[:, row_count + PER // 2 : row_count + PER]
    grad_taps = jnp.roll(jnp.flip(grad_taps.reshape(PER, LANES), 1), 1, axis=1)
    return (out, grad_weight, grad_taps)


def sharded(mesh):
    return jax.shard_map(
        body,
        mesh=mesh,
        in_specs=(P(CTX + ZERO, None), P(None, ZERO, CTX), P(CTX, None), P(None, ZERO), P(CTX + ZERO, None)),
        out_specs=(P(CTX + ZERO, None), P(None, ZERO, CTX), P(CTX, None)),
        check_vma=False,
    )


def solution(mesh):
    return sharded(Mesh(mesh.devices.reshape(2, 4, 2, 4, 2, 4), CTX + ZERO))
```

time: 354 us -> 250 us (0.71)
  the two profiles are of different devices: /device:TPU:32 before, /device:TPU:38 now
where the time goes in v2:
time: 250 us; the launch traced here: 249 us
  waiting for transfers between devices  96.9 us (39%)
  starting transfers between devices  89.1 us (36%)
  Pallas kernels  31.6 us (13%)
  between operations  14.6 us (6%)
  local copies, waits for them, and re-layouts  13.3 us (5%)
  other arithmetic  3.09 us (1%)
    all_to_all x4, waiting for transfers between devices, swap_blocks(): return lax.all_to_all(pieces, axes, split_axis=0, concat_axis=0, tiled=True)  47.8 us
    all_to_all x4, starting transfers between devices, swap_blocks(): return lax.all_to_all(pieces, axes, split_axis=0, concat_axis=0, tiled=True)  40.6 us
    ppermute x10, starting transfers between devices, turned(): lax.ppermute(shard, axis, [(i, (i + by) % count) for i in range(count)])  34.4 us
    ppermute x10, waiting for transfers between devices, turned(): lax.ppermute(shard, axis, [(i, (i + by) % count) for i in range(count)])  32.3 us
    ppermute x1, waiting for transfers between devices, halo_back(): most = lax.ppermute(most, SEQ_AX, seq_pairs(-1, 0))  12.8 us
    pallas_call x1, Pallas kernels, weight_grad(): pl.pallas_call(weight_kernel, grid=(lo,), in_specs=[SCALAR, pl.BlockSpec(...  9.67 us
    pallas_call x1, Pallas kernels, project(): pl.pallas_call(project_kernel, grid=(blocks // at_once,), in_specs=[SCALA...  9.41 us
    pallas_call x1, Pallas kernels, front(): pl.pallas_call(front_kernel, grid=(n // at_once,), in_specs=[pl.BlockSpec...  8.75 us
  transfers between devices with their start and end apart: 19, of which 8 were waited for; matrix products, arithmetic and copies ran while one was open for 3% of the time, Pallas kernels for 11%

profile of v2, /device:TPU:38, one launch (start us, length us, event | category | flops | bytes accessed | tf_op | source)
XLA Modules:
  0.0 248.7 jit_solution(3064208969157566001)
XLA Ops:
  7.2 0.7 all-gather.2.cloned.1.call-update
  7.9 0.9 reshape.182
  9.0 0.8 broadcast_in_dim.12
  9.8 15.2 %all-to-all-start = ((bf16[16,96,128]{2,1,0:T(8,128)(2,1)}), bf16[16,96,128]{2,1,0:T(8,128)(2,1)S(1)}, u32[]{:S(2)}, u32[]{:S(2)}) async-start(bf16[16,96,128]{2,1,0:T(8,128)(2,1)} %bitcast.8), calls=%async_computation | async-start | bytes 786432 | tf_op jit(solution)/shard_map/all_to_all | solution.py:23
  25.4 1.1 copy.21
  26.5 23.8 %all-to-all-done = bf16[16,96,128]{2,1,0:T(8,128)(2,1)S(1)} async-done(((bf16[16,96,128]{2,1,0:T(8,128)(2,1)}), bf16[16,96,128]{2,1,0:T(8,128)(2,1)S(1)}, u32[]{:S(2)}, u32[]{:S(2)}) %all-to-all-start) | async-done | bytes 393248 | tf_op jit(solution)/shard_map/all_to_all | solution.py:23
  50.3 5.9 %all-to-all-start.1 = ((bf16[16,128,128]{2,1,0:T(8,128)(2,1)}), bf16[16,128,128]{2,1,0:T(8,128)(2,1)S(1)}, u32[]{:S(2)}, u32[]{:S(2)}) async-start(bf16[16,128,128]{2,1,0:T(8,128)(2,1)} %copy.21), calls=%async_computation.1 | async-start | bytes 1048576 | tf_op jit(solution)/shard_map/all_to_all | solution.py:23
  56.2 2.0 collective-permute-start
  58.2 5.2 %collective-permute-start.1 = (f32[8,128]{1,0:T(8,128)S(1)}, f32[8,128]{1,0:T(8,128)S(1)}, u32[]{:S(2)}, u32[]{:S(2)}) collective-permute-start(f32[8,128]{1,0:T(8,128)S(1)} %copy-done.12), channel_id=1, source_target_pairs={{0,256},{256,0},{1,257},{257,1},{2,258},{258,2},{3,259},{259,3},{4... | collective-permute-start | bytes 12296 | tf_op jit(solution)/shard_map/ppermute | solution.py:28
  63.4 2.7 %collective-permute-start.4 = (bf16[16,96,128]{2,1,0:T(8,128)(2,1)S(1)}, bf16[16,96,128]{2,1,0:T(8,128)(2,1)S(1)}, u32[]{:S(2)}, u32[]{:S(2)}) collective-permute-start(bf16[16,96,128]{2,1,0:T(8,128)(2,1)S(1)} %all-to-all-done), channel_id=1, source_target_pairs={{0,3},{1,0},{2,1},{3,2},{4,7},{5,4},{6,5},{7,6},{8,11},{9,8},{10,9... | collective-permute-start | bytes 1179656 | tf_op jit(solution)/shard_map/ppermute | solution.py:28
  66.1 3.0 %collective-permute-start.3 = (bf16[16,96,128]{2,1,0:T(8,128)(2,1)S(1)}, bf16[16,96,128]{2,1,0:T(8,128)(2,1)S(1)}, u32[]{:S(2)}, u32[]{:S(2)}) collective-permute-start(bf16[16,96,128]{2,1,0:T(8,128)(2,1)S(1)} %all-to-all-done), channel_id=1, source_target_pairs={{0,2},{1,3},{2,0},{3,1},{4,6},{5,7},{6,4},{7,5},{8,10},{9,11},{10,... | collective-permute-start | bytes 1179656 | tf_op jit(solution)/shard_map/ppermute | solution.py:28
  69.1 4.0 %collective-permute-start.2 = (bf16[16,96,128]{2,1,0:T(8,128)(2,1)S(1)}, bf16[16,96,128]{2,1,0:T(8,128)(2,1)S(1)}, u32[]{:S(2)}, u32[]{:S(2)}) collective-permute-start(bf16[16,96,128]{2,1,0:T(8,128)(2,1)S(1)} %all-to-all-done), channel_id=1, source_target_pairs={{0,1},{1,2},{2,3},{3,0},{4,5},{5,6},{6,7},{7,4},{8,9},{9,10},{10,1... | collective-permute-start | bytes 1179656 | tf_op jit(solution)/shard_map/ppermute | solution.py:28
  73.5 12.3 %collective-permute-done.4 = bf16[16,96,128]{2,1,0:T(8,128)(2,1)S(1)} collective-permute-done((bf16[16,96,128]{2,1,0:T(8,128)(2,1)S(1)}, bf16[16,96,128]{2,1,0:T(8,128)(2,1)S(1)}, u32[]{:S(2)}, u32[]{:S(2)}) %collective-permute-start.4) | collective-permute-done | bytes 393248 | tf_op jit(solution)/shard_map/ppermute | solution.py:28
  85.8 0.7 copy-done.4
  86.5 1.8 collective-permute-done.2
  88.3 0.7 copy-done.6
  89.1 3.4 %all-gather.2.cloned.1.call-done.tok_ref = bf16[2048,2048]{1,0:T(8,128)(2,1)} async-done(((bf16[128,2048]{1,0:T(8,128)(2,1)}), bf16[2048,2048]{1,0:T(8,128)(2,1)}) %all-gather.2.cloned.1.call-update) | async-done | bytes 8388624 | tf_op jit(solution)/shard_map/all_gather | solution.py:311
  92.5 1.0 copy-done.5
  93.5 1.0 copy-done.7
  94.4 9.4 %shard_map.76 = (bf16[16,128,128]{2,1,0:T(8,128)(2,1)S(1)}, bf16[16,128,128]{2,1,0:T(8,128)(2,1)S(1)}, bf16[16,128,128]{2,1,0:T(8,128)(2,1)S(1)}, bf16[16,128,128]{2,1,0:T(8,128)(2,1)S(1)}) custom-call(s32[1]{0:T(128)} %bitcast.6.x_ref, bf16[2048,2048]{1,0:T(8,128)(2,1)} %all-gather.2.cloned.1.call-done.tok_ref, bf16[2,8,3,32,128]{4,3,2,1,0:T(8,128)(2,1)S(1)} %bitcast.91, ...), custom_call_target="tpu_custom_call" | custom-call | flops 3221225472 | bytes 8388608 | tf_op jit(solution)/shard_map/pallas_call | solution.py:188
  103.9 0.8 copy-done.8
  104.7 1.2 copy-done.9
  105.9 3.8 %shard_map.78 = (bf16[16,128,128]{2,1,0:T(8,128)(2,1)S(1)}, f32[16,128,128]{2,1,0:T(8,128)S(1)}) custom-call(s32[16,1,128]{2,1,0:T(1,128)S(1)} %bitcast.95, f32[8,128]{1,0:T(8,128)S(1)} %bitcast.94, bf16[16,128,128]{2,1,0:T(8,128)(2,1)S(1)} %copy-done.9, bf16[16,128,128]{2,1,0:T(8,128)(2,1)S(1)} %all-to-all-done.1.cot_ref), custom_call_target="tpu_custom_call" | custom-call | flops 1073741824 | bytes 2621440 | tf_op jit(solution)/shard_map/pallas_call | solution.py:203
  109.9 4.4 %collective-permute-start.5 = (bf16[1,128,128]{2,1,0:T(8,128)(2,1)S(1)}, bf16[1,128,128]{2,1,0:T(8,128)(2,1)S(1)}, u32[]{:S(2)}, u32[]{:S(2)}) collective-permute-start(bf16[1,128,128]{2,1,0:T(8,128)(2,1)S(1)} %slice_bitcast_fusion.8), channel_id=1, source_target_pairs={{0,1},{1,2},{2,3},{3,8},{8,9},{9,10},{10,11},{11,16},{16,17},{17,1... | collective-permute-start | bytes 98312 | tf_op jit(solution)/shard_map/ppermute | solution.py:273
  114.2 3.4 %collective-permute-start.6 = (bf16[7,128,128]{2,1,0:T(8,128)(2,1)S(1)}, bf16[7,128,128]{2,1,0:T(8,128)(2,1)S(1)}, u32[]{:S(2)}, u32[]{:S(2)}) collective-permute-start(bf16[7,128,128]{2,1,0:T(8,128)(2,1)S(1)} %slice_bitcast_fusion.7), channel_id=1, source_target_pairs={{0,1},{1,2},{2,3},{3,8},{8,9},{9,10},{10,11},{11,16},{16,17},{17,1... | collective-permute-start | bytes 688136 | tf_op jit(solution)/shard_map/ppermute | solution.py:272
  117.6 1.9 collective-permute-start.7
  119.6 3.9 %collective-permute-start.10 = (bf16[1,128,128]{2,1,0:T(8,128)(2,1)S(1)}, bf16[1,128,128]{2,1,0:T(8,128)(2,1)S(1)}, u32[]{:S(2)}, u32[]{:S(2)}) collective-permute-start(bf16[1,128,128]{2,1,0:T(8,128)(2,1)S(1)} %fusion.7), channel_id=1, source_target_pairs={{0,283},{1,0},{2,1},{3,2},{8,3},{9,8},{10,9},{11,10},{16,11},{17,1... | collective-permute-start | bytes 98312 | tf_op jit(solution)/shard_map/ppermute | solution.py:285
  123.5 2.4 collective-permute-start.9
  126.0 0.7 slice_bitcast_fusion.4
  126.7 12.8 %collective-permute-done.9 = bf16[7,128,128]{2,1,0:T(8,128)(2,1)S(1)} collective-permute-done((bf16[7,128,128]{2,1,0:T(8,128)(2,1)S(1)}, bf16[7,128,128]{2,1,0:T(8,128)(2,1)S(1)}, u32[]{:S(2)}, u32[]{:S(2)}) %collective-permute-start.9) | collective-permute-done | bytes 229408 | tf_op jit(solution)/shard_map/ppermute | solution.py:284
  139.5 1.9 collective-permute-start.8
  141.6 8.7 %shard_map.77 = (bf16[16,128,128]{2,1,0:T(8,128)(2,1)S(1)}, bf16[16,128,128]{2,1,0:T(8,128)(2,1)S(1)}, f32[8,128]{1,0:T(8,128)S(1)}) custom-call(s32[16,1,128]{2,1,0:T(1,128)S(1)} %bitcast.96, f32[8,128]{1,0:T(8,128)S(1)} %pad_maximum_fusion.3.taps_ref, bf16[16,128,128]{2,1,0:T(8,128)(2,1)S(1)} %copy-done.10, ...), custom_call_target="tpu_custom_call" | custom-call | flops 2147483648 | bytes 3145728 | tf_op jit(solution)/shard_map/pallas_call | solution.py:218
  150.4 0.8 copy-done.1
  151.2 5.8 %all-to-all-start.2 = ((bf16[16,128,128]{2,1,0:T(8,128)(2,1)}), bf16[16,128,128]{2,1,0:T(8,128)(2,1)S(1)}, u32[]{:S(2)}, u32[]{:S(2)}) async-start(bf16[16,128,128]{2,1,0:T(8,128)(2,1)} %copy-done.1), calls=%async_computation.2 | async-start | bytes 1048576 | tf_op jit(solution)/shard_map/all_to_all | solution.py:23
  157.0 1.0 select_bitcast_fusion.1
  158.1 9.7 %shard_map.79 = bf16[4,2,8,112,128]{4,3,2,1,0:T(8,128)(2,1)S(1)} custom-call(s32[1]{0:T(128)} %bitcast.6.x_ref, bf16[2048,2048]{1,0:T(8,128)(2,1)} %all-gather.2.cloned.1.call-done.tok_ref, bf16[16,128,128]{2,1,0:T(8,128)(2,1)S(1)} %get-tuple-element.15.gq_ref, f32[16,128,128]{2,1,0:T(8,128)S(1)} %get-tuple-element.16.own_ref, ...), custom_call_target="tpu_custom_call" | custom-call | flops 3221225472 | bytes 8388608 | tf_op jit(solution)/shard_map/pallas_call | solution.py:234
  167.9 6.3 %collective-permute-start.11 = (bf16[2,8,112,128]{3,2,1,0:T(8,128)(2,1)S(1)}, bf16[2,8,112,128]{3,2,1,0:T(8,128)(2,1)S(1)}, u32[]{:S(2)}, u32[]{:S(2)}) collective-permute-start(bf16[2,8,112,128]{3,2,1,0:T(8,128)(2,1)S(1)} %get-tuple-element.28), channel_id=1, source_target_pairs={{0,1},{1,2},{2,3},{3,0},{4,5},{5,6},{6,7},{7,4},{8,9},{9,10},{10,1... | collective-permute-start | bytes 1376264 | tf_op jit(solution)/shard_map/ppermute | solution.py:28
  174.2 1.9 collective-permute-start.13
  176.1 5.4 %collective-permute-start.12 = (bf16[2,8,112,128]{3,2,1,0:T(8,128)(2,1)S(1)}, bf16[2,8,112,128]{3,2,1,0:T(8,128)(2,1)S(1)}, u32[]{:S(2)}, u32[]{:S(2)}) collective-permute-start(bf16[2,8,112,128]{3,2,1,0:T(8,128)(2,1)S(1)} %get-tuple-element.30), channel_id=1, source_target_pairs={{0,2},{1,3},{2,0},{3,1},{4,6},{5,7},{6,4},{7,5},{8,10},{9,11},{10,... | collective-permute-start | bytes 1376264 | tf_op jit(solution)/shard_map/ppermute | solution.py:28
  181.5 12.6 %collective-permute-done.11 = bf16[2,8,112,128]{3,2,1,0:T(8,128)(2,1)S(1)} collective-permute-done((bf16[2,8,112,128]{3,2,1,0:T(8,128)(2,1)S(1)}, bf16[2,8,112,128]{3,2,1,0:T(8,128)(2,1)S(1)}, u32[]{:S(2)}, u32[]{:S(2)}) %collective-permute-start.11) | collective-permute-done | bytes 458784 | tf_op jit(solution)/shard_map/ppermute | solution.py:28
  194.1 5.6 %collective-permute-done.12 = bf16[2,8,112,128]{3,2,1,0:T(8,128)(2,1)S(1)} collective-permute-done((bf16[2,8,112,128]{3,2,1,0:T(8,128)(2,1)S(1)}, bf16[2,8,112,128]{3,2,1,0:T(8,128)(2,1)S(1)}, u32[]{:S(2)}, u32[]{:S(2)}) %collective-permute-start.12) | collective-permute-done | bytes 458784 | tf_op jit(solution)/shard_map/ppermute | solution.py:28
  200.0 0.8 pad_maximum_fusion.2
  200.8 13.7 %all-to-all-start.3 = ((bf16[16,112,128]{2,1,0:T(8,128)(2,1)}), bf16[16,112,128]{2,1,0:T(8,128)(2,1)S(1)}, u32[]{:S(2)}, u32[]{:S(2)}) async-start(bf16[16,112,128]{2,1,0:T(8,128)(2,1)} %bitcast.42), calls=%async_computation.3 | async-start | bytes 917504 | tf_op jit(solution)/shard_map/all_to_all | solution.py:23
  214.5 0.3 copy.26
  214.8 1.0 copy.30
  215.9 24.0 %all-to-all-done.3 = bf16[16,112,128]{2,1,0:T(8,128)(2,1)S(1)} async-done(((bf16[16,112,128]{2,1,0:T(8,128)(2,1)}), bf16[16,112,128]{2,1,0:T(8,128)(2,1)S(1)}, u32[]{:S(2)}, u32[]{:S(2)}) %all-to-all-start.3) | async-done | bytes 458784 | tf_op jit(solution)/shard_map/all_to_all | solution.py:23
  240.4 0.8 reshape.199
  241.2 0.7 pad_maximum_fusion.4
  (68 shorter events, 2.1 us)
Async XLA Ops:
  7.2 49.0 %copy-start = (s32[16,128]{1,0:T(8,128)S(1)}, s32[16,128]{1,0:T(8,128)}, u32[]{:S(2)}) copy-start(s32[16,128]{1,0:T(8,128)} %param.8) | copy-start | bytes 24580
  7.2 17.9 %copy-start.11 = (bf16[128,2048]{1,0:T(8,128)(2,1)S(1)}, bf16[128,2048]{1,0:T(8,128)(2,1)}, u32[]{:S(2)}) copy-start(bf16[128,2048]{1,0:T(8,128)(2,1)} %param.9) | copy-start | bytes 1572868
  7.2 85.3 %all-gather.2.cloned.1.call-start = ((), (), s32[]{:S(2)}) async-start(), calls=%async_computation.4 | async-start | bytes 8912896 | tf_op jit(solution)/shard_map/all_gather | solution.py:311
  9.8 40.4 %all-to-all-start = ((bf16[16,96,128]{2,1,0:T(8,128)(2,1)}), bf16[16,96,128]{2,1,0:T(8,128)(2,1)S(1)}, u32[]{:S(2)}, u32[]{:S(2)}) async-start(bf16[16,96,128]{2,1,0:T(8,128)(2,1)} %bitcast.8), calls=%async_computation | async-start | bytes 786432 | tf_op jit(solution)/shard_map/all_to_all | solution.py:23
  25.3 32.9 %copy-start.12 = (f32[8,128]{1,0:T(8,128)S(1)}, f32[8,128]{1,0:T(8,128)}, u32[]{:S(2)}) copy-start(f32[8,128]{1,0:T(8,128)} %param.7) | copy-start | bytes 12292
  50.3 54.4 %all-to-all-start.1 = ((bf16[16,128,128]{2,1,0:T(8,128)(2,1)}), bf16[16,128,128]{2,1,0:T(8,128)(2,1)S(1)}, u32[]{:S(2)}, u32[]{:S(2)}) async-start(bf16[16,128,128]{2,1,0:T(8,128)(2,1)} %copy.21), calls=%async_computation.1 | async-start | bytes 1048576 | tf_op jit(solution)/shard_map/all_to_all | solution.py:23
  56.2 17.0 %collective-permute-start = (s32[8,128]{1,0:T(8,128)S(1)}, s32[8,128]{1,0:T(8,128)S(1)}, u32[]{:S(2)}, u32[]{:S(2)}) collective-permute-start(s32[8,128]{1,0:T(8,128)S(1)} %constant_dynamic-slice_fusion), channel_id=1, source_target_pairs={{0,4},{4,0},{1,5},{5,1},{2,6},{6,2},{3,7},{7,3},{8,12},{12,8},{9,1... | collective-permute-start | bytes 12296 | tf_op jit(solution)/shard_map/ppermute | solution.py:28
  58.2 15.0 %collective-permute-start.1 = (f32[8,128]{1,0:T(8,128)S(1)}, f32[8,128]{1,0:T(8,128)S(1)}, u32[]{:S(2)}, u32[]{:S(2)}) collective-permute-start(f32[8,128]{1,0:T(8,128)S(1)} %copy-done.12), channel_id=1, source_target_pairs={{0,256},{256,0},{1,257},{257,1},{2,258},{258,2},{3,259},{259,3},{4... | collective-permute-start | bytes 12296 | tf_op jit(solution)/shard_map/ppermute | solution.py:28
  63.4 22.4 %collective-permute-start.4 = (bf16[16,96,128]{2,1,0:T(8,128)(2,1)S(1)}, bf16[16,96,128]{2,1,0:T(8,128)(2,1)S(1)}, u32[]{:S(2)}, u32[]{:S(2)}) collective-permute-start(bf16[16,96,128]{2,1,0:T(8,128)(2,1)S(1)} %all-to-all-done), channel_id=1, source_target_pairs={{0,3},{1,0},{2,1},{3,2},{4,7},{5,4},{6,5},{7,6},{8,11},{9,8},{10,9... | collective-permute-start | bytes 1179656 | tf_op jit(solution)/shard_map/ppermute | solution.py:28
  66.1 19.7 %collective-permute-start.3 = (bf16[16,96,128]{2,1,0:T(8,128)(2,1)S(1)}, bf16[16,96,128]{2,1,0:T(8,128)(2,1)S(1)}, u32[]{:S(2)}, u32[]{:S(2)}) collective-permute-start(bf16[16,96,128]{2,1,0:T(8,128)(2,1)S(1)} %all-to-all-done), channel_id=1, source_target_pairs={{0,2},{1,3},{2,0},{3,1},{4,6},{5,7},{6,4},{7,5},{8,10},{9,11},{10,... | collective-permute-start | bytes 1179656 | tf_op jit(solution)/shard_map/ppermute | solution.py:28
  69.1 19.2 %collective-permute-start.2 = (bf16[16,96,128]{2,1,0:T(8,128)(2,1)S(1)}, bf16[16,96,128]{2,1,0:T(8,128)(2,1)S(1)}, u32[]{:S(2)}, u32[]{:S(2)}) collective-permute-start(bf16[16,96,128]{2,1,0:T(8,128)(2,1)S(1)} %all-to-all-done), channel_id=1, source_target_pairs={{0,1},{1,2},{2,3},{3,0},{4,5},{5,6},{6,7},{7,4},{8,9},{9,10},{10,1... | collective-permute-start | bytes 1179656 | tf_op jit(solution)/shard_map/ppermute | solution.py:28
  85.8 0.7 copy-start.4
  88.3 0.7 copy-start.6
  92.5 1.0 copy-start.5
  93.5 1.0 copy-start.7
  103.9 0.8 copy-start.8
  104.7 5.1 %copy-start.2 = (bf16[16,128,128]{2,1,0:T(8,128)(2,1)}, bf16[16,128,128]{2,1,0:T(8,128)(2,1)S(1)}, u32[]{:S(2)}) copy-start(bf16[16,128,128]{2,1,0:T(8,128)(2,1)S(1)} %get-tuple-element.13.prod_ref) | copy-start | bytes 1572868
  104.7 1.2 copy-start.9
  109.8 31.8 %copy-start.3 = (bf16[16,128,128]{2,1,0:T(8,128)(2,1)S(1)}, bf16[16,128,128]{2,1,0:T(8,128)(2,1)}, u32[]{:S(2)}) copy-start(bf16[16,128,128]{2,1,0:T(8,128)(2,1)} %copy-done.2) | copy-start | bytes 1572868
  109.8 31.8 %copy-start.10 = (bf16[16,128,128]{2,1,0:T(8,128)(2,1)S(1)}, bf16[16,128,128]{2,1,0:T(8,128)(2,1)}, u32[]{:S(2)}) copy-start(bf16[16,128,128]{2,1,0:T(8,128)(2,1)} %copy-done.8) | copy-start | bytes 1572868
  109.9 31.6 %collective-permute-start.5 = (bf16[1,128,128]{2,1,0:T(8,128)(2,1)S(1)}, bf16[1,128,128]{2,1,0:T(8,128)(2,1)S(1)}, u32[]{:S(2)}, u32[]{:S(2)}) collective-permute-start(bf16[1,128,128]{2,1,0:T(8,128)(2,1)S(1)} %slice_bitcast_fusion.8), channel_id=1, source_target_pairs={{0,1},{1,2},{2,3},{3,8},{8,9},{9,10},{10,11},{11,16},{16,17},{17,1... | collective-permute-start | bytes 98312 | tf_op jit(solution)/shard_map/ppermute | solution.py:273
  114.2 27.2 %collective-permute-start.6 = (bf16[7,128,128]{2,1,0:T(8,128)(2,1)S(1)}, bf16[7,128,128]{2,1,0:T(8,128)(2,1)S(1)}, u32[]{:S(2)}, u32[]{:S(2)}) collective-permute-start(bf16[7,128,128]{2,1,0:T(8,128)(2,1)S(1)} %slice_bitcast_fusion.7), channel_id=1, source_target_pairs={{0,1},{1,2},{2,3},{3,8},{8,9},{9,10},{10,11},{11,16},{16,17},{17,1... | collective-permute-start | bytes 688136 | tf_op jit(solution)/shard_map/ppermute | solution.py:272
  117.6 23.9 %collective-permute-start.7 = (bf16[8,128,128]{2,1,0:T(8,128)(2,1)S(1)}, bf16[8,128,128]{2,1,0:T(8,128)(2,1)S(1)}, u32[]{:S(2)}, u32[]{:S(2)}) collective-permute-start(bf16[8,128,128]{2,1,0:T(8,128)(2,1)S(1)} %get-tuple-element.34), channel_id=1, source_target_pairs={{0,1},{1,2},{2,3},{3,0},{4,5},{5,6},{6,7},{7,4},{8,9},{9,10},{10,1... | collective-permute-start | bytes 786440 | tf_op jit(solution)/shard_map/ppermute | solution.py:28
  119.6 21.8 %collective-permute-start.10 = (bf16[1,128,128]{2,1,0:T(8,128)(2,1)S(1)}, bf16[1,128,128]{2,1,0:T(8,128)(2,1)S(1)}, u32[]{:S(2)}, u32[]{:S(2)}) collective-permute-start(bf16[1,128,128]{2,1,0:T(8,128)(2,1)S(1)} %fusion.7), channel_id=1, source_target_pairs={{0,283},{1,0},{2,1},{3,2},{8,3},{9,8},{10,9},{11,10},{16,11},{17,1... | collective-permute-start | bytes 98312 | tf_op jit(solution)/shard_map/ppermute | solution.py:285
  123.5 16.0 %collective-permute-start.9 = (bf16[7,128,128]{2,1,0:T(8,128)(2,1)S(1)}, bf16[7,128,128]{2,1,0:T(8,128)(2,1)S(1)}, u32[]{:S(2)}, u32[]{:S(2)}) collective-permute-start(bf16[7,128,128]{2,1,0:T(8,128)(2,1)S(1)} %fusion.3), channel_id=1, source_target_pairs={{0,27},{1,0},{2,1},{3,2},{8,3},{9,8},{10,9},{11,10},{16,11},{17,16... | collective-permute-start | bytes 688136 | tf_op jit(solution)/shard_map/ppermute | solution.py:284
  139.5 17.5 %collective-permute-start.8 = (bf16[8,128,128]{2,1,0:T(8,128)(2,1)}, bf16[8,128,128]{2,1,0:T(8,128)(2,1)}, u32[]{:S(2)}, u32[]{:S(2)}) collective-permute-start(bf16[8,128,128]{2,1,0:T(8,128)(2,1)} %slice_bitcast_fusion.4), channel_id=1, source_target_pairs={{0,3},{1,0},{2,1},{3,2},{4,7},{5,4},{6,5},{7,6},{8,11},{9,8},{10,9... | collective-permute-start | bytes 786440 | tf_op jit(solution)/shard_map/ppermute | solution.py:28
  150.4 0.8 copy-start.1
  151.2 49.7 %all-to-all-start.2 = ((bf16[16,128,128]{2,1,0:T(8,128)(2,1)}), bf16[16,128,128]{2,1,0:T(8,128)(2,1)S(1)}, u32[]{:S(2)}, u32[]{:S(2)}) async-start(bf16[16,128,128]{2,1,0:T(8,128)(2,1)} %copy-done.1), calls=%async_computation.2 | async-start | bytes 1048576 | tf_op jit(solution)/shard_map/all_to_all | solution.py:23
  167.9 26.2 %collective-permute-start.11 = (bf16[2,8,112,128]{3,2,1,0:T(8,128)(2,1)S(1)}, bf16[2,8,112,128]{3,2,1,0:T(8,128)(2,1)S(1)}, u32[]{:S(2)}, u32[]{:S(2)}) collective-permute-start(bf16[2,8,112,128]{3,2,1,0:T(8,128)(2,1)S(1)} %get-tuple-element.28), channel_id=1, source_target_pairs={{0,1},{1,2},{2,3},{3,0},{4,5},{5,6},{6,7},{7,4},{8,9},{9,10},{10,1... | collective-permute-start | bytes 1376264 | tf_op jit(solution)/shard_map/ppermute | solution.py:28
  174.2 19.9 %collective-permute-start.13 = (bf16[2,8,112,128]{3,2,1,0:T(8,128)(2,1)S(1)}, bf16[2,8,112,128]{3,2,1,0:T(8,128)(2,1)S(1)}, u32[]{:S(2)}, u32[]{:S(2)}) collective-permute-start(bf16[2,8,112,128]{3,2,1,0:T(8,128)(2,1)S(1)} %get-tuple-element.29), channel_id=1, source_target_pairs={{0,3},{1,0},{2,1},{3,2},{4,7},{5,4},{6,5},{7,6},{8,11},{9,8},{10,9... | collective-permute-start | bytes 1376264 | tf_op jit(solution)/shard_map/ppermute | solution.py:28
  176.1 23.5 %collective-permute-start.12 = (bf16[2,8,112,128]{3,2,1,0:T(8,128)(2,1)S(1)}, bf16[2,8,112,128]{3,2,1,0:T(8,128)(2,1)S(1)}, u32[]{:S(2)}, u32[]{:S(2)}) collective-permute-start(bf16[2,8,112,128]{3,2,1,0:T(8,128)(2,1)S(1)} %get-tuple-element.30), channel_id=1, source_target_pairs={{0,2},{1,3},{2,0},{3,1},{4,6},{5,7},{6,4},{7,5},{8,10},{9,11},{10,... | collective-permute-start | bytes 1376264 | tf_op jit(solution)/shard_map/ppermute | solution.py:28
  200.8 39.0 %all-to-all-start.3 = ((bf16[16,112,128]{2,1,0:T(8,128)(2,1)}), bf16[16,112,128]{2,1,0:T(8,128)(2,1)S(1)}, u32[]{:S(2)}, u32[]{:S(2)}) async-start(bf16[16,112,128]{2,1,0:T(8,128)(2,1)} %bitcast.42), calls=%async_computation.3 | async-start | bytes 917504 | tf_op jit(solution)/shard_map/all_to_all | solution.py:23
Sparse Core Ops, SparseCore 0:
  10.1 82.2 all-gather.1

commit v3 on v2

--- a/solution.py
+++ b/solution.py
@@ -53,44 +53,40 @@
         table_ref[g] = pltpu.roll(rows, 0, 1, stride=1, stride_axis=0).astype(BF)
 
 
-def project_kernel(x_ref, tok_ref, *refs):
-    w_refs, (q_ref, k_ref, v_ref, prod_ref, table) = refs[:-5], refs[-5:]
-    hi, lo, parts, short, _ = w_refs[0].shape
+def unpack_kernel(x_ref, *refs):
+    w_refs, table = refs[:-1], refs[-1]
+    _, lo, parts, short, _ = w_refs[0].shape
     xs = len(w_refs)
-
-    @pl.when(pl.program_id(0) == 0)
-    def _():
-        for step, w_ref in enumerate(w_refs):
-            x = lax.rem(x_ref[0] - step + xs, xs)
-            for l in range(lo):
-                at = pl.multiple_of((l * xs + x) * (2 * short), 2 * short)
-                for p in range(parts):
-                    cols = slice(p * LANES, (p + 1) * LANES)
-                    top, low = lane_halves(w_ref[0, l, p].astype(F32), w_ref[1, l, p].astype(F32))
-                    table[pl.ds(at, short), cols] = top.astype(BF)
-                    table[pl.ds(at + short, short), cols] = low.astype(BF)
-
-    result = jnp.dot(tok_ref[...], table[...], preferred_element_type=F32).astype(BF)
-    count, rows = q_ref.shape[:2]
-    q, k, v = [result[:, p * LANES : (p + 1) * LANES] for p in range(parts)]
-    product = (k.astype(F32) * v.astype(F32)).astype(BF)
-    for ref, side in ((q_ref, q), (k_ref, k), (v_ref, v), (prod_ref, product)):
-        for j in range(count):
-            ref[j] = side[j * rows : (j + 1) * rows]
-
-
-def back_kernel(off_ref, taps_ref, q_ref, cot_ref, prev_ref, own_ref, table):
+    for step, w_ref in enumerate(w_refs):
+        x = lax.rem(x_ref[0] - step + xs, xs)
+        for l in range(lo):
+            at = pl.multiple_of((l * xs + x) * (2 * short), 2 * short)
+            for p in range(parts):
+                cols = slice(p * LANES, (p + 1) * LANES)
+                top, low = lane_halves(w_ref[0, l, p].astype(F32), w_ref[1, l, p].astype(F32))
+                table[pl.ds(at, short), cols] = top.astype(BF)
+                table[pl.ds(at + short, short), cols] = low.astype(BF)
+
+
+def project_kernel(off_ref, taps_ref, tok_ref, w_ref, cot_ref, q_ref, k_ref, v_ref, prod_ref, prev_ref, own_ref, table):
     @pl.when(pl.program_id(0) == 0)
     def _():
         circulants(taps_ref, table)
 
+    count, rows = q_ref.shape[:2]
+    result = jnp.dot(tok_ref[...], w_ref[...], preferred_element_type=F32).astype(BF)
     u, t = iotas()
     lag = t - u
-    for j in range(q_ref.shape[0]):
+    for j in range(count):
+        q, k, v = [result[j * rows : (j + 1) * rows, p * LANES : (p + 1) * LANES] for p in range(3)]
+        q_ref[j] = q
+        k_ref[j] = k
+        v_ref[j] = v
+        prod_ref[j] = (k.astype(F32) * v.astype(F32)).astype(BF)
         off = jnp.broadcast_to(off_ref[j], (LANES, LANES))
         m_own = jnp.where((lag >= 0) & (lag <= off), 1.0, 0.0).astype(BF)
         m_prev = jnp.where((lag < 0) & (lag + LANES <= off), 1.0, 0.0).astype(BF)
-        grad = (cot_ref[j].astype(F32) * q_ref[j].astype(F32)).astype(BF)
+        grad = (cot_ref[j].astype(F32) * q.astype(F32)).astype(BF)
         right = jnp.concatenate([group_lanes(grad, g) for g in range(PER)], 0)
         prev = jnp.concatenate([table[g] * m_prev for g in range(PER)], 1)
         own = jnp.concatenate([table[g] * m_own for g in range(PER)], 1)
@@ -156,14 +152,16 @@
             grads[at, 2 * LANES :] = (grad * k_ref[j].astype(F32)).astype(BF)
 
     result = lax.dot_general(tok_ref[...], grads[...], (((0,), (0,)), ((), ())), preferred_element_type=F32)
-    for x in range(xs):
-        slot = lax.rem(x - x_ref[0] + xs, xs)
-        for p in range(3):
-            block = result[x * 2 * short : (x + 1) * 2 * short, p * LANES : (p + 1) * LANES]
-            for h, piece in enumerate(lane_halves(block[:short], block[short:])):
-                out_ref[slot, h, 0, p * short : (p + 1) * short] = piece.astype(BF)
-        for h in range(hi):
-            out_ref[slot, h, 0, 3 * short :] = taps_ref[h]
+    for l in range(out_ref.shape[2]):
+        for x in range(xs):
+            slot = lax.rem(x - x_ref[0] + xs, xs)
+            at = (l * xs + x) * 2 * short
+            for p in range(3):
+                block = result[at : at + 2 * short, p * LANES : (p + 1) * LANES]
+                for h, piece in enumerate(lane_halves(block[:short], block[short:])):
+                    out_ref[slot, h, l, p * short : (p + 1) * short] = piece.astype(BF)
+            for h in range(hi):
+                out_ref[slot, h, l, 3 * short :] = taps_ref[h]
 
 
 def block_spec(count):
@@ -182,35 +180,38 @@
     return pl.CostEstimate(flops=flops, bytes_accessed=moved, transcendentals=0)
 
 
-def project(x, tokens, pieces):
+def unpack(x, pieces):
+    hi, lo, parts, short, _ = pieces[0].shape
+    return pl.pallas_call(
+        unpack_kernel,
+        in_specs=[SCALAR] + [pl.BlockSpec(memory_space=pltpu.VMEM)] * len(pieces),
+        out_specs=pl.BlockSpec(memory_space=pltpu.VMEM),
+        out_shape=jax.ShapeDtypeStruct((lo * len(pieces) * 2 * short, parts * LANES), BF),
+        compiler_params=pltpu.CompilerParams(vmem_limit_bytes=48 << 20),
+        cost_estimate=cost(pieces[0].size * 8, pieces[0].size * 16),
+    )(x, *pieces)
+
+
+def project(off, taps, tokens, table, cot):
     depth = tokens.shape[1]
-    blocks, at_once = tokens.shape[0] // LANES, 2
+    blocks, at_once = tokens.shape[0] // LANES, 4
+    shape = (blocks, LANES, LANES)
     return pl.pallas_call(
         project_kernel,
         grid=(blocks // at_once,),
-        in_specs=[SCALAR, pl.BlockSpec((at_once * LANES, depth), lambda i: (i, 0))]
-        + [whole_spec(piece.shape) for piece in pieces],
-        out_specs=[block_spec(at_once)] * 4,
-        out_shape=[jax.ShapeDtypeStruct((blocks, LANES, LANES), BF)] * 4,
-        scratch_shapes=[pltpu.VMEM((depth, 3 * LANES), BF)],
-        compiler_params=PARAMS,
-        cost_estimate=cost(2 * tokens.size * 3 * LANES, 2 * tokens.size),
-    )(x, tokens, *pieces)
-
-
-def back(off, taps, q, cot):
-    n, at_once = q.shape[0], 2
-    return pl.pallas_call(
-        back_kernel,
-        grid=(n // at_once,),
-        in_specs=[pl.BlockSpec((at_once, 1, LANES), lambda i: (i, 0, 0)), whole_spec(taps.shape)]
-        + [block_spec(at_once)] * 2,
-        out_specs=[block_spec(at_once)] * 2,
-        out_shape=[jax.ShapeDtypeStruct(q.shape, BF), jax.ShapeDtypeStruct(q.shape, F32)],
+        in_specs=[
+            pl.BlockSpec((at_once, 1, LANES), lambda i: (i, 0, 0)),
+            whole_spec(taps.shape),
+            pl.BlockSpec((at_once * LANES, depth), lambda i: (i, 0)),
+            whole_spec(table.shape),
+            block_spec(at_once),
+        ],
+        out_specs=[block_spec(at_once)] * 6,
+        out_shape=[jax.ShapeDtypeStruct(shape, BF)] * 5 + [jax.ShapeDtypeStruct(shape, F32)],
         scratch_shapes=[pltpu.VMEM((PER, LANES, LANES), BF)],
         compiler_params=PARAMS,
-        cost_estimate=cost(2 * q.size * 2 * LANES * PER, 10 * q.size),
-    )(off, taps, q, cot)
+        cost_estimate=cost(2 * tokens.size * 3 * LANES + 4 * cot.size * LANES * PER, 2 * tokens.size),
+    )(off, taps, tokens, table, cot)
 
 
 def front(off, taps, q, cot, product, halo):
@@ -233,10 +234,10 @@
     rows = 3 * feats // 2 + EXTRA
     return pl.pallas_call(
         weight_kernel,
-        grid=(lo,),
-        in_specs=[SCALAR, pl.BlockSpec((tokens.shape[0], xs * feats), lambda i: (0, i))]
+        grid=(lo // 2,),
+        in_specs=[SCALAR, pl.BlockSpec((tokens.shape[0], 2 * xs * feats), lambda i: (0, i))]
         + [whole_spec(operand.shape) for operand in operands],
-        out_specs=pl.BlockSpec((xs, hi, 1, rows, LANES), lambda i: (0, 0, i, 0, 0)),
+        out_specs=pl.BlockSpec((xs, hi, 2, rows, LANES), lambda i: (0, 0, i, 0, 0)),
         out_shape=jax.ShapeDtypeStruct((xs, hi, lo, rows, LANES), BF),
         scratch_shapes=[pltpu.VMEM((tokens.shape[0], 3 * LANES), BF)],
         compiler_params=PARAMS,
@@ -244,50 +245,47 @@
     )(x, tokens, *operands)
 
 
-def seq_pairs(by, turn):
-    halves = lax.axis_size("z_hi")
-    steps = lax.axis_size(("z_p", "x"))
-    pairs = []
-    for h in range(halves):
-        for i in range(steps):
-            to = i + by
-            h_to = h if 0 <= to < steps else (h + turn) % halves
-            pairs.append((h * steps + i, h_to * steps + to % steps))
-    return pairs
+def seq_ring(shard, by):
+    halves, steps = lax.axis_size("z_hi"), lax.axis_size(("z_p", "x"))
+    pairs = [(h * steps + i, h * steps + (i + by) % steps) for h in range(halves) for i in range(steps)]
+    return lax.ppermute(shard, SEQ_AX, pairs)
+
+
+def over_middle(shard):
+    halves, steps = lax.axis_size("z_hi"), lax.axis_size(("z_p", "x"))
+    ends = [(h * steps + steps - 1, (h + 1) * steps) for h in range(halves - 1)]
+    return lax.ppermute(shard, SEQ_AX, ends + [(b, a) for a, b in ends])
 
 
 def at_start():
     return lax.axis_index(("z_p", "x")) == 0
 
 
+def at_end():
+    return lax.axis_index(("z_p", "x")) == lax.axis_size(("z_p", "x")) - 1
+
+
 def at_last_x():
     return lax.axis_index("x") == lax.axis_size("x") - 1
 
 
-def halo_forward(product):
+def halos(product, grad_prev):
     pairs = product.reshape(-1, 2, LANES, LANES)
-    even, odd = pairs[:, 0], pairs[:, 1]
-    far = jnp.where(at_last_x(), odd, even)
-    near = jnp.where(at_last_x(), even, odd)
-    most = lax.ppermute(far[:-1], SEQ_AX, seq_pairs(1, 0))
-    last = lax.ppermute(far[-1:], SEQ_AX, seq_pairs(1, 1))
+    far = jnp.where(at_last_x(), pairs[:, 1], pairs[:, 0])
+    near = jnp.where(at_last_x(), pairs[:, 0], pairs[:, 1])
+    pairs = grad_prev.reshape(-1, 2, LANES, LANES)
+    far_back, near_back = pairs[:, 0], pairs[:, 1]
+    last = over_middle(jnp.where(at_start(), far_back[:1], far[-1:]))
+    far = seq_ring(far, 1)
+    far_back = seq_ring(jnp.where(at_start(), jnp.concatenate([far_back[1:], far_back[:1]], 0), far_back), -1)
     near = turned(near, "x", 1)
-    far = jnp.where(at_start(), jnp.concatenate([last, most], 0), jnp.concatenate([most, last], 0))
-    return jnp.stack([far, near], 1).reshape(product.shape)
-
-
-def halo_back(grad_prev):
-    pairs = grad_prev.reshape(-1, 2, LANES, LANES)
-    far, near = pairs[:, 0], pairs[:, 1]
-    most = jnp.where(at_start(), far[1:], far[:-1])
-    last = jnp.where(at_start(), far[:1], far[-1:])
-    most = lax.ppermute(most, SEQ_AX, seq_pairs(-1, 0))
-    last = lax.ppermute(last, SEQ_AX, seq_pairs(-1, -1))
-    near = turned(near, "x", -1)
-    far = jnp.concatenate([most, last], 0)
-    even = jnp.where(at_last_x(), near, far)
-    odd = jnp.where(at_last_x(), far, near)
-    return jnp.stack([even, odd], 1).reshape(grad_prev.shape)
+    near_back = turned(near_back, "x", -1)
+    far = jnp.where(at_start(), jnp.concatenate([last, far[:-1]], 0), far)
+    halo = jnp.stack([far, near], 1).reshape(product.shape)
+    far_back = jnp.concatenate([far_back[:-1], jnp.where(at_end(), last, far_back[-1:])], 0)
+    even = jnp.where(at_last_x(), near_back, far_back)
+    odd = jnp.where(at_last_x(), far_back, near_back)
+    return halo, jnp.stack([even, odd], 1).reshape(product.shape)
 
 
 def split_rows(values):
@@ -309,13 +307,15 @@
     member = lax.axis_index("z_c")
 
     gathered = lax.all_gather(tokens, TOK_AX, axis=0, tiled=True)
+    cot = cotangent.reshape(rows, hi, places, 2, HALF).transpose(2, 3, 0, 1, 4).reshape(blocks, rows, LANES)
+    cot = swap_blocks(cot, TOK_AX)
+    in_weight, _ = lax.optimization_barrier((in_weight, cot))
     packed = in_weight.reshape(3, 2, short, 2, HALF).transpose(3, 0, 2, 1, 4).reshape(2, row_count, LANES)
     packed = jnp.broadcast_to(packed[None, None], (hi, lo // 2, 2, row_count, LANES))
     by_z = swap_blocks(packed.reshape(hi * lo, row_count, LANES), Z_AX)
     pieces = [by_z] + [turned(by_z, "x", step) for step in range(1, xs)]
     pieces = [piece.reshape(hi, lo, 3, short, LANES) for piece in pieces]
-    cot = cotangent.reshape(rows, hi, places, 2, HALF).transpose(2, 3, 0, 1, 4).reshape(blocks, rows, LANES)
-    cot = swap_blocks(cot, TOK_AX)
+    table = unpack(x, pieces)
 
     other = turned(filters, "z_hi", 1)
     upper = lax.axis_index("z_hi") == 0
@@ -327,10 +327,8 @@
     off = jnp.where(member == 0, jnp.stack([off, off_other], 1), jnp.stack([off_other, off], 1))
     off = off.reshape(blocks, 1, LANES)
 
-    q, k, v, product = project(x, gathered, pieces)
-    halo = halo_forward(product)
-    grad_prev, grad_own = back(off, taps, q, cot)
-    got = halo_back(grad_prev)
+    q, k, v, product, grad_prev, grad_own = project(off, taps, gathered, table, cot)
+    halo, got = halos(product, grad_prev)
     gated, grad_q, grad_taps = front(off, taps_back, q, cot, product, halo)
     out = swap_blocks(gated, TOK_AX)
     out = out.reshape(places, 2, rows, hi, HALF).transpose(2, 3, 0, 1, 4).reshape(rows, -1)

time: 250 us -> 230 us (0.920)
  waiting for transfers between devices: 96.9 us -> 76.3 us
  blocking collectives: 0 us -> 15.3 us
  local copies, waits for them, and re-layouts: 13.3 us -> 7.64 us
  starting transfers between devices: 89.1 us -> 83.6 us
  Pallas kernels: 31.6 us -> 27.3 us
    all_to_all x0 -> x1, blocking collectives: none -> 15.3 us  [swap_blocks(): return lax.all_to_all(pieces, axes, split_axis=0, concat_axis=0, tiled=True)]
    ppermute x10, starting transfers between devices: 34.4 us -> 47.5 us  [turned(): lax.ppermute(shard, axis, [(i, (i + by) % count) for i in range(count)])]
    all_to_all x4 -> x3, waiting for transfers between devices: 47.8 us -> 36 us  [swap_blocks(): return lax.all_to_all(pieces, axes, split_axis=0, concat_axis=0, tiled=True)]
    all_to_all x4 -> x3, starting transfers between devices: 40.6 us -> 28.9 us  [swap_blocks(): return lax.all_to_all(pieces, axes, split_axis=0, concat_axis=0, tiled=True)]
    ppermute x4 -> x3, waiting for transfers between devices: 12.8 us -> 2.77 us  [the longest x2 2.76 us: seq_ring(): return lax.ppermute(shard, SEQ_AX, pairs)]
    ppermute x4 -> x3, starting transfers between devices: 14.1 us -> 7.19 us  [the longest x2 6.53 us: seq_ring(): return lax.ppermute(shard, SEQ_AX, pairs)]
    pallas_call x3, Pallas kernels: 22.9 us -> 17.8 us  [the longest x1 9.32 us: project(): pl.pallas_call(project_kernel, grid=(blocks // at_once,), in_specs=[pl.Bl...]
    unnamed x29 -> x16, local copies, waits for them, and re-layouts: 7.64 us -> 3.4 us
  transfers between devices with their start and end apart: 19 -> 17, of which waited for: 8 -> 9; matrix products, arithmetic and copies ran while one was open for 3% -> 3% of each run, Pallas kernels for 11% -> 8%
where the time goes in v3:
time: 230 us; the launch traced here: 229 us
  starting transfers between devices  83.6 us (36%)
  waiting for transfers between devices  76.3 us (33%)
  Pallas kernels  27.3 us (12%)
  blocking collectives  15.3 us (7%)
  between operations  14.5 us (6%)
  local copies, waits for them, and re-layouts  7.64 us (3%)
  other arithmetic  3.94 us (2%)
    ppermute x10, starting transfers between devices, turned(): lax.ppermute(shard, axis, [(i, (i + by) % count) for i in range(count)])  47.5 us
    all_to_all x3, waiting for transfers between devices, swap_blocks(): return lax.all_to_all(pieces, axes, split_axis=0, concat_axis=0, tiled=True)  36 us
    ppermute x10, waiting for transfers between devices, turned(): lax.ppermute(shard, axis, [(i, (i + by) % count) for i in range(count)])  33.5 us
    all_to_all x3, starting transfers between devices, swap_blocks(): return lax.all_to_all(pieces, axes, split_axis=0, concat_axis=0, tiled=True)  28.9 us
    all_to_all x1, blocking collectives, swap_blocks(): return lax.all_to_all(pieces, axes, split_axis=0, concat_axis=0, tiled=True)  15.3 us
    pallas_call x1, Pallas kernels, front(): pl.pallas_call(front_kernel, grid=(n // at_once,), in_specs=[pl.BlockSpec...  9.56 us
    pallas_call x1, Pallas kernels, project(): pl.pallas_call(project_kernel, grid=(blocks // at_once,), in_specs=[pl.Bl...  9.32 us
    pallas_call x1, Pallas kernels, weight_grad(): pl.pallas_call(weight_kernel, grid=(lo // 2,), in_specs=[SCALAR, pl.Block...  7.77 us
  transfers between devices with their start and end apart: 17, of which 9 were waited for; matrix products, arithmetic and copies ran while one was open for 3% of the time, Pallas kernels for 8%

profile of v3, /device:TPU:38, one launch (start us, length us, event | category | flops | bytes accessed | tf_op | source)
XLA Modules:
  0.0 228.6 jit_solution(4805856770825910134)
XLA Ops:
  7.2 0.7 all-gather.2.cloned.1.call-update
  7.9 1.3 copy.21
  9.3 0.3 copy.23
  9.6 15.3 %all_to_all.20.cot_ref = bf16[16,128,128]{2,1,0:T(8,128)(2,1)} all-to-all(bf16[16,128,128]{2,1,0:T(8,128)(2,1)S(1)} %copy.23), channel_id=1, replica_groups=mesh['z_hi'=2,'y'=4,'core'=2,'z_p'=4,'z_c'=2,'x'=4] {'y','core','z_c'}, dimensions={0} | all-to-all | bytes 1048576 | tf_op jit(solution)/shard_map/all_to_all | solution.py:23
  25.0 0.1 copy.43
  25.1 0.1 broadcast_in_dim.11
  25.2 0.8 broadcast_in_dim.12
  26.0 14.8 %all-to-all-start.1 = ((bf16[16,96,128]{2,1,0:T(8,128)(2,1)}), bf16[16,96,128]{2,1,0:T(8,128)(2,1)S(1)}, u32[]{:S(2)}, u32[]{:S(2)}) async-start(bf16[16,96,128]{2,1,0:T(8,128)(2,1)} %bitcast.11), calls=%async_computation.1 | async-start | bytes 786432 | tf_op jit(solution)/shard_map/all_to_all | solution.py:23
  40.8 2.0 collective-permute-start
  42.8 12.5 %collective-permute-start.1 = (f32[8,128]{1,0:T(8,128)S(1)}, f32[8,128]{1,0:T(8,128)S(1)}, u32[]{:S(2)}, u32[]{:S(2)}) collective-permute-start(f32[8,128]{1,0:T(8,128)S(1)} %copy-done.6), channel_id=1, source_target_pairs={{0,256},{256,0},{1,257},{257,1},{2,258},{258,2},{3,259},{259,3},{4... | collective-permute-start | bytes 12296 | tf_op jit(solution)/shard_map/ppermute | solution.py:28
  55.4 12.0 %all-to-all-done.1 = bf16[16,96,128]{2,1,0:T(8,128)(2,1)S(1)} async-done(((bf16[16,96,128]{2,1,0:T(8,128)(2,1)}), bf16[16,96,128]{2,1,0:T(8,128)(2,1)S(1)}, u32[]{:S(2)}, u32[]{:S(2)}) %all-to-all-start.1) | async-done | bytes 393248 | tf_op jit(solution)/shard_map/all_to_all | solution.py:23
  67.4 2.7 %collective-permute-start.4 = (bf16[16,96,128]{2,1,0:T(8,128)(2,1)S(1)}, bf16[16,96,128]{2,1,0:T(8,128)(2,1)S(1)}, u32[]{:S(2)}, u32[]{:S(2)}) collective-permute-start(bf16[16,96,128]{2,1,0:T(8,128)(2,1)S(1)} %all-to-all-done.1), channel_id=1, source_target_pairs={{0,3},{1,0},{2,1},{3,2},{4,7},{5,4},{6,5},{7,6},{8,11},{9,8},{10,9... | collective-permute-start | bytes 1179656 | tf_op jit(solution)/shard_map/ppermute | solution.py:28
  70.1 3.0 %collective-permute-start.3 = (bf16[16,96,128]{2,1,0:T(8,128)(2,1)S(1)}, bf16[16,96,128]{2,1,0:T(8,128)(2,1)S(1)}, u32[]{:S(2)}, u32[]{:S(2)}) collective-permute-start(bf16[16,96,128]{2,1,0:T(8,128)(2,1)S(1)} %all-to-all-done.1), channel_id=1, source_target_pairs={{0,2},{1,3},{2,0},{3,1},{4,6},{5,7},{6,4},{7,5},{8,10},{9,11},{10,... | collective-permute-start | bytes 1179656 | tf_op jit(solution)/shard_map/ppermute | solution.py:28
  73.2 4.0 %collective-permute-start.2 = (bf16[16,96,128]{2,1,0:T(8,128)(2,1)S(1)}, bf16[16,96,128]{2,1,0:T(8,128)(2,1)S(1)}, u32[]{:S(2)}, u32[]{:S(2)}) collective-permute-start(bf16[16,96,128]{2,1,0:T(8,128)(2,1)S(1)} %all-to-all-done.1), channel_id=1, source_target_pairs={{0,1},{1,2},{2,3},{3,0},{4,5},{5,6},{6,7},{7,4},{8,9},{9,10},{10,1... | collective-permute-start | bytes 1179656 | tf_op jit(solution)/shard_map/ppermute | solution.py:28
  77.5 8.9 %collective-permute-done.4 = bf16[16,96,128]{2,1,0:T(8,128)(2,1)S(1)} collective-permute-done((bf16[16,96,128]{2,1,0:T(8,128)(2,1)S(1)}, bf16[16,96,128]{2,1,0:T(8,128)(2,1)S(1)}, u32[]{:S(2)}, u32[]{:S(2)}) %collective-permute-start.4) | collective-permute-done | bytes 393248 | tf_op jit(solution)/shard_map/ppermute | solution.py:28
  86.4 2.5 %collective-permute-done.2 = bf16[16,96,128]{2,1,0:T(8,128)(2,1)S(1)} collective-permute-done((bf16[16,96,128]{2,1,0:T(8,128)(2,1)S(1)}, bf16[16,96,128]{2,1,0:T(8,128)(2,1)S(1)}, u32[]{:S(2)}, u32[]{:S(2)}) %collective-permute-start.2) | collective-permute-done | bytes 393248 | tf_op jit(solution)/shard_map/ppermute | solution.py:28
  88.9 0.7 shard_map.76.w_ref
  89.6 3.4 %all-gather.2.cloned.1.call-done.tok_ref = bf16[2048,2048]{1,0:T(8,128)(2,1)} async-done(((bf16[128,2048]{1,0:T(8,128)(2,1)}), bf16[2048,2048]{1,0:T(8,128)(2,1)}) %all-gather.2.cloned.1.call-update) | async-done | bytes 8388624 | tf_op jit(solution)/shard_map/all_gather | solution.py:309
  93.0 1.0 copy-done.3
  94.0 9.3 %shard_map.77 = (bf16[16,128,128]{2,1,0:T(8,128)(2,1)S(1)}, bf16[16,128,128]{2,1,0:T(8,128)(2,1)S(1)}, bf16[16,128,128]{2,1,0:T(8,128)(2,1)S(1)}, bf16[16,128,12...) custom-call(s32[16,1,128]{2,1,0:T(1,128)S(1)} %bitcast.111, ...), custom_call_target="tpu_custom_call" | custom-call | flops 4294967296 | bytes 8388608 | tf_op jit(solution)/shard_map/pallas_call | solution.py:199
  103.4 0.8 slice_bitcast_fusion.5
  104.3 4.5 %collective-permute-start.6 = (bf16[8,128,128]{2,1,0:T(8,128)(2,1)S(1)}, bf16[8,128,128]{2,1,0:T(8,128)(2,1)S(1)}, u32[]{:S(2)}, u32[]{:S(2)}) collective-permute-start(bf16[8,128,128]{2,1,0:T(8,128)(2,1)S(1)} %fusion.17), channel_id=1, source_target_pairs={{0,1},{1,2},{2,3},{3,8},{8,9},{9,10},{10,11},{11,16},{16,17},{17,1... | collective-permute-start | bytes 786440 | tf_op jit(solution)/shard_map/ppermute | solution.py:251
  108.8 0.7 collective-permute-start.5
  109.5 1.9 collective-permute-start.7
  111.4 3.9 %collective-permute-start.8 = (bf16[8,128,128]{2,1,0:T(8,128)(2,1)}, bf16[8,128,128]{2,1,0:T(8,128)(2,1)}, u32[]{:S(2)}, u32[]{:S(2)}) collective-permute-start(bf16[8,128,128]{2,1,0:T(8,128)(2,1)} %slice_bitcast_fusion.5), channel_id=1, source_target_pairs={{0,3},{1,0},{2,1},{3,2},{4,7},{5,4},{6,5},{7,6},{8,11},{9,8},{10,9... | collective-permute-start | bytes 786440 | tf_op jit(solution)/shard_map/ppermute | solution.py:28
  115.3 0.8 fusion.2
  116.1 2.0 collective-permute-start.9
  118.2 2.8 %collective-permute-done.6 = bf16[8,128,128]{2,1,0:T(8,128)(2,1)S(1)} collective-permute-done((bf16[8,128,128]{2,1,0:T(8,128)(2,1)S(1)}, bf16[8,128,128]{2,1,0:T(8,128)(2,1)S(1)}, u32[]{:S(2)}, u32[]{:S(2)}) %collective-permute-start.6) | collective-permute-done | bytes 262176 | tf_op jit(solution)/shard_map/ppermute | solution.py:251
  121.0 2.2 collective-permute-done.7
  123.3 9.6 %shard_map.78 = (bf16[16,128,128]{2,1,0:T(8,128)(2,1)}, bf16[16,128,128]{2,1,0:T(8,128)(2,1)S(1)}, f32[8,128]{1,0:T(8,128)S(1)}) custom-call(s32[16,1,128]{2,1,0:T(1,128)S(1)} %bitcast.112, f32[8,128]{1,0:T(8,128)S(1)} %pad_maximum_fusion.4.taps_ref, bf16[16,128,128]{2,1,0:T(8,128)(2,1)S(1)} %get-tuple-element.14.q_ref, bf16[16,128,128]{2,1,0:T(8,128)(2,1)S(1)} %copy-done.4, ...), custom_call_target="tpu_custom_call" | custom-call | flops 2147483648 | bytes 3145728 | tf_op jit(solution)/shard_map/pallas_call | solution.py:219
  132.9 5.5 %all-to-all-start.2 = ((bf16[16,128,128]{2,1,0:T(8,128)(2,1)}), bf16[16,128,128]{2,1,0:T(8,128)(2,1)S(1)}, u32[]{:S(2)}, u32[]{:S(2)}) async-start(bf16[16,128,128]{2,1,0:T(8,128)(2,1)} %get-tuple-element.17), calls=%async_computation.2 | async-start | bytes 1048576 | tf_op jit(solution)/shard_map/all_to_all | solution.py:23
  138.4 1.0 select_bitcast_fusion.1
  139.5 7.8 %shard_map.79 = bf16[4,2,8,112,128]{4,3,2,1,0:T(8,128)(2,1)S(1)} custom-call(s32[1]{0:T(128)} %bitcast.6.x_ref, bf16[2048,2048]{1,0:T(8,128)(2,1)} %all-gather.2.cloned.1.call-done.tok_ref, bf16[16,128,128]{2,1,0:T(8,128)(2,1)S(1)} %get-tuple-element.18.gq_ref, f32[16,128,128]{2,1,0:T(8,128)S(1)} %get-tuple-element.19.own_ref, ...), custom_call_target="tpu_custom_call" | custom-call | flops 3221225472 | bytes 8388608 | tf_op jit(solution)/shard_map/pallas_call | solution.py:235
  147.4 12.1 %collective-permute-start.10 = (bf16[2,8,112,128]{3,2,1,0:T(8,128)(2,1)S(1)}, bf16[2,8,112,128]{3,2,1,0:T(8,128)(2,1)S(1)}, u32[]{:S(2)}, u32[]{:S(2)}) collective-permute-start(bf16[2,8,112,128]{3,2,1,0:T(8,128)(2,1)S(1)} %get-tuple-element.30), channel_id=1, source_target_pairs={{0,1},{1,2},{2,3},{3,0},{4,5},{5,6},{6,7},{7,4},{8,9},{9,10},{10,1... | collective-permute-start | bytes 1376264 | tf_op jit(solution)/shard_map/ppermute | solution.py:28
  159.5 1.9 collective-permute-start.12
  161.4 3.4 %collective-permute-start.11 = (bf16[2,8,112,128]{3,2,1,0:T(8,128)(2,1)S(1)}, bf16[2,8,112,128]{3,2,1,0:T(8,128)(2,1)S(1)}, u32[]{:S(2)}, u32[]{:S(2)}) collective-permute-start(bf16[2,8,112,128]{3,2,1,0:T(8,128)(2,1)S(1)} %get-tuple-element.32), channel_id=1, source_target_pairs={{0,2},{1,3},{2,0},{3,1},{4,6},{5,7},{6,4},{7,5},{8,10},{9,11},{10,... | collective-permute-start | bytes 1376264 | tf_op jit(solution)/shard_map/ppermute | solution.py:28
  164.8 14.6 %collective-permute-done.10 = bf16[2,8,112,128]{3,2,1,0:T(8,128)(2,1)S(1)} collective-permute-done((bf16[2,8,112,128]{3,2,1,0:T(8,128)(2,1)S(1)}, bf16[2,8,112,128]{3,2,1,0:T(8,128)(2,1)S(1)}, u32[]{:S(2)}, u32[]{:S(2)}) %collective-permute-start.10) | collective-permute-done | bytes 458784 | tf_op jit(solution)/shard_map/ppermute | solution.py:28
  179.4 5.3 %collective-permute-done.12 = bf16[2,8,112,128]{3,2,1,0:T(8,128)(2,1)S(1)} collective-permute-done((bf16[2,8,112,128]{3,2,1,0:T(8,128)(2,1)S(1)}, bf16[2,8,112,128]{3,2,1,0:T(8,128)(2,1)S(1)}, u32[]{:S(2)}, u32[]{:S(2)}) %collective-permute-start.12) | collective-permute-done | bytes 458784 | tf_op jit(solution)/shard_map/ppermute | solution.py:28
  184.7 0.2 fusion.1
  185.0 0.8 pad_maximum_fusion.2
  185.9 8.6 %all-to-all-start.3 = ((bf16[16,112,128]{2,1,0:T(8,128)(2,1)}), bf16[16,112,128]{2,1,0:T(8,128)(2,1)S(1)}, u32[]{:S(2)}, u32[]{:S(2)}) async-start(bf16[16,112,128]{2,1,0:T(8,128)(2,1)} %bitcast.43), calls=%async_computation.3 | async-start | bytes 917504 | tf_op jit(solution)/shard_map/all_to_all | solution.py:23
  194.4 0.3 copy.31
  194.8 1.0 copy.36
  195.8 24.0 %all-to-all-done.3 = bf16[16,112,128]{2,1,0:T(8,128)(2,1)S(1)} async-done(((bf16[16,112,128]{2,1,0:T(8,128)(2,1)}), bf16[16,112,128]{2,1,0:T(8,128)(2,1)S(1)}, u32[]{:S(2)}, u32[]{:S(2)}) %all-to-all-start.3) | async-done | bytes 458784 | tf_op jit(solution)/shard_map/all_to_all | solution.py:23
  220.0 0.2 reshape.116
  220.2 0.2 copy.42
  220.3 0.8 reshape.117
  221.1 0.7 pad_maximum_fusion.5
  (57 shorter events, 1.3 us)
Async XLA Ops:
  7.2 33.6 %copy-start = (s32[16,128]{1,0:T(8,128)S(1)}, s32[16,128]{1,0:T(8,128)}, u32[]{:S(2)}) copy-start(s32[16,128]{1,0:T(8,128)} %param.8) | copy-start | bytes 24580
  7.2 85.8 %all-gather.2.cloned.1.call-start = ((), (), s32[]{:S(2)}) async-start(), calls=%async_computation.4 | async-start | bytes 8912896 | tf_op jit(solution)/shard_map/all_gather | solution.py:309
  9.2 15.6 %copy-start.5 = (bf16[3,64,128]{2,1,0:T(8,128)(2,1)S(1)}, bf16[3,64,128]{2,1,0:T(8,128)(2,1)}, u32[]{:S(2)}) copy-start(bf16[3,64,128]{2,1,0:T(8,128)(2,1)} %param.6) | copy-start | bytes 147460
  9.3 33.5 %copy-start.6 = (f32[8,128]{1,0:T(8,128)S(1)}, f32[8,128]{1,0:T(8,128)}, u32[]{:S(2)}) copy-start(f32[8,128]{1,0:T(8,128)} %param.7) | copy-start | bytes 12292
  26.0 41.4 %all-to-all-start.1 = ((bf16[16,96,128]{2,1,0:T(8,128)(2,1)}), bf16[16,96,128]{2,1,0:T(8,128)(2,1)S(1)}, u32[]{:S(2)}, u32[]{:S(2)}) async-start(bf16[16,96,128]{2,1,0:T(8,128)(2,1)} %bitcast.11), calls=%async_computation.1 | async-start | bytes 786432 | tf_op jit(solution)/shard_map/all_to_all | solution.py:23
  40.8 36.5 %collective-permute-start = (s32[8,128]{1,0:T(8,128)S(1)}, s32[8,128]{1,0:T(8,128)S(1)}, u32[]{:S(2)}, u32[]{:S(2)}) collective-permute-start(s32[8,128]{1,0:T(8,128)S(1)} %constant_dynamic-slice_fusion), channel_id=1, source_target_pairs={{0,4},{4,0},{1,5},{5,1},{2,6},{6,2},{3,7},{7,3},{8,12},{12,8},{9,1... | collective-permute-start | bytes 12296 | tf_op jit(solution)/shard_map/ppermute | solution.py:28
  42.8 34.5 %collective-permute-start.1 = (f32[8,128]{1,0:T(8,128)S(1)}, f32[8,128]{1,0:T(8,128)S(1)}, u32[]{:S(2)}, u32[]{:S(2)}) collective-permute-start(f32[8,128]{1,0:T(8,128)S(1)} %copy-done.6), channel_id=1, source_target_pairs={{0,256},{256,0},{1,257},{257,1},{2,258},{258,2},{3,259},{259,3},{4... | collective-permute-start | bytes 12296 | tf_op jit(solution)/shard_map/ppermute | solution.py:28
  67.4 19.0 %collective-permute-start.4 = (bf16[16,96,128]{2,1,0:T(8,128)(2,1)S(1)}, bf16[16,96,128]{2,1,0:T(8,128)(2,1)S(1)}, u32[]{:S(2)}, u32[]{:S(2)}) collective-permute-start(bf16[16,96,128]{2,1,0:T(8,128)(2,1)S(1)} %all-to-all-done.1), channel_id=1, source_target_pairs={{0,3},{1,0},{2,1},{3,2},{4,7},{5,4},{6,5},{7,6},{8,11},{9,8},{10,9... | collective-permute-start | bytes 1179656 | tf_op jit(solution)/shard_map/ppermute | solution.py:28
  70.1 16.2 %collective-permute-start.3 = (bf16[16,96,128]{2,1,0:T(8,128)(2,1)S(1)}, bf16[16,96,128]{2,1,0:T(8,128)(2,1)S(1)}, u32[]{:S(2)}, u32[]{:S(2)}) collective-permute-start(bf16[16,96,128]{2,1,0:T(8,128)(2,1)S(1)} %all-to-all-done.1), channel_id=1, source_target_pairs={{0,2},{1,3},{2,0},{3,1},{4,6},{5,7},{6,4},{7,5},{8,10},{9,11},{10,... | collective-permute-start | bytes 1179656 | tf_op jit(solution)/shard_map/ppermute | solution.py:28
  73.2 15.7 %collective-permute-start.2 = (bf16[16,96,128]{2,1,0:T(8,128)(2,1)S(1)}, bf16[16,96,128]{2,1,0:T(8,128)(2,1)S(1)}, u32[]{:S(2)}, u32[]{:S(2)}) collective-permute-start(bf16[16,96,128]{2,1,0:T(8,128)(2,1)S(1)} %all-to-all-done.1), channel_id=1, source_target_pairs={{0,1},{1,2},{2,3},{3,0},{4,5},{5,6},{6,7},{7,4},{8,9},{9,10},{10,1... | collective-permute-start | bytes 1179656 | tf_op jit(solution)/shard_map/ppermute | solution.py:28
  93.0 1.0 copy-start.3
  103.3 12.8 %copy-start.1 = (bf16[16,128,128]{2,1,0:T(8,128)(2,1)}, bf16[16,128,128]{2,1,0:T(8,128)(2,1)S(1)}, u32[]{:S(2)}) copy-start(bf16[16,128,128]{2,1,0:T(8,128)(2,1)S(1)} %get-tuple-element.21.v_ref) | copy-start | bytes 1572868
  104.3 16.6 %collective-permute-start.6 = (bf16[8,128,128]{2,1,0:T(8,128)(2,1)S(1)}, bf16[8,128,128]{2,1,0:T(8,128)(2,1)S(1)}, u32[]{:S(2)}, u32[]{:S(2)}) collective-permute-start(bf16[8,128,128]{2,1,0:T(8,128)(2,1)S(1)} %fusion.17), channel_id=1, source_target_pairs={{0,1},{1,2},{2,3},{3,8},{8,9},{9,10},{10,11},{11,16},{16,17},{17,1... | collective-permute-start | bytes 786440 | tf_op jit(solution)/shard_map/ppermute | solution.py:251
  108.8 12.1 %collective-permute-start.5 = (bf16[1,128,128]{2,1,0:T(8,128)(2,1)S(1)}, bf16[1,128,128]{2,1,0:T(8,128)(2,1)S(1)}, u32[]{:S(2)}, u32[]{:S(2)}) collective-permute-start(bf16[1,128,128]{2,1,0:T(8,128)(2,1)S(1)} %fusion.8), channel_id=1, source_target_pairs={{27,256},{256,27},{31,260},{260,31},{59,288},{288,59},{63,292},{29... | collective-permute-start | bytes 98312 | tf_op jit(solution)/shard_map/ppermute | solution.py:257
  109.5 13.7 %collective-permute-start.7 = (bf16[8,128,128]{2,1,0:T(8,128)(2,1)S(1)}, bf16[8,128,128]{2,1,0:T(8,128)(2,1)S(1)}, u32[]{:S(2)}, u32[]{:S(2)}) collective-permute-start(bf16[8,128,128]{2,1,0:T(8,128)(2,1)S(1)} %fusion.4), channel_id=1, source_target_pairs={{0,1},{1,2},{2,3},{3,0},{4,5},{5,6},{6,7},{7,4},{8,9},{9,10},{10,1... | collective-permute-start | bytes 786440 | tf_op jit(solution)/shard_map/ppermute | solution.py:28
  111.4 27.0 %collective-permute-start.8 = (bf16[8,128,128]{2,1,0:T(8,128)(2,1)}, bf16[8,128,128]{2,1,0:T(8,128)(2,1)}, u32[]{:S(2)}, u32[]{:S(2)}) collective-permute-start(bf16[8,128,128]{2,1,0:T(8,128)(2,1)} %slice_bitcast_fusion.5), channel_id=1, source_target_pairs={{0,3},{1,0},{2,1},{3,2},{4,7},{5,4},{6,5},{7,6},{8,11},{9,8},{10,9... | collective-permute-start | bytes 786440 | tf_op jit(solution)/shard_map/ppermute | solution.py:28
  116.1 7.2 %copy-start.4 = (bf16[16,128,128]{2,1,0:T(8,128)(2,1)S(1)}, bf16[16,128,128]{2,1,0:T(8,128)(2,1)}, u32[]{:S(2)}) copy-start(bf16[16,128,128]{2,1,0:T(8,128)(2,1)} %all_to_all.20.cot_ref) | copy-start | bytes 1572868
  116.1 22.3 %collective-permute-start.9 = (bf16[8,128,128]{2,1,0:T(8,128)(2,1)}, bf16[8,128,128]{2,1,0:T(8,128)(2,1)S(1)}, u32[]{:S(2)}, u32[]{:S(2)}) collective-permute-start(bf16[8,128,128]{2,1,0:T(8,128)(2,1)} %fusion.2), channel_id=1, source_target_pairs={{0,27},{1,0},{2,1},{3,2},{8,3},{9,8},{10,9},{11,10},{16,11},{17,16... | collective-permute-start | bytes 786440 | tf_op jit(solution)/shard_map/ppermute | solution.py:251
  132.9 6.7 %copy-start.2 = (bf16[16,128,128]{2,1,0:T(8,128)(2,1)S(1)}, bf16[16,128,128]{2,1,0:T(8,128)(2,1)}, u32[]{:S(2)}) copy-start(bf16[16,128,128]{2,1,0:T(8,128)(2,1)} %copy-done.1) | copy-start | bytes 1572868
  132.9 53.0 %all-to-all-start.2 = ((bf16[16,128,128]{2,1,0:T(8,128)(2,1)}), bf16[16,128,128]{2,1,0:T(8,128)(2,1)S(1)}, u32[]{:S(2)}, u32[]{:S(2)}) async-start(bf16[16,128,128]{2,1,0:T(8,128)(2,1)} %get-tuple-element.17), calls=%async_computation.2 | async-start | bytes 1048576 | tf_op jit(solution)/shard_map/all_to_all | solution.py:23
  147.4 32.0 %collective-permute-start.10 = (bf16[2,8,112,128]{3,2,1,0:T(8,128)(2,1)S(1)}, bf16[2,8,112,128]{3,2,1,0:T(8,128)(2,1)S(1)}, u32[]{:S(2)}, u32[]{:S(2)}) collective-permute-start(bf16[2,8,112,128]{3,2,1,0:T(8,128)(2,1)S(1)} %get-tuple-element.30), channel_id=1, source_target_pairs={{0,1},{1,2},{2,3},{3,0},{4,5},{5,6},{6,7},{7,4},{8,9},{9,10},{10,1... | collective-permute-start | bytes 1376264 | tf_op jit(solution)/shard_map/ppermute | solution.py:28
  159.5 25.2 %collective-permute-start.12 = (bf16[2,8,112,128]{3,2,1,0:T(8,128)(2,1)S(1)}, bf16[2,8,112,128]{3,2,1,0:T(8,128)(2,1)S(1)}, u32[]{:S(2)}, u32[]{:S(2)}) collective-permute-start(bf16[2,8,112,128]{3,2,1,0:T(8,128)(2,1)S(1)} %get-tuple-element.31), channel_id=1, source_target_pairs={{0,3},{1,0},{2,1},{3,2},{4,7},{5,4},{6,5},{7,6},{8,11},{9,8},{10,9... | collective-permute-start | bytes 1376264 | tf_op jit(solution)/shard_map/ppermute | solution.py:28
  161.4 23.3 %collective-permute-start.11 = (bf16[2,8,112,128]{3,2,1,0:T(8,128)(2,1)S(1)}, bf16[2,8,112,128]{3,2,1,0:T(8,128)(2,1)S(1)}, u32[]{:S(2)}, u32[]{:S(2)}) collective-permute-start(bf16[2,8,112,128]{3,2,1,0:T(8,128)(2,1)S(1)} %get-tuple-element.32), channel_id=1, source_target_pairs={{0,2},{1,3},{2,0},{3,1},{4,6},{5,7},{6,4},{7,5},{8,10},{9,11},{10,... | collective-permute-start | bytes 1376264 | tf_op jit(solution)/shard_map/ppermute | solution.py:28
  185.9 33.9 %all-to-all-start.3 = ((bf16[16,112,128]{2,1,0:T(8,128)(2,1)}), bf16[16,112,128]{2,1,0:T(8,128)(2,1)S(1)}, u32[]{:S(2)}, u32[]{:S(2)}) async-start(bf16[16,112,128]{2,1,0:T(8,128)(2,1)} %bitcast.43), calls=%async_computation.3 | async-start | bytes 917504 | tf_op jit(solution)/shard_map/all_to_all | solution.py:23
Sparse Core Ops, SparseCore 0:
  10.1 82.7 all-gather.1

commit v4 on v3

--- a/solution.py
+++ b/solution.py
@@ -14,7 +14,7 @@
 EXTRA = 16
 CTX = ("z_hi", "y", "core")
 ZERO = ("z_p", "z_c", "x")
-TOK_AX = ("y", "core", "z_c")
+TOK_AX = ("z_c", "y", "core")
 Z_AX = ("z_hi", "z_p", "z_c")
 SEQ_AX = ("z_hi", "z_p", "x")
 
@@ -53,19 +53,16 @@
         table_ref[g] = pltpu.roll(rows, 0, 1, stride=1, stride_axis=0).astype(BF)
 
 
-def unpack_kernel(x_ref, *refs):
-    w_refs, table = refs[:-1], refs[-1]
-    _, lo, parts, short, _ = w_refs[0].shape
-    xs = len(w_refs)
-    for step, w_ref in enumerate(w_refs):
-        x = lax.rem(x_ref[0] - step + xs, xs)
+def unpack_kernel(w_ref, table):
+    xs, _, lo, parts, short, _ = w_ref.shape
+    for x in range(xs):
         for l in range(lo):
-            at = pl.multiple_of((l * xs + x) * (2 * short), 2 * short)
+            at = (l * xs + x) * (2 * short)
             for p in range(parts):
                 cols = slice(p * LANES, (p + 1) * LANES)
-                top, low = lane_halves(w_ref[0, l, p].astype(F32), w_ref[1, l, p].astype(F32))
-                table[pl.ds(at, short), cols] = top.astype(BF)
-                table[pl.ds(at + short, short), cols] = low.astype(BF)
+                top, low = lane_halves(w_ref[x, 0, l, p].astype(F32), w_ref[x, 1, l, p].astype(F32))
+                table[at : at + short, cols] = top.astype(BF)
+                table[at + short : at + 2 * short, cols] = low.astype(BF)
 
 
 def project_kernel(off_ref, taps_ref, tok_ref, w_ref, cot_ref, q_ref, k_ref, v_ref, prod_ref, prev_ref, own_ref, table):
@@ -129,12 +126,25 @@
 
     @pl.when(step == pl.num_programs(0) - 1)
     def _():
+        sums = []
         for g in range(PER):
             lined = acc[g]
             for bit in range(7):
                 moved = pltpu.roll(lined, LANES - (1 << bit), 1)
                 lined = jnp.where((t >> bit) & 1 == 1, moved, lined)
-            df_ref[g : g + 1, :] = jnp.sum(lined, axis=0, keepdims=True)
+            sums.append(jnp.sum(lined, axis=0, keepdims=True))
+        sums = jnp.concatenate(sums, 0)
+        upper = sums.astype(BF)
+        lower = (sums - upper.astype(F32)).astype(BF)
+        mirror = jnp.where((t + u) % LANES == 0, 1.0, 0.0).astype(BF)
+        upper = jnp.dot(upper, mirror, preferred_element_type=F32)
+        lower = jnp.dot(lower, mirror, preferred_element_type=F32)
+        hi = df_ref.shape[0]
+        own = PER // hi
+        for h in range(hi):
+            at = slice(h * own, (h + 1) * own)
+            rows = jnp.concatenate([upper[at], lower[at], jnp.zeros((EXTRA - 2 * own, LANES), F32)], 0)
+            df_ref[h] = rows.astype(BF)
 
 
 def weight_kernel(x_ref, tok_ref, gq_ref, own_ref, got_ref, k_ref, v_ref, taps_ref, out_ref, grads):
@@ -180,16 +190,16 @@
     return pl.CostEstimate(flops=flops, bytes_accessed=moved, transcendentals=0)
 
 
-def unpack(x, pieces):
-    hi, lo, parts, short, _ = pieces[0].shape
+def unpack(pieces):
+    xs, hi, lo, parts, short, _ = pieces.shape
     return pl.pallas_call(
         unpack_kernel,
-        in_specs=[SCALAR] + [pl.BlockSpec(memory_space=pltpu.VMEM)] * len(pieces),
+        in_specs=[pl.BlockSpec(memory_space=pltpu.VMEM)],
         out_specs=pl.BlockSpec(memory_space=pltpu.VMEM),
-        out_shape=jax.ShapeDtypeStruct((lo * len(pieces) * 2 * short, parts * LANES), BF),
+        out_shape=jax.ShapeDtypeStruct((lo * xs * 2 * short, parts * LANES), BF),
         compiler_params=pltpu.CompilerParams(vmem_limit_bytes=48 << 20),
-        cost_estimate=cost(pieces[0].size * 8, pieces[0].size * 16),
-    )(x, *pieces)
+        cost_estimate=cost(2 * pieces.size, 4 * pieces.size),
+    )(pieces)
 
 
 def project(off, taps, tokens, table, cot):
@@ -214,15 +224,15 @@
     )(off, taps, tokens, table, cot)
 
 
-def front(off, taps, q, cot, product, halo):
+def front(hi, off, taps, q, cot, product, halo):
     n, at_once = q.shape[0], 2
     return pl.pallas_call(
         front_kernel,
         grid=(n // at_once,),
         in_specs=[pl.BlockSpec((at_once, 1, LANES), lambda i: (i, 0, 0)), whole_spec(taps.shape)]
         + [block_spec(at_once)] * 4,
-        out_specs=[block_spec(at_once)] * 2 + [whole_spec(taps.shape)],
-        out_shape=[jax.ShapeDtypeStruct(q.shape, BF)] * 2 + [jax.ShapeDtypeStruct(taps.shape, F32)],
+        out_specs=[block_spec(at_once)] * 2 + [whole_spec((hi, EXTRA, LANES))],
+        out_shape=[jax.ShapeDtypeStruct(q.shape, BF)] * 2 + [jax.ShapeDtypeStruct((hi, EXTRA, LANES), BF)],
         scratch_shapes=[pltpu.VMEM((PER, LANES, LANES), BF), pltpu.VMEM((PER, LANES, LANES), F32)],
         compiler_params=PARAMS,
         cost_estimate=cost(4 * q.size * 2 * LANES * PER, 12 * q.size),
@@ -270,22 +280,24 @@
 
 
 def halos(product, grad_prev):
-    pairs = product.reshape(-1, 2, LANES, LANES)
-    far = jnp.where(at_last_x(), pairs[:, 1], pairs[:, 0])
-    near = jnp.where(at_last_x(), pairs[:, 0], pairs[:, 1])
-    pairs = grad_prev.reshape(-1, 2, LANES, LANES)
-    far_back, near_back = pairs[:, 0], pairs[:, 1]
+    even, odd = product[: product.shape[0] // 2], product[product.shape[0] // 2 :]
+    far = jnp.where(at_last_x(), odd, even)
+    near = jnp.where(at_last_x(), even, odd)
+    far_back, near_back = grad_prev[: even.shape[0]], grad_prev[even.shape[0] :]
     last = over_middle(jnp.where(at_start(), far_back[:1], far[-1:]))
     far = seq_ring(far, 1)
     far_back = seq_ring(jnp.where(at_start(), jnp.concatenate([far_back[1:], far_back[:1]], 0), far_back), -1)
     near = turned(near, "x", 1)
     near_back = turned(near_back, "x", -1)
     far = jnp.where(at_start(), jnp.concatenate([last, far[:-1]], 0), far)
-    halo = jnp.stack([far, near], 1).reshape(product.shape)
+    return jnp.concatenate([far, near], 0), (far_back, near_back, last)
+
+
+def placed_back(far_back, near_back, last):
     far_back = jnp.concatenate([far_back[:-1], jnp.where(at_end(), last, far_back[-1:])], 0)
     even = jnp.where(at_last_x(), near_back, far_back)
     odd = jnp.where(at_last_x(), far_back, near_back)
-    return halo, jnp.stack([even, odd], 1).reshape(product.shape)
+    return jnp.concatenate([even, odd], 0)
 
 
 def split_rows(values):
@@ -307,35 +319,35 @@
     member = lax.axis_index("z_c")
 
     gathered = lax.all_gather(tokens, TOK_AX, axis=0, tiled=True)
-    cot = cotangent.reshape(rows, hi, places, 2, HALF).transpose(2, 3, 0, 1, 4).reshape(blocks, rows, LANES)
-    cot = swap_blocks(cot, TOK_AX)
-    in_weight, _ = lax.optimization_barrier((in_weight, cot))
     packed = in_weight.reshape(3, 2, short, 2, HALF).transpose(3, 0, 2, 1, 4).reshape(2, row_count, LANES)
     packed = jnp.broadcast_to(packed[None, None], (hi, lo // 2, 2, row_count, LANES))
     by_z = swap_blocks(packed.reshape(hi * lo, row_count, LANES), Z_AX)
-    pieces = [by_z] + [turned(by_z, "x", step) for step in range(1, xs)]
-    pieces = [piece.reshape(hi, lo, 3, short, LANES) for piece in pieces]
-    table = unpack(x, pieces)
-
     other = turned(filters, "z_hi", 1)
+    off = lax.dynamic_slice_in_dim(doc_offset, lax.axis_index("z_hi") * places, places, 0)
+    off_other = turned(off, "z_c", 1)
+    by_z, other, off_other = lax.optimization_barrier((by_z, other, off_other))
+    pieces = swap_blocks(jnp.broadcast_to(by_z[None], (xs,) + by_z.shape), "x")
+    cotangent, pieces = lax.optimization_barrier((cotangent, pieces))
+    cot = cotangent.reshape(rows, hi, places, 2, HALF).transpose(3, 2, 0, 1, 4).reshape(blocks, rows, LANES)
+    cot = swap_blocks(cot, TOK_AX)
+    table = unpack(pieces.reshape(xs, hi, lo, 3, short, LANES))
+
     upper = lax.axis_index("z_hi") == 0
     taps = jnp.where(upper, jnp.stack([filters, other]), jnp.stack([other, filters]))
     taps = lax.dynamic_slice_in_dim(taps, member * (PER // 2), PER // 2, 1).reshape(PER, LANES)
     taps_back = jnp.roll(jnp.flip(taps, 1), 1, axis=1)
-    off = lax.dynamic_slice_in_dim(doc_offset, lax.axis_index("z_hi") * places, places, 0)
-    off_other = turned(off, "z_c", 1)
-    off = jnp.where(member == 0, jnp.stack([off, off_other], 1), jnp.stack([off_other, off], 1))
+    off = jnp.where(member == 0, jnp.stack([off, off_other]), jnp.stack([off_other, off]))
     off = off.reshape(blocks, 1, LANES)
 
     q, k, v, product, grad_prev, grad_own = project(off, taps, gathered, table, cot)
-    halo, got = halos(product, grad_prev)
-    gated, grad_q, grad_taps = front(off, taps_back, q, cot, product, halo)
+    halo, back = halos(product, grad_prev)
+    gated, grad_q, grad_taps = front(hi, off, taps_back, q, cot, product, halo)
+    back, grad_q = lax.optimization_barrier((back, grad_q))
+    got = placed_back(*back)
+    partial = weight_grad(x, gathered, (grad_q, grad_own, got, k, v, grad_taps), (xs, hi, lo, feats))
+    gated, partial = lax.optimization_barrier((gated, partial))
     out = swap_blocks(gated, TOK_AX)
-    out = out.reshape(places, 2, rows, hi, HALF).transpose(2, 3, 0, 1, 4).reshape(rows, -1)
-
-    grad_taps = split_rows(grad_taps.reshape(hi, PER // 2, LANES))
-    grad_taps = jnp.pad(grad_taps, ((0, 0), (0, EXTRA - PER), (0, 0)))
-    partial = weight_grad(x, gathered, (grad_q, grad_own, got, k, v, grad_taps), (xs, hi, lo, feats))
+    out = out.reshape(2, places, rows, hi, HALF).transpose(2, 3, 1, 0, 4).reshape(rows, -1)
     parts = [partial[0]] + [turned(partial[step], "x", step) for step in range(1, xs)]
     over_x = sum(part.astype(F32) for part in parts)
     taps_x = over_x[:, :, row_count : row_count + PER // 2] + over_x[:, :, row_count + PER // 2 : row_count + PER]
@@ -346,7 +358,7 @@
     grad_weight = over_z[:, :row_count].reshape(2, 3, short, 2, HALF).transpose(1, 3, 2, 0, 4)
     grad_weight = grad_weight.reshape(3, feats, width)
     grad_taps = over_z[:, row_count : row_count + PER // 2] + over_z[:, row_count + PER // 2 : row_count + PER]
-    grad_taps = jnp.roll(jnp.flip(grad_taps.reshape(PER, LANES), 1), 1, axis=1)
+    grad_taps = grad_taps.reshape(PER, LANES)
     return (out, grad_weight, grad_taps)
 
 

time: 230 us -> 226 us (0.983)
  blocking collectives: 15.3 us -> 21.6 us
  starting transfers between devices: 83.6 us -> 78.3 us
  waiting for transfers between devices: 76.3 us -> 73.9 us
    ppermute x10 -> x7, starting transfers between devices: 47.5 us -> 34.5 us  [turned(): lax.ppermute(shard, axis, [(i, (i + by) % count) for i in range(count)])]
    all_to_all x3 -> x4, starting transfers between devices: 28.9 us -> 36.8 us  [swap_blocks(): return lax.all_to_all(pieces, axes, split_axis=0, concat_axis=0, tiled=True)]
    all_to_all x1, blocking collectives: 15.3 us -> 21.6 us  [swap_blocks(): return lax.all_to_all(pieces, axes, split_axis=0, concat_axis=0, tiled=True)]
    ppermute x10 -> x7, waiting for transfers between devices: 33.5 us -> 38.1 us  [turned(): lax.ppermute(shard, axis, [(i, (i + by) % count) for i in range(count)])]
    all_to_all x3 -> x4, waiting for transfers between devices: 36 us -> 32.5 us  [swap_blocks(): return lax.all_to_all(pieces, axes, split_axis=0, concat_axis=0, tiled=True)]
    all_gather x1, waiting for transfers between devices: 3.37 us -> 0.01 us  [body(): gathered = lax.all_gather(tokens, TOK_AX, axis=0, tiled=True)]
    unnamed x16 -> x7, local copies, waits for them, and re-layouts: 3.4 us -> 1.04 us
  transfers between devices with their start and end apart: 17 -> 15, of which waited for: 9 -> 8; matrix products, arithmetic and copies ran while one was open for 3% -> 3% of each run, Pallas kernels for 8% -> 5%
where the time goes in v4:
time: 226 us; the launch traced here: 224 us
  starting transfers between devices  78.3 us (35%)
  waiting for transfers between devices  73.9 us (33%)
  Pallas kernels  27.9 us (12%)
  blocking collectives  21.6 us (10%)
  between operations  14.4 us (6%)
  local copies, waits for them, and re-layouts  6.29 us (3%)
    ppermute x7, waiting for transfers between devices, turned(): lax.ppermute(shard, axis, [(i, (i + by) % count) for i in range(count)])  38.1 us
    all_to_all x4, starting transfers between devices, swap_blocks(): return lax.all_to_all(pieces, axes, split_axis=0, concat_axis=0, tiled=True)  36.8 us
    ppermute x7, starting transfers between devices, turned(): lax.ppermute(shard, axis, [(i, (i + by) % count) for i in range(count)])  34.5 us
    all_to_all x4, waiting for transfers between devices, swap_blocks(): return lax.all_to_all(pieces, axes, split_axis=0, concat_axis=0, tiled=True)  32.5 us
    all_to_all x1, blocking collectives, swap_blocks(): return lax.all_to_all(pieces, axes, split_axis=0, concat_axis=0, tiled=True)  21.6 us
    pallas_call x1, Pallas kernels, front(): pl.pallas_call(front_kernel, grid=(n // at_once,), in_specs=[pl.BlockSpec...  10.1 us
    pallas_call x1, Pallas kernels, project(): pl.pallas_call(project_kernel, grid=(blocks // at_once,), in_specs=[pl.Bl...  9.35 us
    pallas_call x1, Pallas kernels, weight_grad(): pl.pallas_call(weight_kernel, grid=(lo // 2,), in_specs=[SCALAR, pl.Block...  7.75 us
  transfers between devices with their start and end apart: 15, of which 8 were waited for; matrix products, arithmetic and copies ran while one was open for 3% of the time, Pallas kernels for 5%

profile of v4, /device:TPU:38, one launch (start us, length us, event | category | flops | bytes accessed | tf_op | source)
XLA Modules:
  0.0 224.4 jit_solution(7265307578081404603)
XLA Ops:
  7.2 0.7 all-gather.2.cloned.1.call-update
  7.9 0.9 reshape.69
  8.8 0.1 copy.22
  8.9 0.1 broadcast_in_dim.16
  9.0 0.8 broadcast_in_dim.17
  9.8 15.2 %all-to-all-start = ((bf16[16,96,128]{2,1,0:T(8,128)(2,1)}), bf16[16,96,128]{2,1,0:T(8,128)(2,1)S(1)}, u32[]{:S(2)}, u32[]{:S(2)}) async-start(bf16[16,96,128]{2,1,0:T(8,128)(2,1)} %bitcast.2), calls=%async_computation | async-start | bytes 786432 | tf_op jit(solution)/shard_map/all_to_all | solution.py:23
  25.1 2.0 collective-permute-start.1
  27.1 12.5 %collective-permute-start = (f32[8,128]{1,0:T(8,128)S(1)}, f32[8,128]{1,0:T(8,128)S(1)}, u32[]{:S(2)}, u32[]{:S(2)}) collective-permute-start(f32[8,128]{1,0:T(8,128)S(1)} %copy-done.2), channel_id=1, source_target_pairs={{0,256},{256,0},{1,257},{257,1},{2,258},{258,2},{3,259},{259,3},{4... | collective-permute-start | bytes 12296 | tf_op jit(solution)/shard_map/ppermute | solution.py:28
  39.7 5.4 %collective-permute-done.1 = s32[8,128]{1,0:T(8,128)S(1)} collective-permute-done((s32[8,128]{1,0:T(8,128)S(1)}, s32[8,128]{1,0:T(8,128)S(1)}, u32[]{:S(2)}, u32[]{:S(2)}) %collective-permute-start.1) | collective-permute-done | bytes 4128 | tf_op jit(solution)/shard_map/ppermute | solution.py:28
  45.1 10.2 %collective-permute-done = f32[8,128]{1,0:T(8,128)S(1)} collective-permute-done((f32[8,128]{1,0:T(8,128)S(1)}, f32[8,128]{1,0:T(8,128)S(1)}, u32[]{:S(2)}, u32[]{:S(2)}) %collective-permute-start) | collective-permute-done | bytes 4128 | tf_op jit(solution)/shard_map/ppermute | solution.py:28
  55.3 0.2 broadcast_in_dim.18
  55.5 21.6 %all_to_all.25 = bf16[4,16,96,128]{3,2,1,0:T(8,128)(2,1)S(1)} all-to-all(bf16[4,16,96,128]{3,2,1,0:T(8,128)(2,1)S(1)} %broadcast_in_dim.18), channel_id=1, replica_groups=mesh['z_hi'=2,'y'=4,'core'=2,'z_p'=4,'z_c'=2,'x'=4] {'x'}, dimensions={0} | all-to-all | bytes 3145728 | tf_op jit(solution)/shard_map/all_to_all | solution.py:23
  77.1 0.3 copy.12
  77.4 1.0 copy.14
  78.5 5.9 %all-to-all-start.2 = ((bf16[16,128,128]{2,1,0:T(8,128)(2,1)}), bf16[16,128,128]{2,1,0:T(8,128)(2,1)}, u32[]{:S(2)}, u32[]{:S(2)}) async-start(bf16[16,128,128]{2,1,0:T(8,128)(2,1)} %copy.14), calls=%async_computation.2 | async-start | bytes 1048576 | tf_op jit(solution)/shard_map/all_to_all | solution.py:23
  84.4 0.1 slice.77
  84.4 0.1 slice.78
  84.5 0.1 pad_maximum_fusion.4.taps_ref
  84.6 0.6 shard_map.76.w_ref
  85.2 8.7 %all-to-all-done.2.cot_ref = bf16[16,128,128]{2,1,0:T(8,128)(2,1)} async-done(((bf16[16,128,128]{2,1,0:T(8,128)(2,1)}), bf16[16,128,128]{2,1,0:T(8,128)(2,1)}, u32[]{:S(2)}, u32[]{:S(2)}) %all-to-all-start.2) | async-done | bytes 524320 | tf_op jit(solution)/shard_map/all_to_all | solution.py:23
  93.9 9.3 %shard_map.77 = (bf16[16,128,128]{2,1,0:T(8,128)(2,1)S(1)}, bf16[16,128,128]{2,1,0:T(8,128)(2,1)S(1)}, bf16[16,128,128]{2,1,0:T(8,128)(2,1)S(1)}, bf16[16,128,12...) custom-call(s32[16,1,128]{2,1,0:T(1,128)S(1)} %bitcast.42, ...), custom_call_target="tpu_custom_call" | custom-call | flops 4294967296 | bytes 8388608 | tf_op jit(solution)/shard_map/pallas_call | solution.py:209
  103.3 4.5 %collective-permute-start.3 = (bf16[8,128,128]{2,1,0:T(8,128)(2,1)S(1)}, bf16[8,128,128]{2,1,0:T(8,128)(2,1)S(1)}, u32[]{:S(2)}, u32[]{:S(2)}) collective-permute-start(bf16[8,128,128]{2,1,0:T(8,128)(2,1)S(1)} %get-tuple-element.57), channel_id=1, source_target_pairs={{0,1},{1,2},{2,3},{3,8},{8,9},{9,10},{10,11},{11,16},{16,17},{17,1... | collective-permute-start | bytes 786440 | tf_op jit(solution)/shard_map/ppermute | solution.py:261
  107.9 0.7 collective-permute-start.2
  108.6 2.0 collective-permute-start.4
  110.6 3.9 %collective-permute-start.6 = (bf16[8,128,128]{2,1,0:T(8,128)(2,1)S(1)}, bf16[8,128,128]{2,1,0:T(8,128)(2,1)S(1)}, u32[]{:S(2)}, u32[]{:S(2)}) collective-permute-start(bf16[8,128,128]{2,1,0:T(8,128)(2,1)S(1)} %get-tuple-element.53), channel_id=1, source_target_pairs={{0,3},{1,0},{2,1},{3,2},{4,7},{5,4},{6,5},{7,6},{8,11},{9,8},{10,9... | collective-permute-start | bytes 786440 | tf_op jit(solution)/shard_map/ppermute | solution.py:28
  114.5 1.9 collective-permute-start.5
  116.4 2.6 %collective-permute-done.3 = bf16[8,128,128]{2,1,0:T(8,128)(2,1)S(1)} collective-permute-done((bf16[8,128,128]{2,1,0:T(8,128)(2,1)S(1)}, bf16[8,128,128]{2,1,0:T(8,128)(2,1)S(1)}, u32[]{:S(2)}, u32[]{:S(2)}) %collective-permute-start.3) | collective-permute-done | bytes 262176 | tf_op jit(solution)/shard_map/ppermute | solution.py:261
  119.0 2.6 %collective-permute-done.4 = bf16[8,128,128]{2,1,0:T(8,128)(2,1)S(1)} collective-permute-done((bf16[8,128,128]{2,1,0:T(8,128)(2,1)S(1)}, bf16[8,128,128]{2,1,0:T(8,128)(2,1)S(1)}, u32[]{:S(2)}, u32[]{:S(2)}) %collective-permute-start.4) | collective-permute-done | bytes 262176 | tf_op jit(solution)/shard_map/ppermute | solution.py:28
  121.7 10.1 %shard_map.78 = (bf16[16,128,128]{2,1,0:T(8,128)(2,1)}, bf16[16,128,128]{2,1,0:T(8,128)(2,1)S(1)}, bf16[2,16,128]{2,1,0:T(8,128)(2,1)S(1)}) custom-call(s32[16,1,128]{2,1,0:T(1,128)S(1)} %bitcast.43, f32[8,128]{1,0:T(8,128)S(1)} %pad_maximum_fusion.4.taps_ref, bf16[16,128,128]{2,1,0:T(8,128)(2,1)S(1)} %get-tuple-element.28.q_ref, ...), custom_call_target="tpu_custom_call" | custom-call | flops 2147483648 | bytes 3145728 | tf_op jit(solution)/shard_map/pallas_call | solution.py:229
  131.9 7.7 %shard_map.79 = bf16[4,2,8,112,128]{4,3,2,1,0:T(8,128)(2,1)S(1)} custom-call(s32[1]{0:T(128)} %bitcast.12.x_ref, bf16[2048,2048]{1,0:T(8,128)(2,1)} %all-gather.2.cloned.1.call-done.tok_ref, bf16[16,128,128]{2,1,0:T(8,128)(2,1)S(1)} %get-tuple-element.33.gq_ref, f32[16,128,128]{2,1,0:T(8,128)S(1)} %get-tuple-element.34.own_ref, ...), custom_call_target="tpu_custom_call" | custom-call | flops 3221225472 | bytes 8388608 | tf_op jit(solution)/shard_map/pallas_call | solution.py:245
  139.7 4.8 %all-to-all-start.3 = ((bf16[16,128,128]{2,1,0:T(8,128)(2,1)}), bf16[16,128,128]{2,1,0:T(8,128)(2,1)S(1)}, u32[]{:S(2)}, u32[]{:S(2)}) async-start(bf16[16,128,128]{2,1,0:T(8,128)(2,1)} %get-tuple-element.41), calls=%async_computation.3 | async-start | bytes 1048576 | tf_op jit(solution)/shard_map/all_to_all | solution.py:23
  144.5 0.1 slice_bitcast_fusion.2
  144.6 8.8 %collective-permute-start.7 = (bf16[2,8,112,128]{3,2,1,0:T(8,128)(2,1)S(1)}, bf16[2,8,112,128]{3,2,1,0:T(8,128)(2,1)S(1)}, u32[]{:S(2)}, u32[]{:S(2)}) collective-permute-start(bf16[2,8,112,128]{3,2,1,0:T(8,128)(2,1)S(1)} %get-tuple-element.48), channel_id=1, source_target_pairs={{0,1},{1,2},{2,3},{3,0},{4,5},{5,6},{6,7},{7,4},{8,9},{9,10},{10,1... | collective-permute-start | bytes 1376264 | tf_op jit(solution)/shard_map/ppermute | solution.py:28
  153.4 1.9 collective-permute-start.9
  155.3 3.4 %collective-permute-start.8 = (bf16[2,8,112,128]{3,2,1,0:T(8,128)(2,1)S(1)}, bf16[2,8,112,128]{3,2,1,0:T(8,128)(2,1)S(1)}, u32[]{:S(2)}, u32[]{:S(2)}) collective-permute-start(bf16[2,8,112,128]{3,2,1,0:T(8,128)(2,1)S(1)} %get-tuple-element.50), channel_id=1, source_target_pairs={{0,2},{1,3},{2,0},{3,1},{4,6},{5,7},{6,4},{7,5},{8,10},{9,11},{10,... | collective-permute-start | bytes 1376264 | tf_op jit(solution)/shard_map/ppermute | solution.py:28
  158.7 14.6 %collective-permute-done.7 = bf16[2,8,112,128]{3,2,1,0:T(8,128)(2,1)S(1)} collective-permute-done((bf16[2,8,112,128]{3,2,1,0:T(8,128)(2,1)S(1)}, bf16[2,8,112,128]{3,2,1,0:T(8,128)(2,1)S(1)}, u32[]{:S(2)}, u32[]{:S(2)}) %collective-permute-start.7) | collective-permute-done | bytes 458784 | tf_op jit(solution)/shard_map/ppermute | solution.py:28
  173.3 5.3 %collective-permute-done.9 = bf16[2,8,112,128]{3,2,1,0:T(8,128)(2,1)S(1)} collective-permute-done((bf16[2,8,112,128]{3,2,1,0:T(8,128)(2,1)S(1)}, bf16[2,8,112,128]{3,2,1,0:T(8,128)(2,1)S(1)}, u32[]{:S(2)}, u32[]{:S(2)}) %collective-permute-start.9) | collective-permute-done | bytes 458784 | tf_op jit(solution)/shard_map/ppermute | solution.py:28
  178.6 0.2 fusion.1
  178.9 0.8 pad_maximum_fusion.2
  179.7 10.9 %all-to-all-start.4 = ((bf16[16,112,128]{2,1,0:T(8,128)(2,1)}), bf16[16,112,128]{2,1,0:T(8,128)(2,1)S(1)}, u32[]{:S(2)}, u32[]{:S(2)}) async-start(bf16[16,112,128]{2,1,0:T(8,128)(2,1)} %bitcast.20), calls=%async_computation.4 | async-start | bytes 917504 | tf_op jit(solution)/shard_map/all_to_all | solution.py:23
  190.6 0.3 copy.15
  191.0 1.0 copy.18
  192.0 23.8 %all-to-all-done.4 = bf16[16,112,128]{2,1,0:T(8,128)(2,1)S(1)} async-done(((bf16[16,112,128]{2,1,0:T(8,128)(2,1)}), bf16[16,112,128]{2,1,0:T(8,128)(2,1)S(1)}, u32[]{:S(2)}, u32[]{:S(2)}) %all-to-all-start.4) | async-done | bytes 458784 | tf_op jit(solution)/shard_map/all_to_all | solution.py:23
  215.8 0.1 convert_reduce_fusion
  215.9 0.6 slice_add_fusion.1
  216.5 0.2 reshape.78
  216.6 0.2 copy.21
  216.8 0.8 reshape.79
  (35 shorter events, 0.6 us)
Async XLA Ops:
  7.2 17.9 %copy-start = (s32[16,128]{1,0:T(8,128)S(1)}, s32[16,128]{1,0:T(8,128)}, u32[]{:S(2)}) copy-start(s32[16,128]{1,0:T(8,128)} %param.8) | copy-start | bytes 24580
  7.2 19.9 %copy-start.2 = (f32[8,128]{1,0:T(8,128)S(1)}, f32[8,128]{1,0:T(8,128)}, u32[]{:S(2)}) copy-start(f32[8,128]{1,0:T(8,128)} %param.7) | copy-start | bytes 12292
  7.2 86.8 %all-gather.2.cloned.1.call-start = ((), (), s32[]{:S(2)}) async-start(), calls=%async_computation.5 | async-start | bytes 8912896 | tf_op jit(solution)/shard_map/all_gather | solution.py:321
  9.8 45.4 %all-to-all-start = ((bf16[16,96,128]{2,1,0:T(8,128)(2,1)}), bf16[16,96,128]{2,1,0:T(8,128)(2,1)S(1)}, u32[]{:S(2)}, u32[]{:S(2)}) async-start(bf16[16,96,128]{2,1,0:T(8,128)(2,1)} %bitcast.2), calls=%async_computation | async-start | bytes 786432 | tf_op jit(solution)/shard_map/all_to_all | solution.py:23
  25.1 20.0 %collective-permute-start.1 = (s32[8,128]{1,0:T(8,128)S(1)}, s32[8,128]{1,0:T(8,128)S(1)}, u32[]{:S(2)}, u32[]{:S(2)}) collective-permute-start(s32[8,128]{1,0:T(8,128)S(1)} %constant_dynamic-slice_fusion), channel_id=1, source_target_pairs={{0,4},{4,0},{1,5},{5,1},{2,6},{6,2},{3,7},{7,3},{8,12},{12,8},{9,1... | collective-permute-start | bytes 12296 | tf_op jit(solution)/shard_map/ppermute | solution.py:28
  27.1 28.2 %collective-permute-start = (f32[8,128]{1,0:T(8,128)S(1)}, f32[8,128]{1,0:T(8,128)S(1)}, u32[]{:S(2)}, u32[]{:S(2)}) collective-permute-start(f32[8,128]{1,0:T(8,128)S(1)} %copy-done.2), channel_id=1, source_target_pairs={{0,256},{256,0},{1,257},{257,1},{2,258},{258,2},{3,259},{259,3},{4... | collective-permute-start | bytes 12296 | tf_op jit(solution)/shard_map/ppermute | solution.py:28
  55.5 21.6 %copy-start.1 = (bf16[128,2048]{1,0:T(8,128)(2,1)S(1)}, bf16[128,2048]{1,0:T(8,128)(2,1)}, u32[]{:S(2)}) copy-start(bf16[128,2048]{1,0:T(8,128)(2,1)} %param.9) | copy-start | bytes 1572868
  78.5 15.5 %all-to-all-start.2 = ((bf16[16,128,128]{2,1,0:T(8,128)(2,1)}), bf16[16,128,128]{2,1,0:T(8,128)(2,1)}, u32[]{:S(2)}, u32[]{:S(2)}) async-start(bf16[16,128,128]{2,1,0:T(8,128)(2,1)} %copy.14), calls=%async_computation.2 | async-start | bytes 1048576 | tf_op jit(solution)/shard_map/all_to_all | solution.py:23
  103.3 15.6 %collective-permute-start.3 = (bf16[8,128,128]{2,1,0:T(8,128)(2,1)S(1)}, bf16[8,128,128]{2,1,0:T(8,128)(2,1)S(1)}, u32[]{:S(2)}, u32[]{:S(2)}) collective-permute-start(bf16[8,128,128]{2,1,0:T(8,128)(2,1)S(1)} %get-tuple-element.57), channel_id=1, source_target_pairs={{0,1},{1,2},{2,3},{3,8},{8,9},{9,10},{10,11},{11,16},{16,17},{17,1... | collective-permute-start | bytes 786440 | tf_op jit(solution)/shard_map/ppermute | solution.py:261
  107.9 11.1 %collective-permute-start.2 = (bf16[1,128,128]{2,1,0:T(8,128)(2,1)S(1)}, bf16[1,128,128]{2,1,0:T(8,128)(2,1)S(1)}, u32[]{:S(2)}, u32[]{:S(2)}) collective-permute-start(bf16[1,128,128]{2,1,0:T(8,128)(2,1)S(1)} %get-tuple-element.56), channel_id=1, source_target_pairs={{27,256},{256,27},{31,260},{260,31},{59,288},{288,59},{63,292},{29... | collective-permute-start | bytes 98312 | tf_op jit(solution)/shard_map/ppermute | solution.py:267
  108.6 13.1 %collective-permute-start.4 = (bf16[8,128,128]{2,1,0:T(8,128)(2,1)S(1)}, bf16[8,128,128]{2,1,0:T(8,128)(2,1)S(1)}, u32[]{:S(2)}, u32[]{:S(2)}) collective-permute-start(bf16[8,128,128]{2,1,0:T(8,128)(2,1)S(1)} %get-tuple-element.58), channel_id=1, source_target_pairs={{0,1},{1,2},{2,3},{3,0},{4,5},{5,6},{6,7},{7,4},{8,9},{9,10},{10,1... | collective-permute-start | bytes 786440 | tf_op jit(solution)/shard_map/ppermute | solution.py:28
  110.6 21.2 %collective-permute-start.6 = (bf16[8,128,128]{2,1,0:T(8,128)(2,1)S(1)}, bf16[8,128,128]{2,1,0:T(8,128)(2,1)S(1)}, u32[]{:S(2)}, u32[]{:S(2)}) collective-permute-start(bf16[8,128,128]{2,1,0:T(8,128)(2,1)S(1)} %get-tuple-element.53), channel_id=1, source_target_pairs={{0,3},{1,0},{2,1},{3,2},{4,7},{5,4},{6,5},{7,6},{8,11},{9,8},{10,9... | collective-permute-start | bytes 786440 | tf_op jit(solution)/shard_map/ppermute | solution.py:28
  114.5 17.3 %collective-permute-start.5 = (bf16[8,128,128]{2,1,0:T(8,128)(2,1)S(1)}, bf16[8,128,128]{2,1,0:T(8,128)(2,1)S(1)}, u32[]{:S(2)}, u32[]{:S(2)}) collective-permute-start(bf16[8,128,128]{2,1,0:T(8,128)(2,1)S(1)} %get-tuple-element.54), channel_id=1, source_target_pairs={{0,27},{1,0},{2,1},{3,2},{8,3},{9,8},{10,9},{11,10},{16,11},{17,16... | collective-permute-start | bytes 786440 | tf_op jit(solution)/shard_map/ppermute | solution.py:261
  139.7 40.1 %all-to-all-start.3 = ((bf16[16,128,128]{2,1,0:T(8,128)(2,1)}), bf16[16,128,128]{2,1,0:T(8,128)(2,1)S(1)}, u32[]{:S(2)}, u32[]{:S(2)}) async-start(bf16[16,128,128]{2,1,0:T(8,128)(2,1)} %get-tuple-element.41), calls=%async_computation.3 | async-start | bytes 1048576 | tf_op jit(solution)/shard_map/all_to_all | solution.py:23
  144.6 28.7 %collective-permute-start.7 = (bf16[2,8,112,128]{3,2,1,0:T(8,128)(2,1)S(1)}, bf16[2,8,112,128]{3,2,1,0:T(8,128)(2,1)S(1)}, u32[]{:S(2)}, u32[]{:S(2)}) collective-permute-start(bf16[2,8,112,128]{3,2,1,0:T(8,128)(2,1)S(1)} %get-tuple-element.48), channel_id=1, source_target_pairs={{0,1},{1,2},{2,3},{3,0},{4,5},{5,6},{6,7},{7,4},{8,9},{9,10},{10,1... | collective-permute-start | bytes 1376264 | tf_op jit(solution)/shard_map/ppermute | solution.py:28
  153.4 25.2 %collective-permute-start.9 = (bf16[2,8,112,128]{3,2,1,0:T(8,128)(2,1)S(1)}, bf16[2,8,112,128]{3,2,1,0:T(8,128)(2,1)S(1)}, u32[]{:S(2)}, u32[]{:S(2)}) collective-permute-start(bf16[2,8,112,128]{3,2,1,0:T(8,128)(2,1)S(1)} %get-tuple-element.49), channel_id=1, source_target_pairs={{0,3},{1,0},{2,1},{3,2},{4,7},{5,4},{6,5},{7,6},{8,11},{9,8},{10,9... | collective-permute-start | bytes 1376264 | tf_op jit(solution)/shard_map/ppermute | solution.py:28
  155.3 23.3 %collective-permute-start.8 = (bf16[2,8,112,128]{3,2,1,0:T(8,128)(2,1)S(1)}, bf16[2,8,112,128]{3,2,1,0:T(8,128)(2,1)S(1)}, u32[]{:S(2)}, u32[]{:S(2)}) collective-permute-start(bf16[2,8,112,128]{3,2,1,0:T(8,128)(2,1)S(1)} %get-tuple-element.50), channel_id=1, source_target_pairs={{0,2},{1,3},{2,0},{3,1},{4,6},{5,7},{6,4},{7,5},{8,10},{9,11},{10,... | collective-permute-start | bytes 1376264 | tf_op jit(solution)/shard_map/ppermute | solution.py:28
  179.7 36.1 %all-to-all-start.4 = ((bf16[16,112,128]{2,1,0:T(8,128)(2,1)}), bf16[16,112,128]{2,1,0:T(8,128)(2,1)S(1)}, u32[]{:S(2)}, u32[]{:S(2)}) async-start(bf16[16,112,128]{2,1,0:T(8,128)(2,1)} %bitcast.20), calls=%async_computation.4 | async-start | bytes 917504 | tf_op jit(solution)/shard_map/all_to_all | solution.py:23
Sparse Core Ops, SparseCore 0:
  10.2 73.6 all-gather.1

commit v5 on v4

--- a/solution.py
+++ b/solution.py
@@ -225,7 +225,7 @@
 
 
 def front(hi, off, taps, q, cot, product, halo):
-    n, at_once = q.shape[0], 2
+    n, at_once = q.shape[0], 4
     return pl.pallas_call(
         front_kernel,
         grid=(n // at_once,),
@@ -244,10 +244,10 @@
     rows = 3 * feats // 2 + EXTRA
     return pl.pallas_call(
         weight_kernel,
-        grid=(lo // 2,),
-        in_specs=[SCALAR, pl.BlockSpec((tokens.shape[0], 2 * xs * feats), lambda i: (0, i))]
+        grid=(lo // 4,),
+        in_specs=[SCALAR, pl.BlockSpec((tokens.shape[0], 4 * xs * feats), lambda i: (0, i))]
         + [whole_spec(operand.shape) for operand in operands],
-        out_specs=pl.BlockSpec((xs, hi, 2, rows, LANES), lambda i: (0, 0, i, 0, 0)),
+        out_specs=pl.BlockSpec((xs, hi, 4, rows, LANES), lambda i: (0, 0, i, 0, 0)),
         out_shape=jax.ShapeDtypeStruct((xs, hi, lo, rows, LANES), BF),
         scratch_shapes=[pltpu.VMEM((tokens.shape[0], 3 * LANES), BF)],
         compiler_params=PARAMS,
@@ -342,18 +342,25 @@
     q, k, v, product, grad_prev, grad_own = project(off, taps, gathered, table, cot)
     halo, back = halos(product, grad_prev)
     gated, grad_q, grad_taps = front(hi, off, taps_back, q, cot, product, halo)
-    back, grad_q = lax.optimization_barrier((back, grad_q))
+    back, grad_q, gated = lax.optimization_barrier((back, grad_q, gated))
+    lower = member == 0
+    beside = turned(jnp.where(lower, gated[places:], gated[:places]), "z_c", 1)
     got = placed_back(*back)
     partial = weight_grad(x, gathered, (grad_q, grad_own, got, k, v, grad_taps), (xs, hi, lo, feats))
-    gated, partial = lax.optimization_barrier((gated, partial))
-    out = swap_blocks(gated, TOK_AX)
-    out = out.reshape(2, places, rows, hi, HALF).transpose(2, 3, 1, 0, 4).reshape(rows, -1)
+    beside, partial = lax.optimization_barrier((beside, partial))
+    mine = jnp.where(lower, gated[:places], gated[places:])
+    both = jnp.where(lower, jnp.stack([mine, beside]), jnp.stack([beside, mine]))
+    out = lax.all_gather(both.reshape(blocks * rows, LANES), ("y", "core"), axis=0, tiled=True)
+    out = out.reshape(places, 2, places, rows, LANES)
+    out = lax.dynamic_index_in_dim(out, lax.axis_index(("y", "core")), 2, keepdims=False)
+    out = out.reshape(places, 2, rows, hi, HALF).transpose(2, 3, 0, 1, 4).reshape(rows, -1)
     parts = [partial[0]] + [turned(partial[step], "x", step) for step in range(1, xs)]
     over_x = sum(part.astype(F32) for part in parts)
     taps_x = over_x[:, :, row_count : row_count + PER // 2] + over_x[:, :, row_count + PER // 2 : row_count + PER]
     taps_x = jnp.pad(split_rows(taps_x), ((0, 0), (0, 0), (0, EXTRA - PER), (0, 0)))
     over_x = jnp.concatenate([over_x[:, :, :row_count].astype(BF), taps_x], 2)
     over_z = swap_blocks(over_x.reshape(hi * lo, row_count + EXTRA, LANES), Z_AX)
+    over_z, out = lax.optimization_barrier((over_z, out))
     over_z = jnp.sum(over_z.reshape(hi * lo // 2, 2, row_count + EXTRA, LANES).astype(F32), 0)
     grad_weight = over_z[:, :row_count].reshape(2, 3, short, 2, HALF).transpose(1, 3, 2, 0, 4)
     grad_weight = grad_weight.reshape(3, feats, width)

time: 226 us -> 221 us (0.978)
  the two profiles are of different devices: /device:TPU:38 before, /device:TPU:2 now
where the time goes in v5:
time: 221 us
  starting transfers between devices  81.1 us (37%)
  waiting for transfers between devices  67.7 us (31%)
  Pallas kernels  26 us (12%)
  blocking collectives  20.8 us (9%)
  between operations  14.5 us (7%)
  local copies, waits for them, and re-layouts  7.42 us (3%)
  other arithmetic  3.03 us (1%)
    ppermute x8, starting transfers between devices, turned(): lax.ppermute(shard, axis, [(i, (i + by) % count) for i in range(count)])  40.9 us
    ppermute x8, waiting for transfers between devices, turned(): lax.ppermute(shard, axis, [(i, (i + by) % count) for i in range(count)])  34.8 us
    all_to_all x3, starting transfers between devices, swap_blocks(): return lax.all_to_all(pieces, axes, split_axis=0, concat_axis=0, tiled=True)  32.4 us
    all_to_all x3, waiting for transfers between devices, swap_blocks(): return lax.all_to_all(pieces, axes, split_axis=0, concat_axis=0, tiled=True)  32.1 us
    all_to_all x1, blocking collectives, swap_blocks(): return lax.all_to_all(pieces, axes, split_axis=0, concat_axis=0, tiled=True)  20.8 us
    pallas_call x1, Pallas kernels, project(): pl.pallas_call(project_kernel, grid=(blocks // at_once,), in_specs=[pl.Bl...  9.38 us
    pallas_call x1, Pallas kernels, front(): pl.pallas_call(front_kernel, grid=(n // at_once,), in_specs=[pl.BlockSpec...  8.45 us
    pallas_call x1, Pallas kernels, weight_grad(): pl.pallas_call(weight_kernel, grid=(lo // 4,), in_specs=[SCALAR, pl.Block...  7.53 us
  transfers between devices with their start and end apart: 16, of which 8 were waited for; matrix products, arithmetic and copies ran while one was open for 3% of the time, Pallas kernels for 8%

profile of v5, /device:TPU:2, one launch (start us, length us, event | category | flops | bytes accessed | tf_op | source)
XLA Modules:
  0.0 220.6 jit_solution(10847804676548438940)
XLA Ops:
  7.2 0.7 all-gather.3.cloned.1.call-update
  7.9 0.9 reshape.78
  8.8 0.1 copy.28
  8.9 0.1 broadcast_in_dim.16
  9.0 0.8 broadcast_in_dim.17
  9.8 15.2 %all-to-all-start = ((bf16[16,96,128]{2,1,0:T(8,128)(2,1)}), bf16[16,96,128]{2,1,0:T(8,128)(2,1)S(1)}, u32[]{:S(2)}, u32[]{:S(2)}) async-start(bf16[16,96,128]{2,1,0:T(8,128)(2,1)} %bitcast.2), calls=%async_computation | async-start | bytes 786432 | tf_op jit(solution)/shard_map/all_to_all | solution.py:23
  25.1 3.8 %collective-permute-start.1 = (s32[8,128]{1,0:T(8,128)S(1)}, s32[8,128]{1,0:T(8,128)S(1)}, u32[]{:S(2)}, u32[]{:S(2)}) collective-permute-start(s32[8,128]{1,0:T(8,128)S(1)} %constant_dynamic-slice_fusion.1), channel_id=1, source_target_pairs={{0,4},{4,0},{1,5},{5,1},{2,6},{6,2},{3,7},{7,3},{8,12},{12,8},{9,1... | collective-permute-start | bytes 12296 | tf_op jit(solution)/shard_map/ppermute | solution.py:28
  28.9 11.2 %collective-permute-start = (f32[8,128]{1,0:T(8,128)S(1)}, f32[8,128]{1,0:T(8,128)S(1)}, u32[]{:S(2)}, u32[]{:S(2)}) collective-permute-start(f32[8,128]{1,0:T(8,128)S(1)} %copy-done.2), channel_id=1, source_target_pairs={{0,256},{256,0},{1,257},{257,1},{2,258},{258,2},{3,259},{259,3},{4... | collective-permute-start | bytes 12296 | tf_op jit(solution)/shard_map/ppermute | solution.py:28
  40.1 7.7 %collective-permute-done.1 = s32[8,128]{1,0:T(8,128)S(1)} collective-permute-done((s32[8,128]{1,0:T(8,128)S(1)}, s32[8,128]{1,0:T(8,128)S(1)}, u32[]{:S(2)}, u32[]{:S(2)}) %collective-permute-start.1) | collective-permute-done | bytes 4128 | tf_op jit(solution)/shard_map/ppermute | solution.py:28
  47.8 8.3 %collective-permute-done = f32[8,128]{1,0:T(8,128)S(1)} collective-permute-done((f32[8,128]{1,0:T(8,128)S(1)}, f32[8,128]{1,0:T(8,128)S(1)}, u32[]{:S(2)}, u32[]{:S(2)}) %collective-permute-start) | collective-permute-done | bytes 4128 | tf_op jit(solution)/shard_map/ppermute | solution.py:28
  56.1 0.2 broadcast_in_dim.18
  56.4 20.8 %all_to_all.20 = bf16[4,16,96,128]{3,2,1,0:T(8,128)(2,1)S(1)} all-to-all(bf16[4,16,96,128]{3,2,1,0:T(8,128)(2,1)S(1)} %broadcast_in_dim.18), channel_id=1, replica_groups=mesh['z_hi'=2,'y'=4,'core'=2,'z_p'=4,'z_c'=2,'x'=4] {'x'}, dimensions={0} | all-to-all | bytes 3145728 | tf_op jit(solution)/shard_map/all_to_all | solution.py:23
  77.2 0.3 copy.18
  77.5 1.0 copy.20
  78.6 6.5 %all-to-all-start.2 = ((bf16[16,128,128]{2,1,0:T(8,128)(2,1)}), bf16[16,128,128]{2,1,0:T(8,128)(2,1)}, u32[]{:S(2)}, u32[]{:S(2)}) async-start(bf16[16,128,128]{2,1,0:T(8,128)(2,1)} %copy.20), calls=%async_computation.2 | async-start | bytes 1048576 | tf_op jit(solution)/shard_map/all_to_all | solution.py:23
  85.2 0.1 slice.93
  85.3 0.1 pad_maximum_fusion.4.taps_ref
  85.4 0.6 shard_map.76.w_ref
  86.0 9.9 %all-to-all-done.2.cot_ref = bf16[16,128,128]{2,1,0:T(8,128)(2,1)} async-done(((bf16[16,128,128]{2,1,0:T(8,128)(2,1)}), bf16[16,128,128]{2,1,0:T(8,128)(2,1)}, u32[]{:S(2)}, u32[]{:S(2)}) %all-to-all-start.2) | async-done | bytes 524320 | tf_op jit(solution)/shard_map/all_to_all | solution.py:23
  96.0 9.4 %shard_map.77 = (bf16[16,128,128]{2,1,0:T(8,128)(2,1)S(1)}, bf16[16,128,128]{2,1,0:T(8,128)(2,1)S(1)}, bf16[16,128,128]{2,1,0:T(8,128)(2,1)S(1)}, bf16[16,128,12...) custom-call(s32[16,1,128]{2,1,0:T(1,128)S(1)} %bitcast.47, ...), custom_call_target="tpu_custom_call" | custom-call | flops 4294967296 | bytes 8388608 | tf_op jit(solution)/shard_map/pallas_call | solution.py:209
  105.4 2.1 collective-permute-start.5
  107.6 0.7 collective-permute-start.4
  108.3 3.7 %collective-permute-start.6 = (bf16[8,128,128]{2,1,0:T(8,128)(2,1)S(1)}, bf16[8,128,128]{2,1,0:T(8,128)(2,1)S(1)}, u32[]{:S(2)}, u32[]{:S(2)}) collective-permute-start(bf16[8,128,128]{2,1,0:T(8,128)(2,1)S(1)} %get-tuple-element.64), channel_id=1, source_target_pairs={{0,1},{1,2},{2,3},{3,0},{4,5},{5,6},{6,7},{7,4},{8,9},{9,10},{10,1... | collective-permute-start | bytes 786440 | tf_op jit(solution)/shard_map/ppermute | solution.py:28
  112.0 2.1 collective-permute-start.3
  114.2 4.9 %collective-permute-start.2 = (bf16[8,128,128]{2,1,0:T(8,128)(2,1)S(1)}, bf16[8,128,128]{2,1,0:T(8,128)(2,1)S(1)}, u32[]{:S(2)}, u32[]{:S(2)}) collective-permute-start(bf16[8,128,128]{2,1,0:T(8,128)(2,1)S(1)} %get-tuple-element.69), channel_id=1, source_target_pairs={{0,27},{1,0},{2,1},{3,2},{8,3},{9,8},{10,9},{11,10},{16,11},{17,16... | collective-permute-start | bytes 786440 | tf_op jit(solution)/shard_map/ppermute | solution.py:261
  119.2 1.3 collective-permute-done.6
  120.5 8.5 %shard_map.78 = (bf16[16,128,128]{2,1,0:T(8,128)(2,1)S(1)}, bf16[16,128,128]{2,1,0:T(8,128)(2,1)S(1)}, bf16[2,16,128]{2,1,0:T(8,128)(2,1)S(1)}) custom-call(s32[16,1,128]{2,1,0:T(1,128)S(1)} %bitcast.48, f32[8,128]{1,0:T(8,128)S(1)} %pad_maximum_fusion.4.taps_ref, bf16[16,128,128]{2,1,0:T(8,128)(2,1)S(1)} %get-tuple-element.33.q_ref, ...), custom_call_target="tpu_custom_call" | custom-call | flops 2147483648 | bytes 3145728 | tf_op jit(solution)/shard_map/pallas_call | solution.py:229
  129.1 2.9 %collective-permute-start.7 = (bf16[8,128,128]{2,1,0:T(8,128)(2,1)S(1)}, bf16[8,128,128]{2,1,0:T(8,128)(2,1)S(1)}, u32[]{:S(2)}, u32[]{:S(2)}) collective-permute-start(bf16[8,128,128]{2,1,0:T(8,128)(2,1)S(1)} %get-tuple-element.61), channel_id=1, source_target_pairs={{0,4},{4,0},{1,5},{5,1},{2,6},{6,2},{3,7},{7,3},{8,12},{12,8},{9,1... | collective-permute-start | bytes 786440 | tf_op jit(solution)/shard_map/ppermute | solution.py:28
  132.1 7.5 %shard_map.79 = bf16[4,2,8,112,128]{4,3,2,1,0:T(8,128)(2,1)S(1)} custom-call(s32[1]{0:T(128)} %bitcast.12.x_ref, bf16[2048,2048]{1,0:T(8,128)(2,1)} %all-gather.3.cloned.1.call-done.tok_ref, bf16[16,128,128]{2,1,0:T(8,128)(2,1)S(1)} %get-tuple-element.37.gq_ref, f32[16,128,128]{2,1,0:T(8,128)S(1)} %get-tuple-element.38.own_ref, ...), custom_call_target="tpu_custom_call" | custom-call | flops 3221225472 | bytes 8388608 | tf_op jit(solution)/shard_map/pallas_call | solution.py:245
  139.7 0.9 maximum_select_fusion
  140.6 0.1 slice_bitcast_fusion.2
  140.7 2.2 %collective-permute-start.8 = (bf16[2,8,112,128]{3,2,1,0:T(8,128)(2,1)S(1)}, bf16[2,8,112,128]{3,2,1,0:T(8,128)(2,1)S(1)}, u32[]{:S(2)}, u32[]{:S(2)}) collective-permute-start(bf16[2,8,112,128]{3,2,1,0:T(8,128)(2,1)S(1)} %get-tuple-element.57), channel_id=1, source_target_pairs={{0,1},{1,2},{2,3},{3,0},{4,5},{5,6},{6,7},{7,4},{8,9},{9,10},{10,1... | collective-permute-start | bytes 1376264 | tf_op jit(solution)/shard_map/ppermute | solution.py:28
  142.9 10.9 %collective-permute-start.10 = (bf16[2,8,112,128]{3,2,1,0:T(8,128)(2,1)S(1)}, bf16[2,8,112,128]{3,2,1,0:T(8,128)(2,1)S(1)}, u32[]{:S(2)}, u32[]{:S(2)}) collective-permute-start(bf16[2,8,112,128]{3,2,1,0:T(8,128)(2,1)S(1)} %get-tuple-element.58), channel_id=1, source_target_pairs={{0,3},{1,0},{2,1},{3,2},{4,7},{5,4},{6,5},{7,6},{8,11},{9,8},{10,9... | collective-permute-start | bytes 1376264 | tf_op jit(solution)/shard_map/ppermute | solution.py:28
  153.8 4.0 %collective-permute-start.9 = (bf16[2,8,112,128]{3,2,1,0:T(8,128)(2,1)S(1)}, bf16[2,8,112,128]{3,2,1,0:T(8,128)(2,1)S(1)}, u32[]{:S(2)}, u32[]{:S(2)}) collective-permute-start(bf16[2,8,112,128]{3,2,1,0:T(8,128)(2,1)S(1)} %get-tuple-element.59), channel_id=1, source_target_pairs={{0,2},{1,3},{2,0},{3,1},{4,6},{5,7},{6,4},{7,5},{8,10},{9,11},{10,... | collective-permute-start | bytes 1376264 | tf_op jit(solution)/shard_map/ppermute | solution.py:28
  157.8 5.5 %collective-permute-done.8 = bf16[2,8,112,128]{3,2,1,0:T(8,128)(2,1)S(1)} collective-permute-done((bf16[2,8,112,128]{3,2,1,0:T(8,128)(2,1)S(1)}, bf16[2,8,112,128]{3,2,1,0:T(8,128)(2,1)S(1)}, u32[]{:S(2)}, u32[]{:S(2)}) %collective-permute-start.8) | collective-permute-done | bytes 458784 | tf_op jit(solution)/shard_map/ppermute | solution.py:28
  163.3 1.5 collective-permute-done.10
  164.8 10.5 %collective-permute-done.9 = bf16[2,8,112,128]{3,2,1,0:T(8,128)(2,1)S(1)} collective-permute-done((bf16[2,8,112,128]{3,2,1,0:T(8,128)(2,1)S(1)}, bf16[2,8,112,128]{3,2,1,0:T(8,128)(2,1)S(1)}, u32[]{:S(2)}, u32[]{:S(2)}) %collective-permute-start.9) | collective-permute-done | bytes 458784 | tf_op jit(solution)/shard_map/ppermute | solution.py:28
  175.3 0.2 fusion.1
  175.7 0.8 pad_maximum_fusion.2
  176.5 10.7 %all-to-all-start.3 = ((bf16[16,112,128]{2,1,0:T(8,128)(2,1)}), bf16[16,112,128]{2,1,0:T(8,128)(2,1)S(1)}, u32[]{:S(2)}, u32[]{:S(2)}) async-start(bf16[16,112,128]{2,1,0:T(8,128)(2,1)} %bitcast.17), calls=%async_computation.3 | async-start | bytes 917504 | tf_op jit(solution)/shard_map/all_to_all | solution.py:23
  187.3 1.1 constant_dynamic-slice_fusion
  188.4 0.3 copy.21
  188.7 22.2 %all-to-all-done.3 = bf16[16,112,128]{2,1,0:T(8,128)(2,1)S(1)} async-done(((bf16[16,112,128]{2,1,0:T(8,128)(2,1)}), bf16[16,112,128]{2,1,0:T(8,128)(2,1)S(1)}, u32[]{:S(2)}, u32[]{:S(2)}) %all-to-all-start.3) | async-done | bytes 458784 | tf_op jit(solution)/shard_map/all_to_all | solution.py:23
  211.0 0.6 slice_add_fusion.1
  211.6 1.0 copy.24
  212.6 0.2 reshape.88
  212.8 0.2 copy.27
  212.9 0.8 reshape.89
  (41 shorter events, 0.9 us)
Async XLA Ops:
  7.2 17.9 %copy-start = (s32[16,128]{1,0:T(8,128)S(1)}, s32[16,128]{1,0:T(8,128)}, u32[]{:S(2)}) copy-start(s32[16,128]{1,0:T(8,128)} %param.8) | copy-start | bytes 24580
  7.2 21.7 %copy-start.2 = (f32[8,128]{1,0:T(8,128)S(1)}, f32[8,128]{1,0:T(8,128)}, u32[]{:S(2)}) copy-start(f32[8,128]{1,0:T(8,128)} %param.7) | copy-start | bytes 12292
  7.2 88.8 %all-gather.3.cloned.1.call-start = ((), (), s32[]{:S(2)}) async-start(), calls=%async_computation.4 | async-start | bytes 8912896 | tf_op jit(solution)/shard_map/all_gather | solution.py:321
  9.8 46.3 %all-to-all-start = ((bf16[16,96,128]{2,1,0:T(8,128)(2,1)}), bf16[16,96,128]{2,1,0:T(8,128)(2,1)S(1)}, u32[]{:S(2)}, u32[]{:S(2)}) async-start(bf16[16,96,128]{2,1,0:T(8,128)(2,1)} %bitcast.2), calls=%async_computation | async-start | bytes 786432 | tf_op jit(solution)/shard_map/all_to_all | solution.py:23
  25.1 22.7 %collective-permute-start.1 = (s32[8,128]{1,0:T(8,128)S(1)}, s32[8,128]{1,0:T(8,128)S(1)}, u32[]{:S(2)}, u32[]{:S(2)}) collective-permute-start(s32[8,128]{1,0:T(8,128)S(1)} %constant_dynamic-slice_fusion.1), channel_id=1, source_target_pairs={{0,4},{4,0},{1,5},{5,1},{2,6},{6,2},{3,7},{7,3},{8,12},{12,8},{9,1... | collective-permute-start | bytes 12296 | tf_op jit(solution)/shard_map/ppermute | solution.py:28
  28.9 27.2 %collective-permute-start = (f32[8,128]{1,0:T(8,128)S(1)}, f32[8,128]{1,0:T(8,128)S(1)}, u32[]{:S(2)}, u32[]{:S(2)}) collective-permute-start(f32[8,128]{1,0:T(8,128)S(1)} %copy-done.2), channel_id=1, source_target_pairs={{0,256},{256,0},{1,257},{257,1},{2,258},{258,2},{3,259},{259,3},{4... | collective-permute-start | bytes 12296 | tf_op jit(solution)/shard_map/ppermute | solution.py:28
  56.4 20.9 %copy-start.1 = (bf16[128,2048]{1,0:T(8,128)(2,1)S(1)}, bf16[128,2048]{1,0:T(8,128)(2,1)}, u32[]{:S(2)}) copy-start(bf16[128,2048]{1,0:T(8,128)(2,1)} %param.9) | copy-start | bytes 1572868
  78.6 17.4 %all-to-all-start.2 = ((bf16[16,128,128]{2,1,0:T(8,128)(2,1)}), bf16[16,128,128]{2,1,0:T(8,128)(2,1)}, u32[]{:S(2)}, u32[]{:S(2)}) async-start(bf16[16,128,128]{2,1,0:T(8,128)(2,1)} %copy.20), calls=%async_computation.2 | async-start | bytes 1048576 | tf_op jit(solution)/shard_map/all_to_all | solution.py:23
  85.1 102.2 %all-gather.5.cloned.1.call-start = ((), (), s32[]{:S(2)}) async-start(), calls=%async_computation.5 | async-start | bytes 4718592 | tf_op jit(solution)/shard_map/all_gather | solution.py:353
  105.4 13.7 %collective-permute-start.5 = (bf16[8,128,128]{2,1,0:T(8,128)(2,1)S(1)}, bf16[8,128,128]{2,1,0:T(8,128)(2,1)S(1)}, u32[]{:S(2)}, u32[]{:S(2)}) collective-permute-start(bf16[8,128,128]{2,1,0:T(8,128)(2,1)S(1)} %get-tuple-element.65), channel_id=1, source_target_pairs={{0,1},{1,2},{2,3},{3,8},{8,9},{9,10},{10,11},{11,16},{16,17},{17,1... | collective-permute-start | bytes 786440 | tf_op jit(solution)/shard_map/ppermute | solution.py:261
  107.6 11.6 %collective-permute-start.4 = (bf16[1,128,128]{2,1,0:T(8,128)(2,1)S(1)}, bf16[1,128,128]{2,1,0:T(8,128)(2,1)S(1)}, u32[]{:S(2)}, u32[]{:S(2)}) collective-permute-start(bf16[1,128,128]{2,1,0:T(8,128)(2,1)S(1)} %get-tuple-element.66), channel_id=1, source_target_pairs={{27,256},{256,27},{31,260},{260,31},{59,288},{288,59},{63,292},{29... | collective-permute-start | bytes 98312 | tf_op jit(solution)/shard_map/ppermute | solution.py:267
  108.3 12.2 %collective-permute-start.6 = (bf16[8,128,128]{2,1,0:T(8,128)(2,1)S(1)}, bf16[8,128,128]{2,1,0:T(8,128)(2,1)S(1)}, u32[]{:S(2)}, u32[]{:S(2)}) collective-permute-start(bf16[8,128,128]{2,1,0:T(8,128)(2,1)S(1)} %get-tuple-element.64), channel_id=1, source_target_pairs={{0,1},{1,2},{2,3},{3,0},{4,5},{5,6},{6,7},{7,4},{8,9},{9,10},{10,1... | collective-permute-start | bytes 786440 | tf_op jit(solution)/shard_map/ppermute | solution.py:28
  112.0 16.9 %collective-permute-start.3 = (bf16[8,128,128]{2,1,0:T(8,128)(2,1)S(1)}, bf16[8,128,128]{2,1,0:T(8,128)(2,1)S(1)}, u32[]{:S(2)}, u32[]{:S(2)}) collective-permute-start(bf16[8,128,128]{2,1,0:T(8,128)(2,1)S(1)} %get-tuple-element.68), channel_id=1, source_target_pairs={{0,3},{1,0},{2,1},{3,2},{4,7},{5,4},{6,5},{7,6},{8,11},{9,8},{10,9... | collective-permute-start | bytes 786440 | tf_op jit(solution)/shard_map/ppermute | solution.py:28
  114.2 14.8 %collective-permute-start.2 = (bf16[8,128,128]{2,1,0:T(8,128)(2,1)S(1)}, bf16[8,128,128]{2,1,0:T(8,128)(2,1)S(1)}, u32[]{:S(2)}, u32[]{:S(2)}) collective-permute-start(bf16[8,128,128]{2,1,0:T(8,128)(2,1)S(1)} %get-tuple-element.69), channel_id=1, source_target_pairs={{0,27},{1,0},{2,1},{3,2},{8,3},{9,8},{10,9},{11,10},{16,11},{17,16... | collective-permute-start | bytes 786440 | tf_op jit(solution)/shard_map/ppermute | solution.py:261
  129.1 10.6 %collective-permute-start.7 = (bf16[8,128,128]{2,1,0:T(8,128)(2,1)S(1)}, bf16[8,128,128]{2,1,0:T(8,128)(2,1)S(1)}, u32[]{:S(2)}, u32[]{:S(2)}) collective-permute-start(bf16[8,128,128]{2,1,0:T(8,128)(2,1)S(1)} %get-tuple-element.61), channel_id=1, source_target_pairs={{0,4},{4,0},{1,5},{5,1},{2,6},{6,2},{3,7},{7,3},{8,12},{12,8},{9,1... | collective-permute-start | bytes 786440 | tf_op jit(solution)/shard_map/ppermute | solution.py:28
  140.7 22.6 %collective-permute-start.8 = (bf16[2,8,112,128]{3,2,1,0:T(8,128)(2,1)S(1)}, bf16[2,8,112,128]{3,2,1,0:T(8,128)(2,1)S(1)}, u32[]{:S(2)}, u32[]{:S(2)}) collective-permute-start(bf16[2,8,112,128]{3,2,1,0:T(8,128)(2,1)S(1)} %get-tuple-element.57), channel_id=1, source_target_pairs={{0,1},{1,2},{2,3},{3,0},{4,5},{5,6},{6,7},{7,4},{8,9},{9,10},{10,1... | collective-permute-start | bytes 1376264 | tf_op jit(solution)/shard_map/ppermute | solution.py:28
  142.9 21.9 %collective-permute-start.10 = (bf16[2,8,112,128]{3,2,1,0:T(8,128)(2,1)S(1)}, bf16[2,8,112,128]{3,2,1,0:T(8,128)(2,1)S(1)}, u32[]{:S(2)}, u32[]{:S(2)}) collective-permute-start(bf16[2,8,112,128]{3,2,1,0:T(8,128)(2,1)S(1)} %get-tuple-element.58), channel_id=1, source_target_pairs={{0,3},{1,0},{2,1},{3,2},{4,7},{5,4},{6,5},{7,6},{8,11},{9,8},{10,9... | collective-permute-start | bytes 1376264 | tf_op jit(solution)/shard_map/ppermute | solution.py:28
  153.8 21.5 %collective-permute-start.9 = (bf16[2,8,112,128]{3,2,1,0:T(8,128)(2,1)S(1)}, bf16[2,8,112,128]{3,2,1,0:T(8,128)(2,1)S(1)}, u32[]{:S(2)}, u32[]{:S(2)}) collective-permute-start(bf16[2,8,112,128]{3,2,1,0:T(8,128)(2,1)S(1)} %get-tuple-element.59), channel_id=1, source_target_pairs={{0,2},{1,3},{2,0},{3,1},{4,6},{5,7},{6,4},{7,5},{8,10},{9,11},{10,... | collective-permute-start | bytes 1376264 | tf_op jit(solution)/shard_map/ppermute | solution.py:28
  176.5 34.4 %all-to-all-start.3 = ((bf16[16,112,128]{2,1,0:T(8,128)(2,1)}), bf16[16,112,128]{2,1,0:T(8,128)(2,1)S(1)}, u32[]{:S(2)}, u32[]{:S(2)}) async-start(bf16[16,112,128]{2,1,0:T(8,128)(2,1)} %bitcast.17), calls=%async_computation.3 | async-start | bytes 917504 | tf_op jit(solution)/shard_map/all_to_all | solution.py:23
Sparse Core Ops, SparseCore 0:
  10.2 75.4 all-gather.2
  140.7 45.7 all-gather.4

commit v6 on v5

--- a/solution.py
+++ b/solution.py
@@ -53,16 +53,19 @@
         table_ref[g] = pltpu.roll(rows, 0, 1, stride=1, stride_axis=0).astype(BF)
 
 
-def unpack_kernel(w_ref, table):
-    xs, _, lo, parts, short, _ = w_ref.shape
-    for x in range(xs):
+def unpack_kernel(x_ref, *refs):
+    w_refs, table = refs[:-1], refs[-1]
+    _, lo, parts, short, _ = w_refs[0].shape
+    xs = len(w_refs)
+    for step, w_ref in enumerate(w_refs):
+        x = lax.rem(x_ref[0] - step + xs, xs)
         for l in range(lo):
-            at = (l * xs + x) * (2 * short)
+            at = pl.multiple_of((l * xs + x) * (2 * short), 2 * short)
             for p in range(parts):
                 cols = slice(p * LANES, (p + 1) * LANES)
-                top, low = lane_halves(w_ref[x, 0, l, p].astype(F32), w_ref[x, 1, l, p].astype(F32))
-                table[at : at + short, cols] = top.astype(BF)
-                table[at + short : at + 2 * short, cols] = low.astype(BF)
+                top, low = lane_halves(w_ref[0, l, p].astype(F32), w_ref[1, l, p].astype(F32))
+                table[pl.ds(at, short), cols] = top.astype(BF)
+                table[pl.ds(at + short, short), cols] = low.astype(BF)
 
 
 def project_kernel(off_ref, taps_ref, tok_ref, w_ref, cot_ref, q_ref, k_ref, v_ref, prod_ref, prev_ref, own_ref, table):
@@ -147,6 +150,15 @@
             df_ref[h] = rows.astype(BF)
 
 
+def rows_kernel(_, in_ref, out_ref):
+    places = in_ref.shape[0]
+    for i in range(places):
+        sides = lane_halves(in_ref[i, 0, 0].astype(F32), in_ref[i, 1, 0].astype(F32))
+        for h, side in enumerate(sides):
+            at = (h * places + i) * LANES
+            out_ref[:, at : at + LANES] = side.astype(BF)
+
+
 def weight_kernel(x_ref, tok_ref, gq_ref, own_ref, got_ref, k_ref, v_ref, taps_ref, out_ref, grads):
     blocks, rows, _ = own_ref.shape
     xs, hi = out_ref.shape[:2]
@@ -190,16 +202,16 @@
     return pl.CostEstimate(flops=flops, bytes_accessed=moved, transcendentals=0)
 
 
-def unpack(pieces):
-    xs, hi, lo, parts, short, _ = pieces.shape
+def unpack(x, pieces):
+    hi, lo, parts, short, _ = pieces[0].shape
     return pl.pallas_call(
         unpack_kernel,
-        in_specs=[pl.BlockSpec(memory_space=pltpu.VMEM)],
+        in_specs=[SCALAR] + [pl.BlockSpec(memory_space=pltpu.VMEM)] * len(pieces),
         out_specs=pl.BlockSpec(memory_space=pltpu.VMEM),
-        out_shape=jax.ShapeDtypeStruct((lo * xs * 2 * short, parts * LANES), BF),
+        out_shape=jax.ShapeDtypeStruct((lo * len(pieces) * 2 * short, parts * LANES), BF),
         compiler_params=pltpu.CompilerParams(vmem_limit_bytes=48 << 20),
-        cost_estimate=cost(2 * pieces.size, 4 * pieces.size),
-    )(pieces)
+        cost_estimate=cost(pieces[0].size * 8, pieces[0].size * 16),
+    )(x, *pieces)
 
 
 def project(off, taps, tokens, table, cot):
@@ -239,6 +251,22 @@
     )(off, taps, q, cot, product, halo)
 
 
+def output_rows(mine, gathered):
+    places, two, _, rows, _ = gathered.shape
+    return pl.pallas_call(
+        rows_kernel,
+        grid_spec=pltpu.PrefetchScalarGridSpec(
+            num_scalar_prefetch=1,
+            grid=(1,),
+            in_specs=[pl.BlockSpec((places, two, 1, rows, LANES), lambda i, mine: (0, 0, mine[0], 0, 0))],
+            out_specs=pl.BlockSpec((rows, places * two * LANES), lambda i, mine: (0, 0)),
+        ),
+        out_shape=jax.ShapeDtypeStruct((rows, places * two * LANES), BF),
+        compiler_params=PARAMS,
+        cost_estimate=cost(rows * places * two * LANES, 4 * rows * places * two * LANES),
+    )(mine, gathered)
+
+
 def weight_grad(x, tokens, operands, dims):
     xs, hi, lo, feats = dims
     rows = 3 * feats // 2 + EXTRA
@@ -326,11 +354,12 @@
     off = lax.dynamic_slice_in_dim(doc_offset, lax.axis_index("z_hi") * places, places, 0)
     off_other = turned(off, "z_c", 1)
     by_z, other, off_other = lax.optimization_barrier((by_z, other, off_other))
-    pieces = swap_blocks(jnp.broadcast_to(by_z[None], (xs,) + by_z.shape), "x")
-    cotangent, pieces = lax.optimization_barrier((cotangent, pieces))
+    cotangent, by_z = lax.optimization_barrier((cotangent, by_z))
+    pieces = [by_z] + [turned(by_z, "x", step) for step in range(1, xs)]
+    pieces = [piece.reshape(hi, lo, 3, short, LANES) for piece in pieces]
     cot = cotangent.reshape(rows, hi, places, 2, HALF).transpose(3, 2, 0, 1, 4).reshape(blocks, rows, LANES)
     cot = swap_blocks(cot, TOK_AX)
-    table = unpack(pieces.reshape(xs, hi, lo, 3, short, LANES))
+    table = unpack(x, pieces)
 
     upper = lax.axis_index("z_hi") == 0
     taps = jnp.where(upper, jnp.stack([filters, other]), jnp.stack([other, filters]))
@@ -352,8 +381,7 @@
     both = jnp.where(lower, jnp.stack([mine, beside]), jnp.stack([beside, mine]))
     out = lax.all_gather(both.reshape(blocks * rows, LANES), ("y", "core"), axis=0, tiled=True)
     out = out.reshape(places, 2, places, rows, LANES)
-    out = lax.dynamic_index_in_dim(out, lax.axis_index(("y", "core")), 2, keepdims=False)
-    out = out.reshape(places, 2, rows, hi, HALF).transpose(2, 3, 0, 1, 4).reshape(rows, -1)
+    out = output_rows(lax.axis_index(("y", "core")).astype(jnp.int32)[None], out)
     parts = [partial[0]] + [turned(partial[step], "x", step) for step in range(1, xs)]
     over_x = sum(part.astype(F32) for part in parts)
     taps_x = over_x[:, :, row_count : row_count + PER // 2] + over_x[:, :, row_count + PER // 2 : row_count + PER]

time: 221 us -> 221 us (level)
  the two profiles are of different devices: /device:TPU:2 before, /device:TPU:90 now
where the time goes in v6:
time: 221 us; the launch traced here: 220 us
  starting transfers between devices  92.2 us (42%)
  waiting for transfers between devices  75.2 us (34%)
  Pallas kernels  26.2 us (12%)
  between operations  14.5 us (7%)
  local copies, waits for them, and re-layouts  8.7 us (4%)
  other arithmetic  3.06 us (1%)
    ppermute x11, waiting for transfers between devices, turned(): lax.ppermute(shard, axis, [(i, (i + by) % count) for i in range(count)])  48.6 us
    ppermute x11, starting transfers between devices, turned(): lax.ppermute(shard, axis, [(i, (i + by) % count) for i in range(count)])  48.3 us
    all_to_all x3, starting transfers between devices, swap_blocks(): return lax.all_to_all(pieces, axes, split_axis=0, concat_axis=0, tiled=True)  34.7 us
    all_to_all x3, waiting for transfers between devices, swap_blocks(): return lax.all_to_all(pieces, axes, split_axis=0, concat_axis=0, tiled=True)  21.7 us
    pallas_call x1, Pallas kernels, project(): pl.pallas_call(project_kernel, grid=(blocks // at_once,), in_specs=[pl.Bl...  9.31 us
    ppermute x2, starting transfers between devices, seq_ring(): return lax.ppermute(shard, SEQ_AX, pairs)  8.5 us
    pallas_call x1, Pallas kernels, front(): pl.pallas_call(front_kernel, grid=(n // at_once,), in_specs=[pl.BlockSpec...  7.59 us
    pallas_call x1, Pallas kernels, weight_grad(): pl.pallas_call(weight_kernel, grid=(lo // 4,), in_specs=[SCALAR, pl.Block...  7.55 us
  transfers between devices with their start and end apart: 19, of which 12 were waited for; matrix products, arithmetic and copies ran while one was open for 2% of the time, Pallas kernels for 8%

profile of v6, /device:TPU:90, one launch (start us, length us, event | category | flops | bytes accessed | tf_op | source)
XLA Modules:
  0.0 219.8 jit_solution(14962162930158788544)
XLA Ops:
  7.2 0.7 all-gather.3.cloned.1.call-update
  7.9 0.9 reshape.79
  9.1 0.8 broadcast_in_dim.14
  9.8 14.8 %all-to-all-start = ((bf16[16,96,128]{2,1,0:T(8,128)(2,1)}), bf16[16,96,128]{2,1,0:T(8,128)(2,1)S(1)}, u32[]{:S(2)}, u32[]{:S(2)}) async-start(bf16[16,96,128]{2,1,0:T(8,128)(2,1)} %bitcast.2), calls=%async_computation | async-start | bytes 786432 | tf_op jit(solution)/shard_map/all_to_all | solution.py:23
  24.6 3.4 %collective-permute-start.1 = (s32[8,128]{1,0:T(8,128)S(1)}, s32[8,128]{1,0:T(8,128)S(1)}, u32[]{:S(2)}, u32[]{:S(2)}) collective-permute-start(s32[8,128]{1,0:T(8,128)S(1)} %constant_dynamic-slice_fusion), channel_id=1, source_target_pairs={{0,4},{4,0},{1,5},{5,1},{2,6},{6,2},{3,7},{7,3},{8,12},{12,8},{9,1... | collective-permute-start | bytes 12296 | tf_op jit(solution)/shard_map/ppermute | solution.py:28
  28.0 9.4 %collective-permute-start = (f32[8,128]{1,0:T(8,128)S(1)}, f32[8,128]{1,0:T(8,128)S(1)}, u32[]{:S(2)}, u32[]{:S(2)}) collective-permute-start(f32[8,128]{1,0:T(8,128)S(1)} %copy-done.5), channel_id=1, source_target_pairs={{0,256},{256,0},{1,257},{257,1},{2,258},{258,2},{3,259},{259,3},{4... | collective-permute-start | bytes 12296 | tf_op jit(solution)/shard_map/ppermute | solution.py:28
  37.4 7.9 %collective-permute-done.1 = s32[8,128]{1,0:T(8,128)S(1)} collective-permute-done((s32[8,128]{1,0:T(8,128)S(1)}, s32[8,128]{1,0:T(8,128)S(1)}, u32[]{:S(2)}, u32[]{:S(2)}) %collective-permute-start.1) | collective-permute-done | bytes 4128 | tf_op jit(solution)/shard_map/ppermute | solution.py:28
  45.3 8.0 %collective-permute-done = f32[8,128]{1,0:T(8,128)S(1)} collective-permute-done((f32[8,128]{1,0:T(8,128)S(1)}, f32[8,128]{1,0:T(8,128)S(1)}, u32[]{:S(2)}, u32[]{:S(2)}) %collective-permute-start) | collective-permute-done | bytes 4128 | tf_op jit(solution)/shard_map/ppermute | solution.py:28
  53.3 0.3 copy.11
  53.7 1.0 copy.13
  54.7 4.6 %all-to-all-start.1 = ((bf16[16,128,128]{2,1,0:T(8,128)(2,1)}), bf16[16,128,128]{2,1,0:T(8,128)(2,1)S(1)}, u32[]{:S(2)}, u32[]{:S(2)}) async-start(bf16[16,128,128]{2,1,0:T(8,128)(2,1)} %copy.13), calls=%async_computation.1 | async-start | bytes 1048576 | tf_op jit(solution)/shard_map/all_to_all | solution.py:23
  59.3 2.4 %collective-permute-start.4 = (bf16[16,96,128]{2,1,0:T(8,128)(2,1)S(1)}, bf16[16,96,128]{2,1,0:T(8,128)(2,1)S(1)}, u32[]{:S(2)}, u32[]{:S(2)}) collective-permute-start(bf16[16,96,128]{2,1,0:T(8,128)(2,1)S(1)} %all-to-all-done), channel_id=1, source_target_pairs={{0,3},{1,0},{2,1},{3,2},{4,7},{5,4},{6,5},{7,6},{8,11},{9,8},{10,9... | collective-permute-start | bytes 1179656 | tf_op jit(solution)/shard_map/ppermute | solution.py:28
  61.8 4.3 %collective-permute-start.3 = (bf16[16,96,128]{2,1,0:T(8,128)(2,1)S(1)}, bf16[16,96,128]{2,1,0:T(8,128)(2,1)S(1)}, u32[]{:S(2)}, u32[]{:S(2)}) collective-permute-start(bf16[16,96,128]{2,1,0:T(8,128)(2,1)S(1)} %all-to-all-done), channel_id=1, source_target_pairs={{0,2},{1,3},{2,0},{3,1},{4,6},{5,7},{6,4},{7,5},{8,10},{9,11},{10,... | collective-permute-start | bytes 1179656 | tf_op jit(solution)/shard_map/ppermute | solution.py:28
  66.1 3.7 %collective-permute-start.2 = (bf16[16,96,128]{2,1,0:T(8,128)(2,1)S(1)}, bf16[16,96,128]{2,1,0:T(8,128)(2,1)S(1)}, u32[]{:S(2)}, u32[]{:S(2)}) collective-permute-start(bf16[16,96,128]{2,1,0:T(8,128)(2,1)S(1)} %all-to-all-done), channel_id=1, source_target_pairs={{0,1},{1,2},{2,3},{3,0},{4,5},{5,6},{6,7},{7,4},{8,9},{9,10},{10,1... | collective-permute-start | bytes 1179656 | tf_op jit(solution)/shard_map/ppermute | solution.py:28
  70.1 2.3 %collective-permute-done.4 = bf16[16,96,128]{2,1,0:T(8,128)(2,1)S(1)} collective-permute-done((bf16[16,96,128]{2,1,0:T(8,128)(2,1)S(1)}, bf16[16,96,128]{2,1,0:T(8,128)(2,1)S(1)}, u32[]{:S(2)}, u32[]{:S(2)}) %collective-permute-start.4) | collective-permute-done | bytes 393248 | tf_op jit(solution)/shard_map/ppermute | solution.py:28
  72.4 9.4 %collective-permute-done.3 = bf16[16,96,128]{2,1,0:T(8,128)(2,1)S(1)} collective-permute-done((bf16[16,96,128]{2,1,0:T(8,128)(2,1)S(1)}, bf16[16,96,128]{2,1,0:T(8,128)(2,1)S(1)}, u32[]{:S(2)}, u32[]{:S(2)}) %collective-permute-start.3) | collective-permute-done | bytes 393248 | tf_op jit(solution)/shard_map/ppermute | solution.py:28
  81.8 2.8 %collective-permute-done.2 = bf16[16,96,128]{2,1,0:T(8,128)(2,1)S(1)} collective-permute-done((bf16[16,96,128]{2,1,0:T(8,128)(2,1)S(1)}, bf16[16,96,128]{2,1,0:T(8,128)(2,1)S(1)}, u32[]{:S(2)}, u32[]{:S(2)}) %collective-permute-start.2) | collective-permute-done | bytes 393248 | tf_op jit(solution)/shard_map/ppermute | solution.py:28
  84.6 0.8 copy-done.2
  85.4 1.0 copy-done.3
  86.4 0.7 shard_map.76.w_ref
  87.1 3.3 %all-gather.3.cloned.1.call-done.tok_ref = bf16[2048,2048]{1,0:T(8,128)(2,1)} async-done(((bf16[128,2048]{1,0:T(8,128)(2,1)}), bf16[2048,2048]{1,0:T(8,128)(2,1)}) %all-gather.3.cloned.1.call-update) | async-done | bytes 8388624 | tf_op jit(solution)/shard_map/all_gather | solution.py:349
  90.4 9.3 %shard_map.77 = (bf16[16,128,128]{2,1,0:T(8,128)(2,1)S(1)}, bf16[16,128,128]{2,1,0:T(8,128)(2,1)S(1)}, bf16[16,128,128]{2,1,0:T(8,128)(2,1)S(1)}, bf16[16,128,12...) custom-call(s32[16,1,128]{2,1,0:T(1,128)S(1)} %bitcast.51, ...), custom_call_target="tpu_custom_call" | custom-call | flops 4294967296 | bytes 8388608 | tf_op jit(solution)/shard_map/pallas_call | solution.py:221
  99.8 3.4 %collective-permute-start.8 = (bf16[8,128,128]{2,1,0:T(8,128)(2,1)S(1)}, bf16[8,128,128]{2,1,0:T(8,128)(2,1)S(1)}, u32[]{:S(2)}, u32[]{:S(2)}) collective-permute-start(bf16[8,128,128]{2,1,0:T(8,128)(2,1)S(1)} %get-tuple-element.59), channel_id=1, source_target_pairs={{0,1},{1,2},{2,3},{3,8},{8,9},{9,10},{10,11},{11,16},{16,17},{17,1... | collective-permute-start | bytes 786440 | tf_op jit(solution)/shard_map/ppermute | solution.py:289
  103.2 0.7 collective-permute-start.7
  103.9 3.1 %collective-permute-start.9 = (bf16[8,128,128]{2,1,0:T(8,128)(2,1)S(1)}, bf16[8,128,128]{2,1,0:T(8,128)(2,1)S(1)}, u32[]{:S(2)}, u32[]{:S(2)}) collective-permute-start(bf16[8,128,128]{2,1,0:T(8,128)(2,1)S(1)} %get-tuple-element.58), channel_id=1, source_target_pairs={{0,1},{1,2},{2,3},{3,0},{4,5},{5,6},{6,7},{7,4},{8,9},{9,10},{10,1... | collective-permute-start | bytes 786440 | tf_op jit(solution)/shard_map/ppermute | solution.py:28
  107.1 2.7 %collective-permute-start.6 = (bf16[8,128,128]{2,1,0:T(8,128)(2,1)S(1)}, bf16[8,128,128]{2,1,0:T(8,128)(2,1)S(1)}, u32[]{:S(2)}, u32[]{:S(2)}) collective-permute-start(bf16[8,128,128]{2,1,0:T(8,128)(2,1)S(1)} %get-tuple-element.62), channel_id=1, source_target_pairs={{0,3},{1,0},{2,1},{3,2},{4,7},{5,4},{6,5},{7,6},{8,11},{9,8},{10,9... | collective-permute-start | bytes 786440 | tf_op jit(solution)/shard_map/ppermute | solution.py:28
  109.8 5.1 %collective-permute-start.5 = (bf16[8,128,128]{2,1,0:T(8,128)(2,1)S(1)}, bf16[8,128,128]{2,1,0:T(8,128)(2,1)S(1)}, u32[]{:S(2)}, u32[]{:S(2)}) collective-permute-start(bf16[8,128,128]{2,1,0:T(8,128)(2,1)S(1)} %get-tuple-element.63), channel_id=1, source_target_pairs={{0,27},{1,0},{2,1},{3,2},{8,3},{9,8},{10,9},{11,10},{16,11},{17,16... | collective-permute-start | bytes 786440 | tf_op jit(solution)/shard_map/ppermute | solution.py:289
  115.0 0.7 collective-permute-done.9
  115.8 7.6 %shard_map.78 = (bf16[16,128,128]{2,1,0:T(8,128)(2,1)S(1)}, bf16[16,128,128]{2,1,0:T(8,128)(2,1)S(1)}, bf16[2,16,128]{2,1,0:T(8,128)(2,1)S(1)}) custom-call(s32[16,1,128]{2,1,0:T(1,128)S(1)} %bitcast.52, f32[8,128]{1,0:T(8,128)S(1)} %pad_maximum_fusion.4.taps_ref, bf16[16,128,128]{2,1,0:T(8,128)(2,1)S(1)} %get-tuple-element.33.q_ref, ...), custom_call_target="tpu_custom_call" | custom-call | flops 2147483648 | bytes 3145728 | tf_op jit(solution)/shard_map/pallas_call | solution.py:241
  123.4 0.8 collective-permute-done.5
  124.2 2.5 %collective-permute-start.10 = (bf16[8,128,128]{2,1,0:T(8,128)(2,1)S(1)}, bf16[8,128,128]{2,1,0:T(8,128)(2,1)S(1)}, u32[]{:S(2)}, u32[]{:S(2)}) collective-permute-start(bf16[8,128,128]{2,1,0:T(8,128)(2,1)S(1)} %get-tuple-element.55), channel_id=1, source_target_pairs={{0,4},{4,0},{1,5},{5,1},{2,6},{6,2},{3,7},{7,3},{8,12},{12,8},{9,1... | collective-permute-start | bytes 786440 | tf_op jit(solution)/shard_map/ppermute | solution.py:28
  126.8 7.5 %shard_map.79 = bf16[4,2,8,112,128]{4,3,2,1,0:T(8,128)(2,1)S(1)} custom-call(s32[1]{0:T(128)} %bitcast.8.x_ref, bf16[2048,2048]{1,0:T(8,128)(2,1)} %all-gather.3.cloned.1.call-done.tok_ref, bf16[16,128,128]{2,1,0:T(8,128)(2,1)S(1)} %get-tuple-element.37.gq_ref, f32[16,128,128]{2,1,0:T(8,128)S(1)} %get-tuple-element.38.own_ref, ...), custom_call_target="tpu_custom_call" | custom-call | flops 3221225472 | bytes 8388608 | tf_op jit(solution)/shard_map/pallas_call | solution.py:273
  134.4 0.9 maximum_select_fusion
  135.4 3.6 %collective-permute-start.11 = (bf16[2,8,112,128]{3,2,1,0:T(8,128)(2,1)S(1)}, bf16[2,8,112,128]{3,2,1,0:T(8,128)(2,1)S(1)}, u32[]{:S(2)}, u32[]{:S(2)}) collective-permute-start(bf16[2,8,112,128]{3,2,1,0:T(8,128)(2,1)S(1)} %get-tuple-element.51), channel_id=1, source_target_pairs={{0,1},{1,2},{2,3},{3,0},{4,5},{5,6},{6,7},{7,4},{8,9},{9,10},{10,1... | collective-permute-start | bytes 1376264 | tf_op jit(solution)/shard_map/ppermute | solution.py:28
  139.0 7.2 %collective-permute-start.13 = (bf16[2,8,112,128]{3,2,1,0:T(8,128)(2,1)S(1)}, bf16[2,8,112,128]{3,2,1,0:T(8,128)(2,1)S(1)}, u32[]{:S(2)}, u32[]{:S(2)}) collective-permute-start(bf16[2,8,112,128]{3,2,1,0:T(8,128)(2,1)S(1)} %get-tuple-element.52), channel_id=1, source_target_pairs={{0,3},{1,0},{2,1},{3,2},{4,7},{5,4},{6,5},{7,6},{8,11},{9,8},{10,9... | collective-permute-start | bytes 1376264 | tf_op jit(solution)/shard_map/ppermute | solution.py:28
  146.2 5.9 %collective-permute-start.12 = (bf16[2,8,112,128]{3,2,1,0:T(8,128)(2,1)S(1)}, bf16[2,8,112,128]{3,2,1,0:T(8,128)(2,1)S(1)}, u32[]{:S(2)}, u32[]{:S(2)}) collective-permute-start(bf16[2,8,112,128]{3,2,1,0:T(8,128)(2,1)S(1)} %get-tuple-element.53), channel_id=1, source_target_pairs={{0,2},{1,3},{2,0},{3,1},{4,6},{5,7},{6,4},{7,5},{8,10},{9,11},{10,... | collective-permute-start | bytes 1376264 | tf_op jit(solution)/shard_map/ppermute | solution.py:28
  152.1 3.5 %collective-permute-done.11 = bf16[2,8,112,128]{3,2,1,0:T(8,128)(2,1)S(1)} collective-permute-done((bf16[2,8,112,128]{3,2,1,0:T(8,128)(2,1)S(1)}, bf16[2,8,112,128]{3,2,1,0:T(8,128)(2,1)S(1)}, u32[]{:S(2)}, u32[]{:S(2)}) %collective-permute-start.11) | collective-permute-done | bytes 458784 | tf_op jit(solution)/shard_map/ppermute | solution.py:28
  155.6 3.6 %collective-permute-done.13 = bf16[2,8,112,128]{3,2,1,0:T(8,128)(2,1)S(1)} collective-permute-done((bf16[2,8,112,128]{3,2,1,0:T(8,128)(2,1)S(1)}, bf16[2,8,112,128]{3,2,1,0:T(8,128)(2,1)S(1)}, u32[]{:S(2)}, u32[]{:S(2)}) %collective-permute-start.13) | collective-permute-done | bytes 458784 | tf_op jit(solution)/shard_map/ppermute | solution.py:28
  159.2 10.4 %collective-permute-done.12 = bf16[2,8,112,128]{3,2,1,0:T(8,128)(2,1)S(1)} collective-permute-done((bf16[2,8,112,128]{3,2,1,0:T(8,128)(2,1)S(1)}, bf16[2,8,112,128]{3,2,1,0:T(8,128)(2,1)S(1)}, u32[]{:S(2)}, u32[]{:S(2)}) %collective-permute-start.12) | collective-permute-done | bytes 458784 | tf_op jit(solution)/shard_map/ppermute | solution.py:28
  169.6 0.2 fusion.1
  170.0 0.8 pad_maximum_fusion.2
  170.8 15.4 %all-to-all-start.2 = ((bf16[16,112,128]{2,1,0:T(8,128)(2,1)}), bf16[16,112,128]{2,1,0:T(8,128)(2,1)S(1)}, u32[]{:S(2)}, u32[]{:S(2)}) async-start(bf16[16,112,128]{2,1,0:T(8,128)(2,1)} %bitcast.20), calls=%async_computation.2 | async-start | bytes 917504 | tf_op jit(solution)/shard_map/all_to_all | solution.py:23
  186.2 2.2 copy-done.1
  188.4 1.1 shard_map.80
  189.5 21.7 %all-to-all-done.2 = bf16[16,112,128]{2,1,0:T(8,128)(2,1)S(1)} async-done(((bf16[16,112,128]{2,1,0:T(8,128)(2,1)}), bf16[16,112,128]{2,1,0:T(8,128)(2,1)S(1)}, u32[]{:S(2)}, u32[]{:S(2)}) %all-to-all-start.2) | async-done | bytes 458784 | tf_op jit(solution)/shard_map/all_to_all | solution.py:23
  211.2 0.6 slice_add_fusion.1
  211.8 0.2 reshape.90
  212.2 0.8 reshape.91
  (48 shorter events, 1.4 us)
Async XLA Ops:
  7.2 17.4 %copy-start = (s32[16,128]{1,0:T(8,128)S(1)}, s32[16,128]{1,0:T(8,128)}, u32[]{:S(2)}) copy-start(s32[16,128]{1,0:T(8,128)} %param.8) | copy-start | bytes 24580
  7.2 20.8 %copy-start.5 = (f32[8,128]{1,0:T(8,128)S(1)}, f32[8,128]{1,0:T(8,128)}, u32[]{:S(2)}) copy-start(f32[8,128]{1,0:T(8,128)} %param.7) | copy-start | bytes 12292
  7.2 46.2 %copy-start.4 = (bf16[128,2048]{1,0:T(8,128)(2,1)S(1)}, bf16[128,2048]{1,0:T(8,128)(2,1)}, u32[]{:S(2)}) copy-start(bf16[128,2048]{1,0:T(8,128)(2,1)} %param.9) | copy-start | bytes 1572868
  7.2 83.2 %all-gather.3.cloned.1.call-start = ((), (), s32[]{:S(2)}) async-start(), calls=%async_computation.3 | async-start | bytes 8912896 | tf_op jit(solution)/shard_map/all_gather | solution.py:349
  9.8 43.5 %all-to-all-start = ((bf16[16,96,128]{2,1,0:T(8,128)(2,1)}), bf16[16,96,128]{2,1,0:T(8,128)(2,1)S(1)}, u32[]{:S(2)}, u32[]{:S(2)}) async-start(bf16[16,96,128]{2,1,0:T(8,128)(2,1)} %bitcast.2), calls=%async_computation | async-start | bytes 786432 | tf_op jit(solution)/shard_map/all_to_all | solution.py:23
  24.6 20.7 %collective-permute-start.1 = (s32[8,128]{1,0:T(8,128)S(1)}, s32[8,128]{1,0:T(8,128)S(1)}, u32[]{:S(2)}, u32[]{:S(2)}) collective-permute-start(s32[8,128]{1,0:T(8,128)S(1)} %constant_dynamic-slice_fusion), channel_id=1, source_target_pairs={{0,4},{4,0},{1,5},{5,1},{2,6},{6,2},{3,7},{7,3},{8,12},{12,8},{9,1... | collective-permute-start | bytes 12296 | tf_op jit(solution)/shard_map/ppermute | solution.py:28
  28.0 25.3 %collective-permute-start = (f32[8,128]{1,0:T(8,128)S(1)}, f32[8,128]{1,0:T(8,128)S(1)}, u32[]{:S(2)}, u32[]{:S(2)}) collective-permute-start(f32[8,128]{1,0:T(8,128)S(1)} %copy-done.5), channel_id=1, source_target_pairs={{0,256},{256,0},{1,257},{257,1},{2,258},{258,2},{3,259},{259,3},{4... | collective-permute-start | bytes 12296 | tf_op jit(solution)/shard_map/ppermute | solution.py:28
  54.7 32.4 %all-to-all-start.1 = ((bf16[16,128,128]{2,1,0:T(8,128)(2,1)}), bf16[16,128,128]{2,1,0:T(8,128)(2,1)S(1)}, u32[]{:S(2)}, u32[]{:S(2)}) async-start(bf16[16,128,128]{2,1,0:T(8,128)(2,1)} %copy.13), calls=%async_computation.1 | async-start | bytes 1048576 | tf_op jit(solution)/shard_map/all_to_all | solution.py:23
  59.3 126.9 %all-gather.5.cloned.1.call-start = ((), (), s32[]{:S(2)}) async-start(), calls=%async_computation.4 | async-start | bytes 4718592 | tf_op jit(solution)/shard_map/all_gather | solution.py:382
  59.3 13.1 %collective-permute-start.4 = (bf16[16,96,128]{2,1,0:T(8,128)(2,1)S(1)}, bf16[16,96,128]{2,1,0:T(8,128)(2,1)S(1)}, u32[]{:S(2)}, u32[]{:S(2)}) collective-permute-start(bf16[16,96,128]{2,1,0:T(8,128)(2,1)S(1)} %all-to-all-done), channel_id=1, source_target_pairs={{0,3},{1,0},{2,1},{3,2},{4,7},{5,4},{6,5},{7,6},{8,11},{9,8},{10,9... | collective-permute-start | bytes 1179656 | tf_op jit(solution)/shard_map/ppermute | solution.py:28
  61.8 20.0 %collective-permute-start.3 = (bf16[16,96,128]{2,1,0:T(8,128)(2,1)S(1)}, bf16[16,96,128]{2,1,0:T(8,128)(2,1)S(1)}, u32[]{:S(2)}, u32[]{:S(2)}) collective-permute-start(bf16[16,96,128]{2,1,0:T(8,128)(2,1)S(1)} %all-to-all-done), channel_id=1, source_target_pairs={{0,2},{1,3},{2,0},{3,1},{4,6},{5,7},{6,4},{7,5},{8,10},{9,11},{10,... | collective-permute-start | bytes 1179656 | tf_op jit(solution)/shard_map/ppermute | solution.py:28
  66.1 18.4 %collective-permute-start.2 = (bf16[16,96,128]{2,1,0:T(8,128)(2,1)S(1)}, bf16[16,96,128]{2,1,0:T(8,128)(2,1)S(1)}, u32[]{:S(2)}, u32[]{:S(2)}) collective-permute-start(bf16[16,96,128]{2,1,0:T(8,128)(2,1)S(1)} %all-to-all-done), channel_id=1, source_target_pairs={{0,1},{1,2},{2,3},{3,0},{4,5},{5,6},{6,7},{7,4},{8,9},{9,10},{10,1... | collective-permute-start | bytes 1179656 | tf_op jit(solution)/shard_map/ppermute | solution.py:28
  84.6 0.8 copy-start.2
  85.4 1.0 copy-start.3
  99.8 15.1 %collective-permute-start.8 = (bf16[8,128,128]{2,1,0:T(8,128)(2,1)S(1)}, bf16[8,128,128]{2,1,0:T(8,128)(2,1)S(1)}, u32[]{:S(2)}, u32[]{:S(2)}) collective-permute-start(bf16[8,128,128]{2,1,0:T(8,128)(2,1)S(1)} %get-tuple-element.59), channel_id=1, source_target_pairs={{0,1},{1,2},{2,3},{3,8},{8,9},{9,10},{10,11},{11,16},{16,17},{17,1... | collective-permute-start | bytes 786440 | tf_op jit(solution)/shard_map/ppermute | solution.py:289
  103.2 11.7 %collective-permute-start.7 = (bf16[1,128,128]{2,1,0:T(8,128)(2,1)S(1)}, bf16[1,128,128]{2,1,0:T(8,128)(2,1)S(1)}, u32[]{:S(2)}, u32[]{:S(2)}) collective-permute-start(bf16[1,128,128]{2,1,0:T(8,128)(2,1)S(1)} %get-tuple-element.60), channel_id=1, source_target_pairs={{27,256},{256,27},{31,260},{260,31},{59,288},{288,59},{63,292},{29... | collective-permute-start | bytes 98312 | tf_op jit(solution)/shard_map/ppermute | solution.py:295
  103.9 11.8 %collective-permute-start.9 = (bf16[8,128,128]{2,1,0:T(8,128)(2,1)S(1)}, bf16[8,128,128]{2,1,0:T(8,128)(2,1)S(1)}, u32[]{:S(2)}, u32[]{:S(2)}) collective-permute-start(bf16[8,128,128]{2,1,0:T(8,128)(2,1)S(1)} %get-tuple-element.58), channel_id=1, source_target_pairs={{0,1},{1,2},{2,3},{3,0},{4,5},{5,6},{6,7},{7,4},{8,9},{9,10},{10,1... | collective-permute-start | bytes 786440 | tf_op jit(solution)/shard_map/ppermute | solution.py:28
  107.1 16.3 %collective-permute-start.6 = (bf16[8,128,128]{2,1,0:T(8,128)(2,1)S(1)}, bf16[8,128,128]{2,1,0:T(8,128)(2,1)S(1)}, u32[]{:S(2)}, u32[]{:S(2)}) collective-permute-start(bf16[8,128,128]{2,1,0:T(8,128)(2,1)S(1)} %get-tuple-element.62), channel_id=1, source_target_pairs={{0,3},{1,0},{2,1},{3,2},{4,7},{5,4},{6,5},{7,6},{8,11},{9,8},{10,9... | collective-permute-start | bytes 786440 | tf_op jit(solution)/shard_map/ppermute | solution.py:28
  109.8 14.3 %collective-permute-start.5 = (bf16[8,128,128]{2,1,0:T(8,128)(2,1)S(1)}, bf16[8,128,128]{2,1,0:T(8,128)(2,1)S(1)}, u32[]{:S(2)}, u32[]{:S(2)}) collective-permute-start(bf16[8,128,128]{2,1,0:T(8,128)(2,1)S(1)} %get-tuple-element.63), channel_id=1, source_target_pairs={{0,27},{1,0},{2,1},{3,2},{8,3},{9,8},{10,9},{11,10},{16,11},{17,16... | collective-permute-start | bytes 786440 | tf_op jit(solution)/shard_map/ppermute | solution.py:289
  124.2 10.2 %collective-permute-start.10 = (bf16[8,128,128]{2,1,0:T(8,128)(2,1)S(1)}, bf16[8,128,128]{2,1,0:T(8,128)(2,1)S(1)}, u32[]{:S(2)}, u32[]{:S(2)}) collective-permute-start(bf16[8,128,128]{2,1,0:T(8,128)(2,1)S(1)} %get-tuple-element.55), channel_id=1, source_target_pairs={{0,4},{4,0},{1,5},{5,1},{2,6},{6,2},{3,7},{7,3},{8,12},{12,8},{9,1... | collective-permute-start | bytes 786440 | tf_op jit(solution)/shard_map/ppermute | solution.py:28
  135.4 20.2 %collective-permute-start.11 = (bf16[2,8,112,128]{3,2,1,0:T(8,128)(2,1)S(1)}, bf16[2,8,112,128]{3,2,1,0:T(8,128)(2,1)S(1)}, u32[]{:S(2)}, u32[]{:S(2)}) collective-permute-start(bf16[2,8,112,128]{3,2,1,0:T(8,128)(2,1)S(1)} %get-tuple-element.51), channel_id=1, source_target_pairs={{0,1},{1,2},{2,3},{3,0},{4,5},{5,6},{6,7},{7,4},{8,9},{9,10},{10,1... | collective-permute-start | bytes 1376264 | tf_op jit(solution)/shard_map/ppermute | solution.py:28
  139.0 20.2 %collective-permute-start.13 = (bf16[2,8,112,128]{3,2,1,0:T(8,128)(2,1)S(1)}, bf16[2,8,112,128]{3,2,1,0:T(8,128)(2,1)S(1)}, u32[]{:S(2)}, u32[]{:S(2)}) collective-permute-start(bf16[2,8,112,128]{3,2,1,0:T(8,128)(2,1)S(1)} %get-tuple-element.52), channel_id=1, source_target_pairs={{0,3},{1,0},{2,1},{3,2},{4,7},{5,4},{6,5},{7,6},{8,11},{9,8},{10,9... | collective-permute-start | bytes 1376264 | tf_op jit(solution)/shard_map/ppermute | solution.py:28
  146.2 23.4 %collective-permute-start.12 = (bf16[2,8,112,128]{3,2,1,0:T(8,128)(2,1)S(1)}, bf16[2,8,112,128]{3,2,1,0:T(8,128)(2,1)S(1)}, u32[]{:S(2)}, u32[]{:S(2)}) collective-permute-start(bf16[2,8,112,128]{3,2,1,0:T(8,128)(2,1)S(1)} %get-tuple-element.53), channel_id=1, source_target_pairs={{0,2},{1,3},{2,0},{3,1},{4,6},{5,7},{6,4},{7,5},{8,10},{9,11},{10,... | collective-permute-start | bytes 1376264 | tf_op jit(solution)/shard_map/ppermute | solution.py:28
  170.8 40.4 %all-to-all-start.2 = ((bf16[16,112,128]{2,1,0:T(8,128)(2,1)}), bf16[16,112,128]{2,1,0:T(8,128)(2,1)S(1)}, u32[]{:S(2)}, u32[]{:S(2)}) async-start(bf16[16,112,128]{2,1,0:T(8,128)(2,1)} %bitcast.20), calls=%async_computation.2 | async-start | bytes 917504 | tf_op jit(solution)/shard_map/all_to_all | solution.py:23
  186.2 2.2 copy-start.1
Sparse Core Ops, SparseCore 0:
  10.2 80.1 all-gather.2
  135.4 48.3 all-gather.4

commit v7 on v6

--- a/solution.py
+++ b/solution.py
@@ -94,7 +94,7 @@
         own_ref[j] = jnp.dot(own, right, preferred_element_type=F32)
 
 
-def front_kernel(off_ref, taps_ref, q_ref, cot_ref, prod_ref, halo_ref, gated_ref, gq_ref, df_ref, table, acc):
+def front_kernel(_, off_ref, taps_ref, q_ref, cot_ref, prod_ref, halo_ref, gated_ref, gq_ref, df_ref, table, acc):
     step = pl.program_id(0)
 
     @pl.when(step == 0)
@@ -150,10 +150,12 @@
             df_ref[h] = rows.astype(BF)
 
 
-def rows_kernel(_, in_ref, out_ref):
+def rows_kernel(mine_ref, in_ref, out_ref):
     places = in_ref.shape[0]
+    lower = mine_ref[1] == 0
     for i in range(places):
-        sides = lane_halves(in_ref[i, 0, 0].astype(F32), in_ref[i, 1, 0].astype(F32))
+        own, beside = in_ref[i, 0, 0].astype(F32), in_ref[i, 1, 0].astype(F32)
+        sides = lane_halves(jnp.where(lower, own, beside), jnp.where(lower, beside, own))
         for h, side in enumerate(sides):
             at = (h * places + i) * LANES
             out_ref[:, at : at + LANES] = side.astype(BF)
@@ -236,19 +238,30 @@
     )(off, taps, tokens, table, cot)
 
 
-def front(hi, off, taps, q, cot, product, halo):
-    n, at_once = q.shape[0], 4
+def front(hi, member, off, taps, q, cot, product, halo):
+    n = q.shape[0]
+    at_once = min(4, n // 2)
+    steps = n // at_once
+    block = pl.BlockSpec((at_once, LANES, LANES), lambda i, member: (i, 0, 0))
+    shape = (at_once, LANES, LANES)
+    own_first = pl.BlockSpec(shape, lambda i, member: (lax.rem(i + member[0] * (steps // 2), steps), 0, 0))
     return pl.pallas_call(
         front_kernel,
-        grid=(n // at_once,),
-        in_specs=[pl.BlockSpec((at_once, 1, LANES), lambda i: (i, 0, 0)), whole_spec(taps.shape)]
-        + [block_spec(at_once)] * 4,
-        out_specs=[block_spec(at_once)] * 2 + [whole_spec((hi, EXTRA, LANES))],
+        grid_spec=pltpu.PrefetchScalarGridSpec(
+            num_scalar_prefetch=1,
+            grid=(steps,),
+            in_specs=[
+                pl.BlockSpec((at_once, 1, LANES), lambda i, member: (i, 0, 0)),
+                pl.BlockSpec(taps.shape, lambda i, member: (0, 0)),
+            ]
+            + [block] * 4,
+            out_specs=[own_first, block, pl.BlockSpec((hi, EXTRA, LANES), lambda i, member: (0, 0, 0))],
+            scratch_shapes=[pltpu.VMEM((PER, LANES, LANES), BF), pltpu.VMEM((PER, LANES, LANES), F32)],
+        ),
         out_shape=[jax.ShapeDtypeStruct(q.shape, BF)] * 2 + [jax.ShapeDtypeStruct((hi, EXTRA, LANES), BF)],
-        scratch_shapes=[pltpu.VMEM((PER, LANES, LANES), BF), pltpu.VMEM((PER, LANES, LANES), F32)],
         compiler_params=PARAMS,
         cost_estimate=cost(4 * q.size * 2 * LANES * PER, 12 * q.size),
-    )(off, taps, q, cot, product, halo)
+    )(member, off, taps, q, cot, product, halo)
 
 
 def output_rows(mine, gathered):
@@ -370,18 +383,16 @@
 
     q, k, v, product, grad_prev, grad_own = project(off, taps, gathered, table, cot)
     halo, back = halos(product, grad_prev)
-    gated, grad_q, grad_taps = front(hi, off, taps_back, q, cot, product, halo)
+    gated, grad_q, grad_taps = front(hi, member.astype(jnp.int32)[None], off, taps_back, q, cot, product, halo)
     back, grad_q, gated = lax.optimization_barrier((back, grad_q, gated))
-    lower = member == 0
-    beside = turned(jnp.where(lower, gated[places:], gated[:places]), "z_c", 1)
+    beside = turned(gated[places:], "z_c", 1)
     got = placed_back(*back)
     partial = weight_grad(x, gathered, (grad_q, grad_own, got, k, v, grad_taps), (xs, hi, lo, feats))
     beside, partial = lax.optimization_barrier((beside, partial))
-    mine = jnp.where(lower, gated[:places], gated[places:])
-    both = jnp.where(lower, jnp.stack([mine, beside]), jnp.stack([beside, mine]))
+    both = jnp.concatenate([gated[:places], beside], 0)
     out = lax.all_gather(both.reshape(blocks * rows, LANES), ("y", "core"), axis=0, tiled=True)
     out = out.reshape(places, 2, places, rows, LANES)
-    out = output_rows(lax.axis_index(("y", "core")).astype(jnp.int32)[None], out)
+    out = output_rows(jnp.stack([lax.axis_index(("y", "core")), member]).astype(jnp.int32), out)
     parts = [partial[0]] + [turned(partial[step], "x", step) for step in range(1, xs)]
     over_x = sum(part.astype(F32) for part in parts)
     taps_x = over_x[:, :, row_count : row_count + PER // 2] + over_x[:, :, row_count + PER // 2 : row_count + PER]

time: 221 us -> 221 us (level)
  no operation moved by 1% of the time
where the time goes in v7:
time: 221 us; the launch traced here: 220 us
  starting transfers between devices  92.2 us (42%)
  waiting for transfers between devices  74.5 us (34%)
  Pallas kernels  26.8 us (12%)
  between operations  14.5 us (7%)
  local copies, waits for them, and re-layouts  8.74 us (4%)
  other arithmetic  3.07 us (1%)
    ppermute x11, waiting for transfers between devices, turned(): lax.ppermute(shard, axis, [(i, (i + by) % count) for i in range(count)])  48.6 us
    ppermute x11, starting transfers between devices, turned(): lax.ppermute(shard, axis, [(i, (i + by) % count) for i in range(count)])  48.3 us
    all_to_all x3, starting transfers between devices, swap_blocks(): return lax.all_to_all(pieces, axes, split_axis=0, concat_axis=0, tiled=True)  34.7 us
    all_to_all x3, waiting for transfers between devices, swap_blocks(): return lax.all_to_all(pieces, axes, split_axis=0, concat_axis=0, tiled=True)  21.1 us
    pallas_call x1, Pallas kernels, project(): pl.pallas_call(project_kernel, grid=(blocks // at_once,), in_specs=[pl.Bl...  9.31 us
    ppermute x2, starting transfers between devices, seq_ring(): return lax.ppermute(shard, SEQ_AX, pairs)  8.5 us
    pallas_call x1, Pallas kernels, front(): pl.pallas_call(front_kernel, grid_spec=pltpu.PrefetchScalarGridSpec(num_s...  7.6 us
    pallas_call x1, Pallas kernels, weight_grad(): pl.pallas_call(weight_kernel, grid=(lo // 4,), in_specs=[SCALAR, pl.Block...  7.54 us
  transfers between devices with their start and end apart: 19, of which 12 were waited for; matrix products, arithmetic and copies ran while one was open for 2% of the time, Pallas kernels for 8%

profile of v7, /device:TPU:90, one launch (start us, length us, event | category | flops | bytes accessed | tf_op | source)
XLA Modules:
  0.0 219.8 jit_solution(6279174765421615424)
XLA Ops:
  7.2 0.7 all-gather.3.cloned.1.call-update
  7.9 0.9 reshape.77
  9.1 0.8 broadcast_in_dim.14
  9.8 14.8 %all-to-all-start = ((bf16[16,96,128]{2,1,0:T(8,128)(2,1)}), bf16[16,96,128]{2,1,0:T(8,128)(2,1)S(1)}, u32[]{:S(2)}, u32[]{:S(2)}) async-start(bf16[16,96,128]{2,1,0:T(8,128)(2,1)} %bitcast.2), calls=%async_computation | async-start | bytes 786432 | tf_op jit(solution)/shard_map/all_to_all | solution.py:23
  24.6 3.4 %collective-permute-start.1 = (s32[8,128]{1,0:T(8,128)S(1)}, s32[8,128]{1,0:T(8,128)S(1)}, u32[]{:S(2)}, u32[]{:S(2)}) collective-permute-start(s32[8,128]{1,0:T(8,128)S(1)} %constant_dynamic-slice_fusion), channel_id=1, source_target_pairs={{0,4},{4,0},{1,5},{5,1},{2,6},{6,2},{3,7},{7,3},{8,12},{12,8},{9,1... | collective-permute-start | bytes 12296 | tf_op jit(solution)/shard_map/ppermute | solution.py:28
  28.0 9.4 %collective-permute-start = (f32[8,128]{1,0:T(8,128)S(1)}, f32[8,128]{1,0:T(8,128)S(1)}, u32[]{:S(2)}, u32[]{:S(2)}) collective-permute-start(f32[8,128]{1,0:T(8,128)S(1)} %copy-done.5), channel_id=1, source_target_pairs={{0,256},{256,0},{1,257},{257,1},{2,258},{258,2},{3,259},{259,3},{4... | collective-permute-start | bytes 12296 | tf_op jit(solution)/shard_map/ppermute | solution.py:28
  37.4 7.9 %collective-permute-done.1 = s32[8,128]{1,0:T(8,128)S(1)} collective-permute-done((s32[8,128]{1,0:T(8,128)S(1)}, s32[8,128]{1,0:T(8,128)S(1)}, u32[]{:S(2)}, u32[]{:S(2)}) %collective-permute-start.1) | collective-permute-done | bytes 4128 | tf_op jit(solution)/shard_map/ppermute | solution.py:28
  45.3 8.0 %collective-permute-done = f32[8,128]{1,0:T(8,128)S(1)} collective-permute-done((f32[8,128]{1,0:T(8,128)S(1)}, f32[8,128]{1,0:T(8,128)S(1)}, u32[]{:S(2)}, u32[]{:S(2)}) %collective-permute-start) | collective-permute-done | bytes 4128 | tf_op jit(solution)/shard_map/ppermute | solution.py:28
  53.3 0.3 copy.11
  53.7 1.0 copy.13
  54.7 4.6 %all-to-all-start.1 = ((bf16[16,128,128]{2,1,0:T(8,128)(2,1)}), bf16[16,128,128]{2,1,0:T(8,128)(2,1)S(1)}, u32[]{:S(2)}, u32[]{:S(2)}) async-start(bf16[16,128,128]{2,1,0:T(8,128)(2,1)} %copy.13), calls=%async_computation.1 | async-start | bytes 1048576 | tf_op jit(solution)/shard_map/all_to_all | solution.py:23
  59.3 2.4 %collective-permute-start.4 = (bf16[16,96,128]{2,1,0:T(8,128)(2,1)S(1)}, bf16[16,96,128]{2,1,0:T(8,128)(2,1)S(1)}, u32[]{:S(2)}, u32[]{:S(2)}) collective-permute-start(bf16[16,96,128]{2,1,0:T(8,128)(2,1)S(1)} %all-to-all-done), channel_id=1, source_target_pairs={{0,3},{1,0},{2,1},{3,2},{4,7},{5,4},{6,5},{7,6},{8,11},{9,8},{10,9... | collective-permute-start | bytes 1179656 | tf_op jit(solution)/shard_map/ppermute | solution.py:28
  61.8 4.3 %collective-permute-start.3 = (bf16[16,96,128]{2,1,0:T(8,128)(2,1)S(1)}, bf16[16,96,128]{2,1,0:T(8,128)(2,1)S(1)}, u32[]{:S(2)}, u32[]{:S(2)}) collective-permute-start(bf16[16,96,128]{2,1,0:T(8,128)(2,1)S(1)} %all-to-all-done), channel_id=1, source_target_pairs={{0,2},{1,3},{2,0},{3,1},{4,6},{5,7},{6,4},{7,5},{8,10},{9,11},{10,... | collective-permute-start | bytes 1179656 | tf_op jit(solution)/shard_map/ppermute | solution.py:28
  66.1 3.7 %collective-permute-start.2 = (bf16[16,96,128]{2,1,0:T(8,128)(2,1)S(1)}, bf16[16,96,128]{2,1,0:T(8,128)(2,1)S(1)}, u32[]{:S(2)}, u32[]{:S(2)}) collective-permute-start(bf16[16,96,128]{2,1,0:T(8,128)(2,1)S(1)} %all-to-all-done), channel_id=1, source_target_pairs={{0,1},{1,2},{2,3},{3,0},{4,5},{5,6},{6,7},{7,4},{8,9},{9,10},{10,1... | collective-permute-start | bytes 1179656 | tf_op jit(solution)/shard_map/ppermute | solution.py:28
  70.1 2.3 %collective-permute-done.4 = bf16[16,96,128]{2,1,0:T(8,128)(2,1)S(1)} collective-permute-done((bf16[16,96,128]{2,1,0:T(8,128)(2,1)S(1)}, bf16[16,96,128]{2,1,0:T(8,128)(2,1)S(1)}, u32[]{:S(2)}, u32[]{:S(2)}) %collective-permute-start.4) | collective-permute-done | bytes 393248 | tf_op jit(solution)/shard_map/ppermute | solution.py:28
  72.4 9.4 %collective-permute-done.3 = bf16[16,96,128]{2,1,0:T(8,128)(2,1)S(1)} collective-permute-done((bf16[16,96,128]{2,1,0:T(8,128)(2,1)S(1)}, bf16[16,96,128]{2,1,0:T(8,128)(2,1)S(1)}, u32[]{:S(2)}, u32[]{:S(2)}) %collective-permute-start.3) | collective-permute-done | bytes 393248 | tf_op jit(solution)/shard_map/ppermute | solution.py:28
  81.8 2.8 %collective-permute-done.2 = bf16[16,96,128]{2,1,0:T(8,128)(2,1)S(1)} collective-permute-done((bf16[16,96,128]{2,1,0:T(8,128)(2,1)S(1)}, bf16[16,96,128]{2,1,0:T(8,128)(2,1)S(1)}, u32[]{:S(2)}, u32[]{:S(2)}) %collective-permute-start.2) | collective-permute-done | bytes 393248 | tf_op jit(solution)/shard_map/ppermute | solution.py:28
  84.6 0.8 copy-done.2
  85.4 1.0 copy-done.3
  86.4 0.7 shard_map.76.w_ref
  87.1 3.3 %all-gather.3.cloned.1.call-done.tok_ref = bf16[2048,2048]{1,0:T(8,128)(2,1)} async-done(((bf16[128,2048]{1,0:T(8,128)(2,1)}), bf16[2048,2048]{1,0:T(8,128)(2,1)}) %all-gather.3.cloned.1.call-update) | async-done | bytes 8388624 | tf_op jit(solution)/shard_map/all_gather | solution.py:362
  90.4 9.3 %shard_map.77 = (bf16[16,128,128]{2,1,0:T(8,128)(2,1)S(1)}, bf16[16,128,128]{2,1,0:T(8,128)(2,1)S(1)}, bf16[16,128,128]{2,1,0:T(8,128)(2,1)S(1)}, bf16[16,128,12...) custom-call(s32[16,1,128]{2,1,0:T(1,128)S(1)} %bitcast.49, ...), custom_call_target="tpu_custom_call" | custom-call | flops 4294967296 | bytes 8388608 | tf_op jit(solution)/shard_map/pallas_call | solution.py:223
  99.8 3.4 %collective-permute-start.8 = (bf16[8,128,128]{2,1,0:T(8,128)(2,1)S(1)}, bf16[8,128,128]{2,1,0:T(8,128)(2,1)S(1)}, u32[]{:S(2)}, u32[]{:S(2)}) collective-permute-start(bf16[8,128,128]{2,1,0:T(8,128)(2,1)S(1)} %get-tuple-element.59), channel_id=1, source_target_pairs={{0,1},{1,2},{2,3},{3,8},{8,9},{9,10},{10,11},{11,16},{16,17},{17,1... | collective-permute-start | bytes 786440 | tf_op jit(solution)/shard_map/ppermute | solution.py:302
  103.2 0.7 collective-permute-start.7
  103.9 3.1 %collective-permute-start.9 = (bf16[8,128,128]{2,1,0:T(8,128)(2,1)S(1)}, bf16[8,128,128]{2,1,0:T(8,128)(2,1)S(1)}, u32[]{:S(2)}, u32[]{:S(2)}) collective-permute-start(bf16[8,128,128]{2,1,0:T(8,128)(2,1)S(1)} %get-tuple-element.58), channel_id=1, source_target_pairs={{0,1},{1,2},{2,3},{3,0},{4,5},{5,6},{6,7},{7,4},{8,9},{9,10},{10,1... | collective-permute-start | bytes 786440 | tf_op jit(solution)/shard_map/ppermute | solution.py:28
  107.1 2.7 %collective-permute-start.6 = (bf16[8,128,128]{2,1,0:T(8,128)(2,1)S(1)}, bf16[8,128,128]{2,1,0:T(8,128)(2,1)S(1)}, u32[]{:S(2)}, u32[]{:S(2)}) collective-permute-start(bf16[8,128,128]{2,1,0:T(8,128)(2,1)S(1)} %get-tuple-element.62), channel_id=1, source_target_pairs={{0,3},{1,0},{2,1},{3,2},{4,7},{5,4},{6,5},{7,6},{8,11},{9,8},{10,9... | collective-permute-start | bytes 786440 | tf_op jit(solution)/shard_map/ppermute | solution.py:28
  109.8 5.1 %collective-permute-start.5 = (bf16[8,128,128]{2,1,0:T(8,128)(2,1)S(1)}, bf16[8,128,128]{2,1,0:T(8,128)(2,1)S(1)}, u32[]{:S(2)}, u32[]{:S(2)}) collective-permute-start(bf16[8,128,128]{2,1,0:T(8,128)(2,1)S(1)} %get-tuple-element.63), channel_id=1, source_target_pairs={{0,27},{1,0},{2,1},{3,2},{8,3},{9,8},{10,9},{11,10},{16,11},{17,16... | collective-permute-start | bytes 786440 | tf_op jit(solution)/shard_map/ppermute | solution.py:302
  115.0 0.7 collective-permute-done.9
  115.8 7.6 %shard_map.78 = (bf16[16,128,128]{2,1,0:T(8,128)(2,1)S(1)}, bf16[16,128,128]{2,1,0:T(8,128)(2,1)S(1)}, bf16[2,16,128]{2,1,0:T(8,128)(2,1)S(1)}) custom-call(s32[1]{0:T(128)} %bitcast.16._, s32[16,1,128]{2,1,0:T(1,128)S(1)} %bitcast.50, f32[8,128]{1,0:T(8,128)S(1)} %pad_maximum_fusion.5.taps_ref, bf16[16,128,128]{2,1,0:T(8,128)(2,1)S(1)} %get-tuple-element.33.q_ref, ...), custom_call_target="tpu_custom_call" | custom-call | flops 2147483648 | bytes 3145728 | tf_op jit(solution)/shard_map/pallas_call | solution.py:248
  123.4 0.7 collective-permute-done.5
  124.2 2.5 %collective-permute-start.10 = (bf16[8,128,128]{2,1,0:T(8,128)(2,1)S(1)}, bf16[8,128,128]{2,1,0:T(8,128)(2,1)S(1)}, u32[]{:S(2)}, u32[]{:S(2)}) collective-permute-start(bf16[8,128,128]{2,1,0:T(8,128)(2,1)S(1)} %get-tuple-element.55), channel_id=1, source_target_pairs={{0,4},{4,0},{1,5},{5,1},{2,6},{6,2},{3,7},{7,3},{8,12},{12,8},{9,1... | collective-permute-start | bytes 786440 | tf_op jit(solution)/shard_map/ppermute | solution.py:28
  126.8 7.5 %shard_map.79 = bf16[4,2,8,112,128]{4,3,2,1,0:T(8,128)(2,1)S(1)} custom-call(s32[1]{0:T(128)} %bitcast.8.x_ref, bf16[2048,2048]{1,0:T(8,128)(2,1)} %all-gather.3.cloned.1.call-done.tok_ref, bf16[16,128,128]{2,1,0:T(8,128)(2,1)S(1)} %get-tuple-element.37.gq_ref, f32[16,128,128]{2,1,0:T(8,128)S(1)} %get-tuple-element.38.own_ref, ...), custom_call_target="tpu_custom_call" | custom-call | flops 3221225472 | bytes 8388608 | tf_op jit(solution)/shard_map/pallas_call | solution.py:286
  134.4 0.8 pad_maximum_fusion.2
  135.4 3.6 %collective-permute-start.11 = (bf16[2,8,112,128]{3,2,1,0:T(8,128)(2,1)S(1)}, bf16[2,8,112,128]{3,2,1,0:T(8,128)(2,1)S(1)}, u32[]{:S(2)}, u32[]{:S(2)}) collective-permute-start(bf16[2,8,112,128]{3,2,1,0:T(8,128)(2,1)S(1)} %get-tuple-element.51), channel_id=1, source_target_pairs={{0,1},{1,2},{2,3},{3,0},{4,5},{5,6},{6,7},{7,4},{8,9},{9,10},{10,1... | collective-permute-start | bytes 1376264 | tf_op jit(solution)/shard_map/ppermute | solution.py:28
  139.0 7.2 %collective-permute-start.13 = (bf16[2,8,112,128]{3,2,1,0:T(8,128)(2,1)S(1)}, bf16[2,8,112,128]{3,2,1,0:T(8,128)(2,1)S(1)}, u32[]{:S(2)}, u32[]{:S(2)}) collective-permute-start(bf16[2,8,112,128]{3,2,1,0:T(8,128)(2,1)S(1)} %get-tuple-element.52), channel_id=1, source_target_pairs={{0,3},{1,0},{2,1},{3,2},{4,7},{5,4},{6,5},{7,6},{8,11},{9,8},{10,9... | collective-permute-start | bytes 1376264 | tf_op jit(solution)/shard_map/ppermute | solution.py:28
  146.2 5.9 %collective-permute-start.12 = (bf16[2,8,112,128]{3,2,1,0:T(8,128)(2,1)S(1)}, bf16[2,8,112,128]{3,2,1,0:T(8,128)(2,1)S(1)}, u32[]{:S(2)}, u32[]{:S(2)}) collective-permute-start(bf16[2,8,112,128]{3,2,1,0:T(8,128)(2,1)S(1)} %get-tuple-element.53), channel_id=1, source_target_pairs={{0,2},{1,3},{2,0},{3,1},{4,6},{5,7},{6,4},{7,5},{8,10},{9,11},{10,... | collective-permute-start | bytes 1376264 | tf_op jit(solution)/shard_map/ppermute | solution.py:28
  152.1 3.5 %collective-permute-done.11 = bf16[2,8,112,128]{3,2,1,0:T(8,128)(2,1)S(1)} collective-permute-done((bf16[2,8,112,128]{3,2,1,0:T(8,128)(2,1)S(1)}, bf16[2,8,112,128]{3,2,1,0:T(8,128)(2,1)S(1)}, u32[]{:S(2)}, u32[]{:S(2)}) %collective-permute-start.11) | collective-permute-done | bytes 458784 | tf_op jit(solution)/shard_map/ppermute | solution.py:28
  155.6 3.6 %collective-permute-done.13 = bf16[2,8,112,128]{3,2,1,0:T(8,128)(2,1)S(1)} collective-permute-done((bf16[2,8,112,128]{3,2,1,0:T(8,128)(2,1)S(1)}, bf16[2,8,112,128]{3,2,1,0:T(8,128)(2,1)S(1)}, u32[]{:S(2)}, u32[]{:S(2)}) %collective-permute-start.13) | collective-permute-done | bytes 458784 | tf_op jit(solution)/shard_map/ppermute | solution.py:28
  159.2 10.4 %collective-permute-done.12 = bf16[2,8,112,128]{3,2,1,0:T(8,128)(2,1)S(1)} collective-permute-done((bf16[2,8,112,128]{3,2,1,0:T(8,128)(2,1)S(1)}, bf16[2,8,112,128]{3,2,1,0:T(8,128)(2,1)S(1)}, u32[]{:S(2)}, u32[]{:S(2)}) %collective-permute-start.12) | collective-permute-done | bytes 458784 | tf_op jit(solution)/shard_map/ppermute | solution.py:28
  169.6 0.2 fusion.1
  169.9 0.8 pad_maximum_fusion.3
  170.8 15.4 %all-to-all-start.2 = ((bf16[16,112,128]{2,1,0:T(8,128)(2,1)}), bf16[16,112,128]{2,1,0:T(8,128)(2,1)S(1)}, u32[]{:S(2)}, u32[]{:S(2)}) async-start(bf16[16,112,128]{2,1,0:T(8,128)(2,1)} %bitcast.21), calls=%async_computation.2 | async-start | bytes 917504 | tf_op jit(solution)/shard_map/all_to_all | solution.py:23
  186.2 2.2 copy-done.1
  188.4 1.6 shard_map.80
  190.0 21.1 %all-to-all-done.2 = bf16[16,112,128]{2,1,0:T(8,128)(2,1)S(1)} async-done(((bf16[16,112,128]{2,1,0:T(8,128)(2,1)}), bf16[16,112,128]{2,1,0:T(8,128)(2,1)S(1)}, u32[]{:S(2)}, u32[]{:S(2)}) %all-to-all-start.2) | async-done | bytes 458784 | tf_op jit(solution)/shard_map/all_to_all | solution.py:23
  211.2 0.6 slice_add_fusion.1
  211.8 0.2 reshape.89
  212.1 0.8 reshape.90
  (49 shorter events, 1.5 us)
Async XLA Ops:
  7.2 17.4 %copy-start = (s32[16,128]{1,0:T(8,128)S(1)}, s32[16,128]{1,0:T(8,128)}, u32[]{:S(2)}) copy-start(s32[16,128]{1,0:T(8,128)} %param.8) | copy-start | bytes 24580
  7.2 20.8 %copy-start.5 = (f32[8,128]{1,0:T(8,128)S(1)}, f32[8,128]{1,0:T(8,128)}, u32[]{:S(2)}) copy-start(f32[8,128]{1,0:T(8,128)} %param.7) | copy-start | bytes 12292
  7.2 46.2 %copy-start.4 = (bf16[128,2048]{1,0:T(8,128)(2,1)S(1)}, bf16[128,2048]{1,0:T(8,128)(2,1)}, u32[]{:S(2)}) copy-start(bf16[128,2048]{1,0:T(8,128)(2,1)} %param.9) | copy-start | bytes 1572868
  7.2 83.2 %all-gather.3.cloned.1.call-start = ((), (), s32[]{:S(2)}) async-start(), calls=%async_computation.3 | async-start | bytes 8912896 | tf_op jit(solution)/shard_map/all_gather | solution.py:362
  9.8 43.5 %all-to-all-start = ((bf16[16,96,128]{2,1,0:T(8,128)(2,1)}), bf16[16,96,128]{2,1,0:T(8,128)(2,1)S(1)}, u32[]{:S(2)}, u32[]{:S(2)}) async-start(bf16[16,96,128]{2,1,0:T(8,128)(2,1)} %bitcast.2), calls=%async_computation | async-start | bytes 786432 | tf_op jit(solution)/shard_map/all_to_all | solution.py:23
  24.6 20.7 %collective-permute-start.1 = (s32[8,128]{1,0:T(8,128)S(1)}, s32[8,128]{1,0:T(8,128)S(1)}, u32[]{:S(2)}, u32[]{:S(2)}) collective-permute-start(s32[8,128]{1,0:T(8,128)S(1)} %constant_dynamic-slice_fusion), channel_id=1, source_target_pairs={{0,4},{4,0},{1,5},{5,1},{2,6},{6,2},{3,7},{7,3},{8,12},{12,8},{9,1... | collective-permute-start | bytes 12296 | tf_op jit(solution)/shard_map/ppermute | solution.py:28
  28.0 25.3 %collective-permute-start = (f32[8,128]{1,0:T(8,128)S(1)}, f32[8,128]{1,0:T(8,128)S(1)}, u32[]{:S(2)}, u32[]{:S(2)}) collective-permute-start(f32[8,128]{1,0:T(8,128)S(1)} %copy-done.5), channel_id=1, source_target_pairs={{0,256},{256,0},{1,257},{257,1},{2,258},{258,2},{3,259},{259,3},{4... | collective-permute-start | bytes 12296 | tf_op jit(solution)/shard_map/ppermute | solution.py:28
  54.7 32.4 %all-to-all-start.1 = ((bf16[16,128,128]{2,1,0:T(8,128)(2,1)}), bf16[16,128,128]{2,1,0:T(8,128)(2,1)S(1)}, u32[]{:S(2)}, u32[]{:S(2)}) async-start(bf16[16,128,128]{2,1,0:T(8,128)(2,1)} %copy.13), calls=%async_computation.1 | async-start | bytes 1048576 | tf_op jit(solution)/shard_map/all_to_all | solution.py:23
  59.3 127.0 %all-gather.5.cloned.1.call-start = ((), (), s32[]{:S(2)}) async-start(), calls=%async_computation.4 | async-start | bytes 4718592 | tf_op jit(solution)/shard_map/all_gather | solution.py:393
  59.3 13.1 %collective-permute-start.4 = (bf16[16,96,128]{2,1,0:T(8,128)(2,1)S(1)}, bf16[16,96,128]{2,1,0:T(8,128)(2,1)S(1)}, u32[]{:S(2)}, u32[]{:S(2)}) collective-permute-start(bf16[16,96,128]{2,1,0:T(8,128)(2,1)S(1)} %all-to-all-done), channel_id=1, source_target_pairs={{0,3},{1,0},{2,1},{3,2},{4,7},{5,4},{6,5},{7,6},{8,11},{9,8},{10,9... | collective-permute-start | bytes 1179656 | tf_op jit(solution)/shard_map/ppermute | solution.py:28
  61.8 20.0 %collective-permute-start.3 = (bf16[16,96,128]{2,1,0:T(8,128)(2,1)S(1)}, bf16[16,96,128]{2,1,0:T(8,128)(2,1)S(1)}, u32[]{:S(2)}, u32[]{:S(2)}) collective-permute-start(bf16[16,96,128]{2,1,0:T(8,128)(2,1)S(1)} %all-to-all-done), channel_id=1, source_target_pairs={{0,2},{1,3},{2,0},{3,1},{4,6},{5,7},{6,4},{7,5},{8,10},{9,11},{10,... | collective-permute-start | bytes 1179656 | tf_op jit(solution)/shard_map/ppermute | solution.py:28
  66.1 18.4 %collective-permute-start.2 = (bf16[16,96,128]{2,1,0:T(8,128)(2,1)S(1)}, bf16[16,96,128]{2,1,0:T(8,128)(2,1)S(1)}, u32[]{:S(2)}, u32[]{:S(2)}) collective-permute-start(bf16[16,96,128]{2,1,0:T(8,128)(2,1)S(1)} %all-to-all-done), channel_id=1, source_target_pairs={{0,1},{1,2},{2,3},{3,0},{4,5},{5,6},{6,7},{7,4},{8,9},{9,10},{10,1... | collective-permute-start | bytes 1179656 | tf_op jit(solution)/shard_map/ppermute | solution.py:28
  84.6 0.8 copy-start.2
  85.4 1.0 copy-start.3
  99.8 15.1 %collective-permute-start.8 = (bf16[8,128,128]{2,1,0:T(8,128)(2,1)S(1)}, bf16[8,128,128]{2,1,0:T(8,128)(2,1)S(1)}, u32[]{:S(2)}, u32[]{:S(2)}) collective-permute-start(bf16[8,128,128]{2,1,0:T(8,128)(2,1)S(1)} %get-tuple-element.59), channel_id=1, source_target_pairs={{0,1},{1,2},{2,3},{3,8},{8,9},{9,10},{10,11},{11,16},{16,17},{17,1... | collective-permute-start | bytes 786440 | tf_op jit(solution)/shard_map/ppermute | solution.py:302
  103.2 11.7 %collective-permute-start.7 = (bf16[1,128,128]{2,1,0:T(8,128)(2,1)S(1)}, bf16[1,128,128]{2,1,0:T(8,128)(2,1)S(1)}, u32[]{:S(2)}, u32[]{:S(2)}) collective-permute-start(bf16[1,128,128]{2,1,0:T(8,128)(2,1)S(1)} %get-tuple-element.60), channel_id=1, source_target_pairs={{27,256},{256,27},{31,260},{260,31},{59,288},{288,59},{63,292},{29... | collective-permute-start | bytes 98312 | tf_op jit(solution)/shard_map/ppermute | solution.py:308
  103.9 11.8 %collective-permute-start.9 = (bf16[8,128,128]{2,1,0:T(8,128)(2,1)S(1)}, bf16[8,128,128]{2,1,0:T(8,128)(2,1)S(1)}, u32[]{:S(2)}, u32[]{:S(2)}) collective-permute-start(bf16[8,128,128]{2,1,0:T(8,128)(2,1)S(1)} %get-tuple-element.58), channel_id=1, source_target_pairs={{0,1},{1,2},{2,3},{3,0},{4,5},{5,6},{6,7},{7,4},{8,9},{9,10},{10,1... | collective-permute-start | bytes 786440 | tf_op jit(solution)/shard_map/ppermute | solution.py:28
  107.1 16.3 %collective-permute-start.6 = (bf16[8,128,128]{2,1,0:T(8,128)(2,1)S(1)}, bf16[8,128,128]{2,1,0:T(8,128)(2,1)S(1)}, u32[]{:S(2)}, u32[]{:S(2)}) collective-permute-start(bf16[8,128,128]{2,1,0:T(8,128)(2,1)S(1)} %get-tuple-element.62), channel_id=1, source_target_pairs={{0,3},{1,0},{2,1},{3,2},{4,7},{5,4},{6,5},{7,6},{8,11},{9,8},{10,9... | collective-permute-start | bytes 786440 | tf_op jit(solution)/shard_map/ppermute | solution.py:28
  109.8 14.3 %collective-permute-start.5 = (bf16[8,128,128]{2,1,0:T(8,128)(2,1)S(1)}, bf16[8,128,128]{2,1,0:T(8,128)(2,1)S(1)}, u32[]{:S(2)}, u32[]{:S(2)}) collective-permute-start(bf16[8,128,128]{2,1,0:T(8,128)(2,1)S(1)} %get-tuple-element.63), channel_id=1, source_target_pairs={{0,27},{1,0},{2,1},{3,2},{8,3},{9,8},{10,9},{11,10},{16,11},{17,16... | collective-permute-start | bytes 786440 | tf_op jit(solution)/shard_map/ppermute | solution.py:302
  124.2 10.2 %collective-permute-start.10 = (bf16[8,128,128]{2,1,0:T(8,128)(2,1)S(1)}, bf16[8,128,128]{2,1,0:T(8,128)(2,1)S(1)}, u32[]{:S(2)}, u32[]{:S(2)}) collective-permute-start(bf16[8,128,128]{2,1,0:T(8,128)(2,1)S(1)} %get-tuple-element.55), channel_id=1, source_target_pairs={{0,4},{4,0},{1,5},{5,1},{2,6},{6,2},{3,7},{7,3},{8,12},{12,8},{9,1... | collective-permute-start | bytes 786440 | tf_op jit(solution)/shard_map/ppermute | solution.py:28
  135.4 20.2 %collective-permute-start.11 = (bf16[2,8,112,128]{3,2,1,0:T(8,128)(2,1)S(1)}, bf16[2,8,112,128]{3,2,1,0:T(8,128)(2,1)S(1)}, u32[]{:S(2)}, u32[]{:S(2)}) collective-permute-start(bf16[2,8,112,128]{3,2,1,0:T(8,128)(2,1)S(1)} %get-tuple-element.51), channel_id=1, source_target_pairs={{0,1},{1,2},{2,3},{3,0},{4,5},{5,6},{6,7},{7,4},{8,9},{9,10},{10,1... | collective-permute-start | bytes 1376264 | tf_op jit(solution)/shard_map/ppermute | solution.py:28
  139.0 20.2 %collective-permute-start.13 = (bf16[2,8,112,128]{3,2,1,0:T(8,128)(2,1)S(1)}, bf16[2,8,112,128]{3,2,1,0:T(8,128)(2,1)S(1)}, u32[]{:S(2)}, u32[]{:S(2)}) collective-permute-start(bf16[2,8,112,128]{3,2,1,0:T(8,128)(2,1)S(1)} %get-tuple-element.52), channel_id=1, source_target_pairs={{0,3},{1,0},{2,1},{3,2},{4,7},{5,4},{6,5},{7,6},{8,11},{9,8},{10,9... | collective-permute-start | bytes 1376264 | tf_op jit(solution)/shard_map/ppermute | solution.py:28
  146.2 23.4 %collective-permute-start.12 = (bf16[2,8,112,128]{3,2,1,0:T(8,128)(2,1)S(1)}, bf16[2,8,112,128]{3,2,1,0:T(8,128)(2,1)S(1)}, u32[]{:S(2)}, u32[]{:S(2)}) collective-permute-start(bf16[2,8,112,128]{3,2,1,0:T(8,128)(2,1)S(1)} %get-tuple-element.53), channel_id=1, source_target_pairs={{0,2},{1,3},{2,0},{3,1},{4,6},{5,7},{6,4},{7,5},{8,10},{9,11},{10,... | collective-permute-start | bytes 1376264 | tf_op jit(solution)/shard_map/ppermute | solution.py:28
  170.8 40.4 %all-to-all-start.2 = ((bf16[16,112,128]{2,1,0:T(8,128)(2,1)}), bf16[16,112,128]{2,1,0:T(8,128)(2,1)S(1)}, u32[]{:S(2)}, u32[]{:S(2)}) async-start(bf16[16,112,128]{2,1,0:T(8,128)(2,1)} %bitcast.21), calls=%async_computation.2 | async-start | bytes 917504 | tf_op jit(solution)/shard_map/all_to_all | solution.py:23
  186.2 2.2 copy-start.1
Sparse Core Ops, SparseCore 0:
  10.2 80.1 all-gather.2
  135.4 48.3 all-gather.4
